TPU v7x, 128 devices: a whole 4x4x4 slice. The times are simulated.
128 devices in a mesh: prompt: 8 (over y, x_lo), comp: 16 (over z, x_hi, core).
Axes of the slice: x: 4 (x_hi: 2, x_lo: 2; x = x_hi * 2 + x_lo), y: 4, z: 4, core: 2. Of those that a mesh axis runs over, the one named last changes fastest.
Arguments:
- q_nope: bfloat16 [2048, 16384], P('comp', 'prompt'), may hold values from -6 to 6
- q_rope: bfloat16 [2048, 8192], P('comp', 'prompt'), may hold values from -250 to 250
- d_out: bfloat16 [2048, 16384], P('comp', 'prompt'), may hold values from -6 to 6
- w_uk: bfloat16 [128, 128, 512], P('prompt'), may hold values from -0.5 to 0.5
- w_uv: bfloat16 [128, 512, 128], P('prompt'), may hold values from -0.25 to 0.25
- latent: bfloat16 [1024, 512], P('prompt'), may hold values from -6 to 6
- rope_key: bfloat16 [1024, 64], P('prompt'), may hold values from -5 to 5
- comp_latent: bfloat16 [2048, 512], P('comp'), may hold values from -6 to 6
- comp_rope: bfloat16 [2048, 64], P('comp'), may hold values from -6 to 6
- lengths: int32 [32], P('comp'), may hold values from 1 to 64
Outputs:
- d_w_uk: float32 [128, 128, 512], P(('prompt', 'comp'))
- d_w_uv: float32 [128, 512, 128], P(('prompt', 'comp'))
- d_latent: float32 [1024, 512], P(('prompt', 'comp'))
- d_rope_key: float32 [1024, 64], P(('prompt', 'comp'))
- d_comp_latent: float32 [2048, 512], P('comp', 'prompt')
- d_comp_rope: float32 [2048, 64], P('comp', 'prompt')
All inputs are finite; a program needn't handle non-finite values.
Results may differ from a plain program's by a relative error of at most 0.012.
Values may be sent and summed in bfloat16 or wider, within the bound.
No kernel may reach another device: no remote copies, remote signals or barrier semaphores. Data moves between devices by JAX's collectives and lax.ppermute only.
A program may use at most 128 MiB of HBM per device.

v0:
```python
import jax
import jax.numpy as jnp
from jax import lax
from jax.sharding import PartitionSpec as P

D_ROPE = 64
D_NOPE = 128


def local(q_nope, q_rope, d_out, w_uk, w_uv, latent, rope_key, comp_latent, comp_rope, lengths):
    f32 = jnp.float32
    bf16 = jnp.bfloat16
    scale = 1.0 / (D_NOPE + D_ROPE) ** 0.5
    rows = q_nope.shape[0]
    heads = w_uk.shape[0]
    samples = lengths.shape[0]
    slen = rows // samples
    width = w_uk.shape[2]
    whole_lat, whole_rope = (
        lax.all_gather(latent, "prompt", axis=0, tiled=True),
        lax.all_gather(rope_key, "prompt", axis=0, tiled=True),
    )
    prompt_len = whole_lat.shape[0]
    row_ids = jnp.arange(rows, dtype=jnp.int32)
    owner = row_ids // slen
    limit = jnp.sum(
        jnp.where(
            owner[:, None] == jnp.arange(samples, dtype=jnp.int32)[None, :], lengths[None, :], 0
        ),
        axis=1,
    )
    grads = jnp.where((row_ids % slen < limit)[:, None], d_out, jnp.zeros_like(d_out))
    qn_all = q_nope.reshape(rows, heads, -1).transpose(1, 0, 2)
    qr_all = q_rope.reshape(rows, heads, -1).transpose(1, 0, 2)
    g_all = grads.reshape(rows, heads, -1).transpose(1, 0, 2)
    nope = qn_all.shape[2]
    rdim = qr_all.shape[2]
    block = 4
    groups = heads // block
    clat_s = comp_latent.reshape(samples, slen, width)
    crop_s = comp_rope.reshape(samples, slen, rdim)
    causal = jnp.arange(slen)[:, None] >= jnp.arange(slen)[None, :]

    def group_step(carry, xs):
        d_lat, d_rop, d_clat, d_crop = carry
        qn, qr, g, wk, wv = xs
        q_lat = jnp.einsum("hrn,hnl->hrl", qn, wk, preferred_element_type=f32).astype(bf16)
        ql_s = q_lat.reshape(block, samples, slen, width)
        qr_s = qr.reshape(block, samples, slen, rdim)
        sp = (
            jnp.einsum("hrl,pl->hrp", q_lat, whole_lat, preferred_element_type=f32)
            + jnp.einsum("hrd,pd->hrp", qr, whole_rope, preferred_element_type=f32)
        ) * scale
        ss = (
            jnp.einsum("hstl,sul->hstu", ql_s, clat_s, preferred_element_type=f32)
            + jnp.einsum("hstd,sud->hstu", qr_s, crop_s, preferred_element_type=f32)
        ) * scale
        ss = jnp.where(causal[None, None], ss, -jnp.inf)
        top = jnp.maximum(jnp.max(sp, axis=-1), jnp.max(ss, axis=-1).reshape(block, rows))
        ep = jnp.exp(sp - top[..., None])
        es = jnp.exp(ss - top.reshape(block, samples, slen)[..., None])
        total = jnp.sum(ep, axis=-1) + jnp.sum(es, axis=-1).reshape(block, rows)
        pp = ep / total[..., None]
        ps = es / total.reshape(block, samples, slen)[..., None]
        ppb = pp.astype(bf16)
        psb = ps.astype(bf16)
        o_lat = (
            jnp.einsum("hrp,pl->hrl", ppb, whole_lat, preferred_element_type=f32)
            + jnp.einsum("hstu,sul->hstl", psb, clat_s, preferred_element_type=f32).reshape(
                block, rows, width
            )
        ).astype(bf16)
        d_olat = jnp.einsum("hrv,hlv->hrl", g, wv, preferred_element_type=f32).astype(bf16)
        do_s = d_olat.reshape(block, samples, slen, width)
        dpp = jnp.einsum("hrl,pl->hrp", d_olat, whole_lat, preferred_element_type=f32)
        dps = jnp.einsum("hstl,sul->hstu", do_s, clat_s, preferred_element_type=f32)
        delta = jnp.sum(pp * dpp, axis=-1) + jnp.sum(ps * dps, axis=-1).reshape(block, rows)
        dsp = (scale * pp * (dpp - delta[..., None])).astype(bf16)
        dss = (scale * ps * (dps - delta.reshape(block, samples, slen)[..., None])).astype(bf16)
        d_qlat = (
            jnp.einsum("hrp,pl->hrl", dsp, whole_lat, preferred_element_type=f32)
            + jnp.einsum("hstu,sul->hstl", dss, clat_s, preferred_element_type=f32).reshape(
                block, rows, width
            )
        ).astype(bf16)
        d_lat = (
            d_lat
            + jnp.einsum("hrp,hrl->pl", dsp, q_lat, preferred_element_type=f32)
            + jnp.einsum("hrp,hrl->pl", ppb, d_olat, preferred_element_type=f32)
        )
        d_rop = d_rop + jnp.einsum("hrp,hrd->pd", dsp, qr, preferred_element_type=f32)
        d_clat = d_clat + (
            jnp.einsum("hstu,hstl->sul", dss, ql_s, preferred_element_type=f32)
            + jnp.einsum("hstu,hstl->sul", psb, do_s, preferred_element_type=f32)
        ).reshape(rows, width)
        d_crop = d_crop + jnp.einsum(
            "hstu,hstd->sud", dss, qr_s, preferred_element_type=f32
        ).reshape(rows, rdim)
        produced = (
            jnp.einsum("hrn,hrl->hnl", qn, d_qlat, preferred_element_type=f32),
            jnp.einsum("hrl,hrv->hlv", o_lat, g, preferred_element_type=f32),
        )
        return ((d_lat, d_rop, d_clat, d_crop), produced)

    init = (
        jnp.zeros((prompt_len, width), f32),
        jnp.zeros((prompt_len, rdim), f32),
        jnp.zeros((rows, width), f32),
        jnp.zeros((rows, rdim), f32),
    )
    inputs = (
        qn_all.reshape(groups, block, rows, nope),
        qr_all.reshape(groups, block, rows, rdim),
        g_all.reshape(groups, block, rows, nope),
        w_uk.reshape(groups, block, nope, width),
        w_uv.reshape(groups, block, width, nope),
    )
    carry, stacked = lax.scan(group_step, init, inputs)
    d_w_uk, d_w_uv = (
        lax.psum_scatter(
            stacked[0].reshape(heads, nope, width), "comp", scatter_dimension=0, tiled=True
        ),
        lax.psum_scatter(
            stacked[1].reshape(heads, width, nope), "comp", scatter_dimension=0, tiled=True
        ),
    )
    d_latent, d_rope_key = (
        lax.psum_scatter(carry[0], ("prompt", "comp"), scatter_dimension=0, tiled=True),
        lax.psum_scatter(carry[1], ("prompt", "comp"), scatter_dimension=0, tiled=True),
    )
    d_comp_latent, d_comp_rope = (
        lax.psum_scatter(carry[2], "prompt", scatter_dimension=1, tiled=True),
        lax.psum_scatter(carry[3], "prompt", scatter_dimension=1, tiled=True),
    )
    return (d_w_uk, d_w_uv, d_latent, d_rope_key, d_comp_latent, d_comp_rope)


def solution(mesh):
    in_specs = (
        P("comp", "prompt"),
        P("comp", "prompt"),
        P("comp", "prompt"),
        P("prompt", None, None),
        P("prompt", None, None),
        P("prompt", None),
        P("prompt", None),
        P("comp", None),
        P("comp", None),
        P("comp"),
    )
    out_specs = (
        P(("prompt", "comp"), None, None),
        P(("prompt", "comp"), None, None),
        P(("prompt", "comp"), None),
        P(("prompt", "comp"), None),
        P("comp", "prompt"),
        P("comp", "prompt"),
    )
    return jax.shard_map(local, mesh=mesh, in_specs=in_specs, out_specs=out_specs, check_vma=False)
```

profile of v0, /device:TPU:0, one launch (start us, length us, event | category | flops | bytes accessed | tf_op | source)
XLA Modules:
  0.0 1248.0 jit_solution(17405961821377516066)
XLA Ops:
  8.0 1.8 copy.113
  9.8 1.4 copy.114
  11.3 27.4 %all_gather.7 = bf16[1024,64]{0,1:T(8,128)(2,1)} all-gather(bf16[128,64]{0,1:T(8,128)(2,1)} %param.18), channel_id=1, replica_groups=mesh['prompt'=8,'comp'=16] {'prompt'}, dimensions={0}, use_global_device_ids=true | all-gather | bytes 147456 | tf_op jit(solution)/shard_map/all_gather | solution.py:21
  41.3 12.3 all-gather.2.cloned.1.call-done
  53.6 198.2 %while.21 = (s32[]{:T(128)}, f32[1024,512]{1,0:T(8,128)}, f32[1024,64]{0,1:T(8,128)}, f32[128,512]{1,0:T(8,128)}, f32[128,64]{1,0:T(8,128)}, /*index=5*/f32[4,4,...) while((s32[]{:T(128)}, f32[1024,512]{1,0:T(8,128)}, ...), condition=%wide.region_8.9_spmd.clone, body=%wide.region_1.8_spmd.clone.sunk | while | flops 3848818688 | bytes 93143784 | solution.py:118
  53.6 1.4 convolution_convert_fusion.4
  57.6 1.4 fusion.159
  59.0 2.1 fusion.160
  68.4 1.3 reshape.190
  70.4 3.5 fusion.170
  74.0 1.5 convolution_convert_fusion.5
  75.5 1.7 multiply_reduce_fusion.5
  77.1 2.1 multiply_reduce_fusion.4
  85.2 3.2 multiply_convert_fusion.4
  88.5 3.7 fusion.169
  96.4 2.0 fusion.165
  99.4 1.4 copy-done.14
  101.8 1.4 convolution_convert_fusion.4
  105.7 1.4 fusion.159
  107.1 2.1 fusion.160
  118.6 3.6 fusion.170
  122.2 1.5 convolution_convert_fusion.5
  123.7 1.7 multiply_reduce_fusion.5
  125.3 2.1 multiply_reduce_fusion.4
  133.4 3.2 multiply_convert_fusion.4
  136.7 3.8 fusion.169
  142.0 1.7 bitcast_add_fusion.8
  145.0 1.5 bitcast_add_fusion.9
  146.4 2.0 fusion.165
  149.4 1.4 copy-done.14
  151.8 1.4 convolution_convert_fusion.4
  155.8 1.4 fusion.159
  157.2 2.1 fusion.160
  168.6 3.6 fusion.170
  172.2 1.5 convolution_convert_fusion.5
  173.7 1.7 multiply_reduce_fusion.5
  175.4 2.1 multiply_reduce_fusion.4
  183.5 3.2 multiply_convert_fusion.4
  186.7 3.8 fusion.169
  192.0 1.7 bitcast_add_fusion.8
  195.0 1.5 bitcast_add_fusion.9
  196.4 2.0 fusion.165
  199.4 1.4 copy-done.14
  201.8 1.4 convolution_convert_fusion.4
  205.8 1.4 fusion.159
  207.2 2.1 fusion.160
  218.6 3.6 fusion.170
  222.2 1.5 convolution_convert_fusion.5
  223.7 1.7 multiply_reduce_fusion.5
  225.4 2.1 multiply_reduce_fusion.4
  233.5 3.2 multiply_convert_fusion.4
  236.7 3.8 fusion.169
  242.0 1.7 bitcast_add_fusion.8
  245.0 1.5 bitcast_add_fusion.9
  246.4 2.0 fusion.165
  249.4 1.4 copy-done.14
  251.8 1.9 copy.116
  253.8 1.8 copy.117
  258.8 32.1 %all-reduce.1 = f32[128,64]{0,1:T(8,128)S(1)} all-reduce(f32[128,64]{0,1:T(8,128)S(1)} %copy.118), channel_id=7, replica_groups=mesh['prompt'=8,'comp'=16] {'prompt'}, use_global_device_ids=true, to_apply=%region_14.15.clone | all-reduce | flops 8192 | bytes 65536
  291.6 105.3 %all-reduce.4.cloned.1.call-done = f32[1024,64]{1,0:T(8,128)} async-done(((f32[1024,64]{1,0:T(8,128)}), f32[1024,64]{1,0:T(8,128)}) %all-reduce.4.cloned.1.call-update) | async-done | bytes 262160
  398.2 38.4 %reduce-scatter.11.cloned.1.call-done = f32[128,64]{0,1:T(8,128)} async-done(((f32[128,512]{0,1:T(8,128)}), f32[128,64]{0,1:T(8,128)}) %reduce-scatter.11.cloned.1.call-update) | async-done | bytes 32784 | tf_op jit(solution)/shard_map/reduce_scatter | solution.py:132
  436.5 641.7 %reduce-scatter.9.cloned.1.call-done = f32[8,512]{1,0:T(8,128)} async-done(((f32[1024,512]{1,0:T(8,128)}), f32[8,512]{1,0:T(8,128)}) %reduce-scatter.9.cloned.1.call-update) | async-done | bytes 16400 | tf_op jit(solution)/shard_map/reduce_scatter | solution.py:128
  1078.2 79.1 %reduce-scatter.5.cloned.1.call-done = f32[1,128,512]{2,1,0:T(8,128)} async-done(((f32[16,128,512]{2,1,0:T(8,128)}), f32[1,128,512]{2,1,0:T(8,128)}) %reduce-scatter.5.cloned.1.call-update) | async-done | bytes 262160 | tf_op jit(solution)/shard_map/reduce_scatter | solution.py:120
  1157.3 83.9 %reduce-scatter.7.cloned.1.call-done = f32[1,512,128]{2,1,0:T(8,128)} async-done(((f32[16,512,128]{2,1,0:T(8,128)}), f32[1,512,128]{2,1,0:T(8,128)}) %reduce-scatter.7.cloned.1.call-update) | async-done | bytes 262160 | tf_op jit(solution)/shard_map/reduce_scatter | solution.py:123
  (318 shorter events, 98.4 us)
Async XLA Ops:
  7.2 32.2 %copy-start = (bf16[128,2048]{1,0:T(8,128)(2,1)S(1)}, bf16[128,2048]{1,0:T(8,128)(2,1)}, u32[]{:S(2)}) copy-start(bf16[128,2048]{1,0:T(8,128)(2,1)} %param.12) | copy-start | bytes 1572868
  7.2 33.1 %copy-start.15 = (bf16[128,2048]{1,0:T(8,128)(2,1)S(1)}, bf16[128,2048]{1,0:T(8,128)(2,1)}, u32[]{:S(2)}) copy-start(bf16[128,2048]{1,0:T(8,128)(2,1)} %param.14) | copy-start | bytes 1572868
  7.2 46.4 %copy-start.3 = (bf16[128,512]{1,0:T(8,128)(2,1)S(1)}, bf16[128,512]{1,0:T(8,128)(2,1)}, u32[]{:S(2)}) copy-start(bf16[128,512]{1,0:T(8,128)(2,1)} %param.19) | copy-start | bytes 393220
  7.2 46.4 %all-gather.2.cloned.1.call-start = ((), (), s32[]{:S(2)}) async-start(), calls=%async_computation.4 | async-start | bytes 1179648 | tf_op jit(solution)/shard_map/all_gather | solution.py:20
  7.9 389.0 %all-reduce.4.cloned.1.call-start = ((), (), s32[]{:S(2)}) async-start(), calls=%async_computation.9 | async-start | bytes 1048576
  56.2 2.7 copy-start.6
  56.5 2.5 copy-start.5
  65.7 4.7 copy-start.17
  70.4 6.7 copy-start.20
  73.9 3.2 copy-start.2
  75.4 3.8 copy-start.8
  77.1 2.2 copy-start.19
  94.5 3.9 copy-start.9
  94.5 3.9 copy-start.13
  94.5 3.9 copy-start.21
  98.4 2.3 copy-start.1
  98.4 2.3 copy-start.7
  98.4 2.3 copy-start.10
  98.4 3.3 copy-start.4
  104.4 2.7 copy-start.6
  104.7 2.5 copy-start.5
  113.8 4.7 copy-start.17
  118.6 6.8 copy-start.20
  122.1 3.2 copy-start.2
  123.6 3.8 copy-start.8
  125.3 2.2 copy-start.19
  143.7 4.7 copy-start.9
  143.7 4.7 copy-start.13
  143.7 4.7 copy-start.21
  148.4 2.3 copy-start.1
  148.5 2.3 copy-start.7
  148.5 2.3 copy-start.10
  148.5 3.3 copy-start.4
  154.4 2.7 copy-start.6
  154.7 2.5 copy-start.5
  163.9 4.7 copy-start.17
  168.6 6.8 copy-start.20
  172.2 3.2 copy-start.2
  173.7 3.8 copy-start.8
  175.4 2.2 copy-start.19
  193.7 4.7 copy-start.9
  193.7 4.7 copy-start.13
  193.7 4.7 copy-start.21
  198.4 2.3 copy-start.1
  198.5 2.3 copy-start.7
  198.5 2.3 copy-start.10
  198.5 3.3 copy-start.4
  204.4 2.7 copy-start.6
  204.7 2.5 copy-start.5
  213.9 4.7 copy-start.17
  218.6 6.8 copy-start.20
  222.2 3.2 copy-start.2
  223.7 3.8 copy-start.8
  243.7 4.7 copy-start.9
  243.7 4.7 copy-start.13
  243.7 4.7 copy-start.21
  248.4 2.3 copy-start.1
  248.4 2.3 copy-start.7
  248.5 2.3 copy-start.10
  248.5 3.4 copy-start.4
  253.8 182.7 %reduce-scatter.11.cloned.1.call-start = ((), (), s32[]{:S(2)}) async-start(), calls=%async_computation.8 | async-start | bytes 294912 | tf_op jit(solution)/shard_map/reduce_scatter | solution.py:132
  255.7 822.5 %reduce-scatter.9.cloned.1.call-start = ((), (), s32[]{:S(2)}) async-start(), calls=%async_computation.7 | async-start | bytes 2113536 | tf_op jit(solution)/shard_map/reduce_scatter | solution.py:128
  256.2 901.1 %reduce-scatter.5.cloned.1.call-start = ((), (), s32[]{:S(2)}) async-start(), calls=%async_computation.5 | async-start | bytes 4456448 | tf_op jit(solution)/shard_map/reduce_scatter | solution.py:120
  256.8 984.3 %reduce-scatter.7.cloned.1.call-start = ((), (), s32[]{:S(2)}) async-start(), calls=%async_computation.6 | async-start | bytes 4456448 | tf_op jit(solution)/shard_map/reduce_scatter | solution.py:123
  (23 other events, 20.0 us)
Sparse Core Ops, SparseCore 0:
  9.7 43.8 all-gather.1
  253.9 142.9 all-reduce.3
  399.9 36.5 reduce-scatter.10
  439.3 638.8 reduce-scatter.8
  1083.2 74.0 reduce-scatter.4
  1161.7 79.3 reduce-scatter.6
where the time goes:
time: 1250 us
  waiting for transfers between devices  963 us (77%)
  matrix products  106 us (8%)
  local copies, waits for them, and re-layouts  60.7 us (5%)
  blocking collectives  59.5 us (5%)
  other arithmetic  43 us (3%)
  between operations  14.9 us (1%)
    reduce_scatter x1, waiting for transfers between devices, local(): lax.psum_scatter(carry[0], ('prompt', 'comp'), scatter_dimension=0, tiled...  642 us
    unnamed x7, waiting for transfers between devices  108 us
    reduce_scatter x1, waiting for transfers between devices, local(): lax.psum_scatter(stacked[1].reshape(heads, width, nope), 'comp', scatter_...  83.9 us
    reduce_scatter x1, waiting for transfers between devices, local(): lax.psum_scatter(stacked[0].reshape(heads, nope, width), 'comp', scatter_...  79.1 us
    reduce_scatter x1, waiting for transfers between devices, local(): lax.psum_scatter(carry[2], 'prompt', scatter_dimension=1, tiled=True)  38.4 us
    unnamed x1, blocking collectives  32.1 us
    all_gather x1, blocking collectives, local(): lax.all_gather(rope_key, 'prompt', axis=0, tiled=True)  27.4 us
  transfers between devices with their start and end apart: 6, of which 6 were waited for; matrix products, arithmetic and copies ran while one was open for 1% of the time, Pallas kernels for 0%

commit v1 on v0

v1 whole, which is shorter than its diff:
```python
import functools

import jax
import jax.numpy as jnp
from jax import lax
from jax.experimental import pallas as pl
from jax.experimental.pallas import tpu as pltpu
from jax.sharding import PartitionSpec as P

f32 = jnp.float32
bf16 = jnp.bfloat16
LOG2E = 1.4426950408889634

ROWS = 128
SLEN = 64
LAT = 512
ROPE = 64
NOPE = 128
KW = 640
HW = 384
PK = 1024
AK = PK + 2 * ROWS
SCALE = 1.0 / (NOPE + ROPE) ** 0.5


def nt(a, b):
    return lax.dot_general(a, b, (((1,), (1,)), ((), ())), preferred_element_type=f32)


def nn(a, b):
    return lax.dot_general(a, b, (((1,), (0,)), ((), ())), preferred_element_type=f32)


def prep_kernel(info, lens, qn, qr, do, lat, rope, clat, crop, keep, send, kv):
    core = info[0]
    row = lax.broadcasted_iota(jnp.int32, (ROWS, 1), 0)
    limit = jnp.where(row < SLEN, lens[0], lens[1])
    valid = (row % SLEN) < limit
    for out, flip in ((keep, 0), (send, 1)):
        par = core ^ flip
        for k in range(8):
            at = pl.multiple_of((2 * k + par) * NOPE, NOPE)
            out[k, :, 0:NOPE] = qn[:, pl.ds(at, NOPE)]
            g = do[:, pl.ds(at, NOPE)]
            out[k, :, NOPE : 2 * NOPE] = jnp.where(valid, g, jnp.zeros_like(g))
            pair = qr[:, 2 * ROPE * k : 2 * ROPE * (k + 1)].astype(f32)
            flipped = pltpu.roll(pair, ROPE, 1)
            out[k, :, 2 * NOPE : HW] = jnp.where(par == 0, pair, flipped).astype(bf16)
        out[8] = clat[:, 0:HW]
        out[9, :, 0 : LAT - HW] = clat[:, HW:LAT]
        out[9, :, LAT - HW : HW] = jnp.concatenate(
            [crop[...], jnp.zeros((ROWS, HW - (LAT - HW) - ROPE), bf16)], axis=1
        )
    mine = jnp.concatenate(
        [lat[...].astype(f32), rope[...].astype(f32), jnp.zeros((ROWS, KW - LAT - ROPE), f32)],
        axis=1,
    ).reshape(8, 2, 8, KW)
    kv[...] = jnp.where(core == 0, mine[:, 0], mine[:, 1]).reshape(64, KW).astype(bf16)


def prep(info, lens, qn, qr, do, lat, rope, clat, crop):
    vm = pl.BlockSpec(memory_space=pltpu.VMEM)
    sm = pl.BlockSpec(memory_space=pltpu.SMEM)
    return pl.pallas_call(
        prep_kernel,
        out_shape=(
            jax.ShapeDtypeStruct((10, ROWS, HW), bf16),
            jax.ShapeDtypeStruct((10, ROWS, HW), bf16),
            jax.ShapeDtypeStruct((64, KW), bf16),
        ),
        in_specs=[sm, sm] + [vm] * 7,
        out_specs=(vm, vm, vm),
        compiler_params=pltpu.CompilerParams(vmem_limit_bytes=24 * 2**20),
        name="prep",
    )(info, lens, qn, qr, do, lat, rope, clat, crop)


def attend_kernel(nh, first, last, info, *refs):
    refs = list(refs)
    take = lambda n: [refs.pop(0) for _ in range(n)]
    (kva, kvb, ckeep, crecv) = take(4)
    keeps, recvs, wks, wvs = take(nh), take(nh), take(nh), take(nh)
    accs = [] if first else take(1)
    dws = take(nh)
    outs = take(2) if last else take(1)
    (kall, kt, s_ref, dp_ref, pb, ds, q, dol) = refs
    W = 2 * ROWS
    kall[0:512] = kva[...]
    kall[512:1024] = kvb[...]
    for at, ref in ((PK, ckeep), (PK + ROWS, crecv)):
        kall[at : at + ROWS, 0:HW] = ref[0]
        kall[at : at + ROWS, HW:KW] = ref[1, :, 0 : KW - HW]
    for b in range(AK // 256):
        kt[:, b * 256 : b * 256 + 256] = kall[b * 256 : b * 256 + 256, 0:LAT].T
    zero = jnp.zeros((ROWS, ROWS), bf16)
    iu = lax.broadcasted_iota(jnp.int32, (ROWS, W), 0)
    it = lax.broadcasted_iota(jnp.int32, (ROWS, W), 1) % ROWS
    seen = ((iu // SLEN) == (it // SLEN)) & (iu <= it)
    NC = PK // 128 + 1
    for h in range(nh):
        lo = h * W
        hs = slice(lo, lo + W)
        qn = jnp.concatenate([keeps[h][0, :, 0:NOPE], recvs[h][0, :, 0:NOPE]], axis=0)
        g = jnp.concatenate(
            [keeps[h][0, :, NOPE : 2 * NOPE], recvs[h][0, :, NOPE : 2 * NOPE]], axis=0
        )
        q[hs, 0:LAT] = nn(qn, wks[h][0, 0]).astype(bf16)
        q[lo : lo + ROWS, LAT:KW] = keeps[h][0, :, 2 * NOPE : HW]
        q[lo + ROWS : lo + W, LAT:KW] = recvs[h][0, :, 2 * NOPE : HW]
        dol[hs] = nt(g, wvs[h][0, 0]).astype(bf16)
        sv, dv = s_ref.at[h % 2], dp_ref.at[h % 2]
        sv[0:PK] = nt(kall[0:PK], q[hs])
        own = nt(kall[PK:AK], q[hs])
        own = jnp.concatenate([own[0:ROWS, 0:ROWS], own[ROWS:W, ROWS:W]], axis=1)
        sv[PK : PK + ROWS] = jnp.where(seen, own, -jnp.inf)
        dv[0:PK] = nt(kall[0:PK, 0:LAT], dol[hs])
        own = nt(kall[PK:AK, 0:LAT], dol[hs])
        dv[PK : PK + ROWS] = jnp.concatenate(
            [own[0:ROWS, 0:ROWS], own[ROWS:W, ROWS:W]], axis=1
        )
        top = jnp.full((8, W), -jnp.inf, f32)
        for c in range(NC):
            x = sv[c * 128 : c * 128 + 128].reshape(16, 8, W)
            top = jnp.maximum(top, jnp.max(x, axis=0))
        top = jnp.max(top, axis=0, keepdims=True)
        total = jnp.zeros((8, W), f32)
        delta = jnp.zeros((8, W), f32)
        for c in range(NC):
            cs = slice(c * 128, c * 128 + 128)
            e = jnp.exp2((sv[cs] - top) * (SCALE * LOG2E))
            sv[cs] = e
            total = total + jnp.sum(e.reshape(16, 8, W), axis=0)
            delta = delta + jnp.sum((e * dv[cs]).reshape(16, 8, W), axis=0)
        inv = 1.0 / jnp.sum(total, axis=0, keepdims=True)
        delta = jnp.sum(delta, axis=0, keepdims=True) * inv
        cinv = inv * SCALE
        for c in range(NC):
            cs = slice(c * 128, c * 128 + 128)
            e = sv[cs]
            p = (e * inv).astype(bf16)
            d = (e * cinv * (dv[cs] - delta)).astype(bf16)
            if c < NC - 1:
                pb[cs, hs] = p
                ds[cs, hs] = d
            else:
                for ref, x in ((pb, p), (ds, d)):
                    ref[PK : PK + ROWS, lo : lo + ROWS] = x[:, 0:ROWS]
                    ref[PK : PK + ROWS, lo + ROWS : lo + W] = zero
                    ref[PK + ROWS : AK, lo : lo + ROWS] = zero
                    ref[PK + ROWS : AK, lo + ROWS : lo + W] = x[:, ROWS:W]
        olat_t = nn(kt[...], pb[:, hs]).astype(bf16)
        dqlat_t = nn(kt[...], ds[:, hs]).astype(bf16)
        dwk = nt(qn.T, dqlat_t)
        for j in range(4):
            dws[h][j * 128 : j * 128 + 128] = dwk[:, j * 128 : j * 128 + 128].astype(bf16)
        dws[h][LAT : 2 * LAT] = nn(olat_t, g).astype(bf16)
    if last:
        stay, give = outs
    for b in range(AK // 128):
        bs = slice(b * 128, b * 128 + 128)
        r = nn(ds[bs], q[...])
        r = jnp.concatenate([r[:, 0:LAT] + nn(pb[bs], dol[...]), r[:, LAT:KW]], axis=1)
        if not first:
            r = r + accs[0][bs]
        if not last:
            outs[0][bs] = r
        elif b < 4:
            stay[bs] = r.astype(bf16)
        elif b < 8:
            give[(b - 4) * 128 : (b - 4) * 128 + 128] = r.astype(bf16)
        elif b == 8:
            stay[512:640] = r.astype(bf16)
        else:
            give[512:640] = r.astype(bf16)


def attend(nh, first, last, info, kva, kvb, keep, recv, w_uk, w_uv, acc):
    W = 2 * ROWS
    vm = pl.BlockSpec(memory_space=pltpu.VMEM)

    def head(i):
        return pl.BlockSpec((1, ROWS, HW), lambda s, info: (info[i + 1], 0, 0))

    ck = pl.BlockSpec((2, ROWS, HW), lambda s, info: (4, 0, 0))

    def wspec(i, a, b):
        return pl.BlockSpec((1, 1, a, b), lambda s, info: (info[i + 1], info[0], 0, 0))

    def full(a, b):
        return pl.BlockSpec((a, b), lambda s, info: (0, 0))

    in_specs = [full(512, KW), full(512, KW), ck, ck]
    in_specs += [head(i) for i in range(nh)] * 2
    in_specs += [wspec(i, NOPE, LAT) for i in range(nh)]
    in_specs += [wspec(i, LAT, NOPE) for i in range(nh)]
    ops = [kva, kvb, keep, recv] + [keep] * nh + [recv] * nh + [w_uk] * nh + [w_uv] * nh
    if not first:
        in_specs.append(full(AK, KW))
        ops.append(acc)
    out_specs = [full(2 * LAT, NOPE)] * nh
    out_shape = [jax.ShapeDtypeStruct((2 * LAT, NOPE), bf16)] * nh
    if last:
        out_specs += [full(640, KW)] * 2
        out_shape += [jax.ShapeDtypeStruct((640, KW), bf16)] * 2
    else:
        out_specs += [full(AK, KW)]
        out_shape += [jax.ShapeDtypeStruct((AK, KW), f32)]
    return pl.pallas_call(
        functools.partial(attend_kernel, nh, first, last),
        out_shape=out_shape,
        grid_spec=pltpu.PrefetchScalarGridSpec(
            num_scalar_prefetch=1,
            grid=(1,),
            in_specs=in_specs,
            out_specs=out_specs,
            scratch_shapes=[
                pltpu.VMEM((AK, KW), bf16),
                pltpu.VMEM((LAT, AK), bf16),
                pltpu.VMEM((2, PK + ROWS, W), f32),
                pltpu.VMEM((2, PK + ROWS, W), f32),
                pltpu.VMEM((AK, nh * W), bf16),
                pltpu.VMEM((AK, nh * W), bf16),
                pltpu.VMEM((nh * W, KW), bf16),
                pltpu.VMEM((nh * W, LAT), bf16),
            ],
        ),
        compiler_params=pltpu.CompilerParams(vmem_limit_bytes=50 * 2**20),
        name="attend",
    )(info, *ops)


def join_kernel(info, stay, got, dlat, dcl):
    prm = info[0]
    for k in range(8):
        to = lax.rem(prm - k + 8, 8)
        at = pl.multiple_of(to * 64, 64)
        ks = slice(k * 64, k * 64 + 64)
        dlat[pl.ds(at, 64)] = (stay[ks].astype(f32) + got[ks].astype(f32)).astype(bf16)
    c = stay[512:640].astype(f32) + got[512:640].astype(f32)
    pad = jnp.zeros((ROWS, 56), f32)
    for j in range(8):
        dcl[j] = jnp.concatenate(
            [c[:, 64 * j : 64 * j + 64], c[:, LAT + 8 * j : LAT + 8 * j + 8], pad], axis=1
        ).astype(bf16)


def join(info, stay, got):
    vm = pl.BlockSpec(memory_space=pltpu.VMEM)
    return pl.pallas_call(
        join_kernel,
        out_shape=(
            jax.ShapeDtypeStruct((512, KW), bf16),
            jax.ShapeDtypeStruct((8, ROWS, 128), bf16),
        ),
        in_specs=[pl.BlockSpec(memory_space=pltpu.SMEM), vm, vm],
        out_specs=(vm, vm),
        compiler_params=pltpu.CompilerParams(vmem_limit_bytes=24 * 2**20),
        name="join",
    )(info, stay, got)


def weights_kernel(*refs):
    parts, (dwk, dwv) = refs[:-2], refs[-2:]
    for j in range(4):
        js = slice(j * 128, j * 128 + 128)
        total = parts[0][js].astype(f32)
        for p in parts[1:]:
            total = total + p[js].astype(f32)
        dwk[:, js] = total
        js = slice(LAT + j * 128, LAT + j * 128 + 128)
        total = parts[0][js].astype(f32)
        for p in parts[1:]:
            total = total + p[js].astype(f32)
        dwv[j * 128 : j * 128 + 128] = total


def weights(parts):
    vm = pl.BlockSpec(memory_space=pltpu.VMEM)
    return pl.pallas_call(
        weights_kernel,
        out_shape=(
            jax.ShapeDtypeStruct((NOPE, LAT), f32),
            jax.ShapeDtypeStruct((LAT, NOPE), f32),
        ),
        in_specs=[vm] * len(parts),
        out_specs=(vm, vm),
        compiler_params=pltpu.CompilerParams(vmem_limit_bytes=24 * 2**20),
        name="weights",
    )(*parts)


def final_kernel(info, dcl, *refs):
    got, dlat, (ol, orp, ocl, ocr) = refs[:7], refs[7], refs[8:]
    total = dcl[info[0]].astype(f32)
    for p in got:
        total = total + p[...].astype(f32)
    ocl[...] = total[:, 0:64]
    ocr[...] = total[:, 64:72]
    x = jnp.sum(dlat[...].astype(f32).reshape(64, 8, KW), axis=0)
    ol[...] = x[:, 0:LAT]
    orp[...] = x[:, LAT : LAT + ROPE]


def final(info, dcl, got, dlat):
    vm = pl.BlockSpec(memory_space=pltpu.VMEM)
    return pl.pallas_call(
        final_kernel,
        out_shape=(
            jax.ShapeDtypeStruct((8, LAT), f32),
            jax.ShapeDtypeStruct((8, ROPE), f32),
            jax.ShapeDtypeStruct((ROWS, 64), f32),
            jax.ShapeDtypeStruct((ROWS, 8), f32),
        ),
        in_specs=[pl.BlockSpec(memory_space=pltpu.SMEM)] + [vm] * 9,
        out_specs=(vm,) * 4,
        compiler_params=pltpu.CompilerParams(vmem_limit_bytes=24 * 2**20),
        name="final",
    )(info, dcl, *got, dlat)


NH = 4
HOPS = ((2, 1), (2, 0), (1, 1), (1, 0), (3, 1), (3, 0), (0, 1), (0, 0))


def chip_perm(dz, dx):
    return [
        (c, (((c >> 2) + dz) % 4) * 4 + ((((c >> 1) & 1) ^ dx) << 1) + (c & 1))
        for c in range(16)
    ]


def local(q_nope, q_rope, d_out, w_uk, w_uv, latent, rope_key, comp_latent, comp_rope, lengths):
    comp = lax.axis_index("comp").astype(jnp.int32)
    prm = lax.axis_index("prompt").astype(jnp.int32)
    core, z, xh = comp % 2, comp // 4, (comp // 2) % 2
    core_perm = [(c, c ^ 1) for c in range(16)]
    keep, send, kv = prep(
        core[None], lengths, q_nope, q_rope, d_out, latent, rope_key, comp_latent, comp_rope
    )
    parts = [kv] + [
        lax.ppermute(kv, "prompt", [(i, (i + k) % 8) for i in range(8)]) for k in range(1, 8)
    ]
    recv = lax.ppermute(send, "comp", core_perm)
    kva = jnp.concatenate(parts, axis=0)
    kvb = lax.ppermute(kva, "comp", core_perm)
    w_uk4 = w_uk.reshape(8, 2, NOPE, LAT)
    w_uv4 = w_uv.reshape(8, 2, LAT, NOPE)
    order = [((z + dz) % 4) * 2 + (xh ^ dx) for dz, dx in HOPS]
    acc = None
    sums = []
    for first in range(0, 8, NH):
        info = jnp.stack([core] + order[first : first + NH])
        done = first + NH == 8
        out = attend(
            NH, first == 0, done, info, kva, kvb, keep, recv, w_uk4, w_uv4, acc
        )
        acc = out[NH]
        for i in range(NH):
            hop = HOPS[first + i]
            if hop == (0, 0):
                sums.append(out[i])
            else:
                sums.append(lax.ppermute(out[i], "comp", chip_perm(*hop)))
    stay, give = out[NH], out[NH + 1]
    got = lax.ppermute(give, "comp", core_perm)
    dlat, dcl = join(prm[None], stay, got)
    pieces = [
        lax.ppermute(
            lax.dynamic_index_in_dim(dcl, (prm + k) % 8, 0, keepdims=False),
            "prompt",
            [(i, (i + k) % 8) for i in range(8)],
        )
        for k in range(1, 8)
    ]
    groups = [[i for i in range(128) if i % 2 == c] for c in range(2)]
    dlat = lax.all_to_all(
        dlat, ("prompt", "comp"), 0, 0, tiled=True, axis_index_groups=groups
    )
    dwk, dwv = weights(sums)
    ol, orp, ocl, ocr = final(prm[None], dcl, pieces, dlat)
    return dwk[None], dwv[None], ol, orp, ocl, ocr


def solution(mesh):
    in_specs = (
        P("comp", "prompt"),
        P("comp", "prompt"),
        P("comp", "prompt"),
        P("prompt", None, None),
        P("prompt", None, None),
        P("prompt", None),
        P("prompt", None),
        P("comp", None),
        P("comp", None),
        P("comp"),
    )
    out_specs = (
        P(("prompt", "comp"), None, None),
        P(("prompt", "comp"), None, None),
        P(("prompt", "comp"), None),
        P(("prompt", "comp"), None),
        P("comp", "prompt"),
        P("comp", "prompt"),
    )
    return jax.shard_map(local, mesh=mesh, in_specs=in_specs, out_specs=out_specs, check_vma=False)
```

time: 1250 us -> 129 us (0.10)
  waiting for transfers between devices: 963 us -> 30.6 us
  matrix products: 106 us -> 0 us
  blocking collectives: 59.5 us -> 0 us
  local copies, waits for them, and re-layouts: 60.7 us -> 10.9 us
  starting transfers between devices: 0.24 us -> 47.3 us
  other arithmetic: 43 us -> 0 us
  Pallas kernels: 0 us -> 38.7 us
  between operations: 14.9 us -> 0.94 us
    reduce_scatter x4 -> x0, waiting for transfers between devices: 843 us -> none  [the longest x1 642 us: local(): lax.psum_scatter(carry[0], ('prompt', 'comp'), scatter_dimension=0, tiled...]
    unnamed x7 -> x0, waiting for transfers between devices: 108 us -> none
    dot_general x72 -> x0, matrix products: 106 us -> none  [the longest x4 15.1 us: group_step(): jnp.einsum('hrn,hrl->hnl', qn, d_qlat, preferred_element_type=f32)]
    pallas_call x0 -> x6, Pallas kernels: none -> 38.7 us  [the longest x2 34.7 us: attend(): pl.pallas_call(functools.partial(attend_kernel, nh, first, last), out_sha...]
    ppermute x0 -> x24, starting transfers between devices: none -> 37.6 us  [the longest x7 15 us: local(): sums.append(lax.ppermute(out[i], 'comp', chip_perm(*hop)))]
    unnamed x1 -> x0, blocking collectives: 32.1 us -> none
    ppermute x0 -> x24, waiting for transfers between devices: none -> 30.6 us  [the longest x7 19.3 us: local(): sums.append(lax.ppermute(out[i], 'comp', chip_perm(*hop)))]
    all_gather x1 -> x0, blocking collectives: 27.4 us -> none  [local(): lax.all_gather(rope_key, 'prompt', axis=0, tiled=True)]
  transfers between devices with their start and end apart: 6 -> 25, of which waited for: 6 -> 10; matrix products, arithmetic and copies ran while one was open for 1% -> 0% of each run, Pallas kernels for 0% -> 1%
where the time goes in v1:
time: 129 us; the launch traced here: 128 us
  starting transfers between devices  47.3 us (37%)
  Pallas kernels  38.7 us (30%)
  waiting for transfers between devices  30.6 us (24%)
  local copies, waits for them, and re-layouts  10.9 us (8%)
    pallas_call x2, Pallas kernels, attend(): pl.pallas_call(functools.partial(attend_kernel, nh, first, last), out_sha...  34.7 us
    ppermute x7, waiting for transfers between devices, local(): sums.append(lax.ppermute(out[i], 'comp', chip_perm(*hop)))  19.3 us
    ppermute x7, starting transfers between devices, local(): sums.append(lax.ppermute(out[i], 'comp', chip_perm(*hop)))  15 us
    ppermute x7, starting transfers between devices, local(): lax.ppermute(kv, 'prompt', [(i, (i + k) % 8) for i in range(8)])  12 us
    unnamed x37, local copies, waits for them, and re-layouts  10.7 us
    all_to_all x1, starting transfers between devices, local(): lax.all_to_all(dlat, ('prompt', 'comp'), 0, 0, tiled=True, axis_index_gro...  9.75 us
    ppermute x7, starting transfers between devices, local(): lax.ppermute(lax.dynamic_index_in_dim(dcl, (prm + k) % 8, 0, keepdims=Fal...  9.68 us
    ppermute x7, waiting for transfers between devices, local(): lax.ppermute(kv, 'prompt', [(i, (i + k) % 8) for i in range(8)])  4.23 us
  transfers between devices with their start and end apart: 25, of which 10 were waited for; matrix products, arithmetic and copies ran while one was open for 0% of the time, Pallas kernels for 1%

profile of v1, /device:TPU:0, one launch (start us, length us, event | category | flops | bytes accessed | tf_op | source)
XLA Modules:
  0.0 128.5 jit_solution(3800540622272722382)
XLA Ops:
  0.6 0.8 copy.16.rope
  1.5 0.8 copy.17.crop
  2.3 0.0 copy-start.1
  2.3 1.0 copy-done.1
  3.4 1.0 copy-done.2
  4.4 0.9 copy-done.3
  5.4 0.9 copy-done.4
  6.3 0.9 copy-done.5
  7.2 0.7 copy-done.6
  7.8 1.0 prep.1
  8.8 1.6 %collective-permute-start = (bf16[64,640]{1,0:T(8,128)(2,1)S(1)}, bf16[64,640]{1,0:T(8,128)(2,1)S(1)}, u32[]{:S(2)}, u32[]{:S(2)}) collective-permute-start(bf16[64,640]{1,0:T(8,128)(2,1)S(1)} %get-tuple-element.28), channel_id=1, source_target_pairs={{0,16},{16,32},{32,48},{48,64},{64,80},{80,96},{96,112},{112,0},{1... | collective-permute-start | bytes 245768 | tf_op jit(solution)/shard_map/ppermute | solution.py:341
  10.5 1.6 %collective-permute-start.1 = (bf16[64,640]{1,0:T(8,128)(2,1)S(1)}, bf16[64,640]{1,0:T(8,128)(2,1)S(1)}, u32[]{:S(2)}, u32[]{:S(2)}) collective-permute-start(bf16[64,640]{1,0:T(8,128)(2,1)S(1)} %get-tuple-element.28), channel_id=1, source_target_pairs={{0,32},{16,48},{32,64},{48,80},{64,96},{80,112},{96,0},{112,16},{1... | collective-permute-start | bytes 245768 | tf_op jit(solution)/shard_map/ppermute | solution.py:341
  12.1 2.3 %collective-permute-start.2 = (bf16[64,640]{1,0:T(8,128)(2,1)S(1)}, bf16[64,640]{1,0:T(8,128)(2,1)S(1)}, u32[]{:S(2)}, u32[]{:S(2)}) collective-permute-start(bf16[64,640]{1,0:T(8,128)(2,1)S(1)} %get-tuple-element.28), channel_id=1, source_target_pairs={{0,48},{16,64},{32,80},{48,96},{64,112},{80,0},{96,16},{112,32},{1... | collective-permute-start | bytes 245768 | tf_op jit(solution)/shard_map/ppermute | solution.py:341
  14.3 1.8 %collective-permute-start.3 = (bf16[64,640]{1,0:T(8,128)(2,1)S(1)}, bf16[64,640]{1,0:T(8,128)(2,1)S(1)}, u32[]{:S(2)}, u32[]{:S(2)}) collective-permute-start(bf16[64,640]{1,0:T(8,128)(2,1)S(1)} %get-tuple-element.28), channel_id=1, source_target_pairs={{0,64},{16,80},{32,96},{48,112},{64,0},{80,16},{96,32},{112,48},{1... | collective-permute-start | bytes 245768 | tf_op jit(solution)/shard_map/ppermute | solution.py:341
  16.2 3.2 %collective-permute-start.4 = (bf16[64,640]{1,0:T(8,128)(2,1)S(1)}, bf16[64,640]{1,0:T(8,128)(2,1)S(1)}, u32[]{:S(2)}, u32[]{:S(2)}) collective-permute-start(bf16[64,640]{1,0:T(8,128)(2,1)S(1)} %get-tuple-element.28), channel_id=1, source_target_pairs={{0,80},{16,96},{32,112},{48,0},{64,16},{80,32},{96,48},{112,64},{1... | collective-permute-start | bytes 245768 | tf_op jit(solution)/shard_map/ppermute | solution.py:341
  19.4 0.0 collective-permute-done
  19.4 1.4 %collective-permute-start.5 = (bf16[64,640]{1,0:T(8,128)(2,1)S(1)}, bf16[64,640]{1,0:T(8,128)(2,1)S(1)}, u32[]{:S(2)}, u32[]{:S(2)}) collective-permute-start(bf16[64,640]{1,0:T(8,128)(2,1)S(1)} %get-tuple-element.28), channel_id=1, source_target_pairs={{0,96},{16,112},{32,0},{48,16},{64,32},{80,48},{96,64},{112,80},{1... | collective-permute-start | bytes 245768 | tf_op jit(solution)/shard_map/ppermute | solution.py:341
  20.9 0.0 collective-permute-done.1
  20.9 0.1 collective-permute-start.6
  21.0 0.0 collective-permute-done.2
  21.0 0.1 collective-permute-start.8
  21.1 0.7 collective-permute-done.3
  21.8 0.0 collective-permute-done.4
  21.8 2.1 %collective-permute-done.5 = bf16[64,640]{1,0:T(8,128)(2,1)S(1)} collective-permute-done((bf16[64,640]{1,0:T(8,128)(2,1)S(1)}, bf16[64,640]{1,0:T(8,128)(2,1)S(1)}, u32[]{:S(2)}, u32[]{:S(2)}) %collective-permute-start.5) | collective-permute-done | bytes 81952 | tf_op jit(solution)/shard_map/ppermute | solution.py:341
  23.9 1.4 %collective-permute-done.6 = bf16[64,640]{1,0:T(8,128)(2,1)S(1)} collective-permute-done((bf16[64,640]{1,0:T(8,128)(2,1)S(1)}, bf16[64,640]{1,0:T(8,128)(2,1)S(1)}, u32[]{:S(2)}, u32[]{:S(2)}) %collective-permute-start.6) | collective-permute-done | bytes 81952 | tf_op jit(solution)/shard_map/ppermute | solution.py:341
  25.4 0.3 collective-permute-start.7
  25.8 0.1 stack.39.info
  25.9 0.1 stack.44.info
  25.9 1.8 %collective-permute-done.7.refs_1_ = bf16[512,640]{1,0:T(8,128)(2,1)S(1)} collective-permute-done((bf16[512,640]{1,0:T(8,128)(2,1)S(1)}, bf16[512,640]{1,0:T(8,128)(2,1)S(1)}, u32[]{:S(2)}, u32[]{:S(2)}) %collective-permute-start.7) | collective-permute-done | bytes 655392 | tf_op jit(solution)/shard_map/ppermute | solution.py:345
  27.7 0.0 collective-permute-done.8.refs_3_.refs_8_.refs_9_.refs_10_.refs_11_
  27.8 17.1 %attend.2 = (bf16[1024,128]{1,0:T(8,128)(2,1)S(1)}, bf16[1024,128]{1,0:T(8,128)(2,1)S(1)}, bf16[1024,128]{1,0:T(8,128)(2,1)S(1)}, bf16[1024,128]{1,0:T(8,128)(2,1)}, f32[1280,640]{1,0:T(8,128)}) custom-call(s32[5]{0:T(128)S(1)} %stack.39.info, bf16[512,640]{1,0:T(8,128)(2,1)S(1)} %constant_dynamic-update-slice_fusion.refs_0_, ...), custom_call_target="tpu_custom_call" | custom-call | tf_op jit(solution)/shard_map/attend/pallas_call | solution.py:208
  44.9 0.7 copy-done.7
  45.6 0.7 copy-done.9
  46.3 0.7 copy-done.11
  47.0 17.6 %attend.3 = (bf16[1024,128]{1,0:T(8,128)(2,1)}, bf16[1024,128]{1,0:T(8,128)(2,1)}, bf16[1024,128]{1,0:T(8,128)(2,1)S(1)}, bf16[1024,128]{1,0:T(8,128)(2,1)S(1)},...) custom-call(s32[5]{0:T(128)S(1)} %stack.44.info, bf16[512,640]{1,0:T(8,128)(2,1)S(1)} %constant_dynamic-update-slice_fusion.refs_0_, ...), custom_call_target="tpu_custom_call" | custom-call | tf_op jit(solution)/shard_map/attend/pallas_call | solution.py:208
  64.6 0.5 collective-permute-start.16
  65.1 2.4 %collective-permute-done.16.got = bf16[640,640]{1,0:T(8,128)(2,1)S(1)} collective-permute-done((bf16[640,640]{1,0:T(8,128)(2,1)}, bf16[640,640]{1,0:T(8,128)(2,1)S(1)}, u32[]{:S(2)}, u32[]{:S(2)}) %collective-permute-start.16) | collective-permute-done | bytes 819232 | tf_op jit(solution)/shard_map/ppermute | solution.py:365
  67.5 1.2 join.1
  68.7 9.8 %all-to-all-start = ((bf16[64,8,640]{2,1,0:T(8,128)(2,1)}), bf16[64,8,640]{2,1,0:T(8,128)(2,1)S(1)}, u32[]{:S(2)}, u32[]{:S(2)}) async-start(bf16[64,8,640]{2,1,0:T(8,128)(2,1)} %bitcast.21), calls=%async_computation | async-start | bytes 1310720 | tf_op jit(solution)/shard_map/all_to_all | solution.py:376
  78.4 5.6 %collective-permute-start.9 = (bf16[1024,128]{1,0:T(8,128)(2,1)S(1)}, bf16[1024,128]{1,0:T(8,128)(2,1)S(1)}, u32[]{:S(2)}, u32[]{:S(2)}) collective-permute-start(bf16[1024,128]{1,0:T(8,128)(2,1)S(1)} %copy-done.12), channel_id=1, source_target_pairs={{0,10},{1,11},{2,8},{3,9},{4,14},{5,15},{6,12},{7,13},{8,2},{9,3},... | collective-permute-start | bytes 786440 | tf_op jit(solution)/shard_map/ppermute | solution.py:363
  84.0 0.6 collective-permute-start.10
  84.6 1.5 %collective-permute-start.11 = (bf16[1024,128]{1,0:T(8,128)(2,1)S(1)}, bf16[1024,128]{1,0:T(8,128)(2,1)S(1)}, u32[]{:S(2)}, u32[]{:S(2)}) collective-permute-start(bf16[1024,128]{1,0:T(8,128)(2,1)S(1)} %copy-done.8), channel_id=1, source_target_pairs={{0,6},{1,7},{2,4},{3,5},{4,10},{5,11},{6,8},{7,9},{8,14},{9,15},{1... | collective-permute-start | bytes 786440 | tf_op jit(solution)/shard_map/ppermute | solution.py:363
  86.0 1.5 %collective-permute-start.12 = (bf16[1024,128]{1,0:T(8,128)(2,1)}, bf16[1024,128]{1,0:T(8,128)(2,1)S(1)}, u32[]{:S(2)}, u32[]{:S(2)}) collective-permute-start(bf16[1024,128]{1,0:T(8,128)(2,1)} %get-tuple-element.34), channel_id=1, source_target_pairs={{0,4},{1,5},{2,6},{3,7},{4,8},{5,9},{6,10},{7,11},{8,12},{9,13},{1... | collective-permute-start | bytes 786440 | tf_op jit(solution)/shard_map/ppermute | solution.py:363
  87.5 4.2 %collective-permute-start.13 = (bf16[1024,128]{1,0:T(8,128)(2,1)}, bf16[1024,128]{1,0:T(8,128)(2,1)S(1)}, u32[]{:S(2)}, u32[]{:S(2)}) collective-permute-start(bf16[1024,128]{1,0:T(8,128)(2,1)} %get-tuple-element.36), channel_id=1, source_target_pairs={{0,14},{1,15},{2,12},{3,13},{4,2},{5,3},{6,0},{7,1},{8,6},{9,7},{1... | collective-permute-start | bytes 786440 | tf_op jit(solution)/shard_map/ppermute | solution.py:363
  91.7 8.0 %collective-permute-done.9.refs_0_ = bf16[1024,128]{1,0:T(8,128)(2,1)S(1)} collective-permute-done((bf16[1024,128]{1,0:T(8,128)(2,1)S(1)}, bf16[1024,128]{1,0:T(8,128)(2,1)S(1)}, u32[]{:S(2)}, u32[]{:S(2)}) %collective-permute-start.9) | collective-permute-done | bytes 262176 | tf_op jit(solution)/shard_map/ppermute | solution.py:363
  99.7 8.8 %collective-permute-done.10.refs_1_ = bf16[1024,128]{1,0:T(8,128)(2,1)S(1)} collective-permute-done((bf16[1024,128]{1,0:T(8,128)(2,1)S(1)}, bf16[1024,128]{1,0:T(8,128)(2,1)S(1)}, u32[]{:S(2)}, u32[]{:S(2)}) %collective-permute-start.10) | collective-permute-done | bytes 262176 | tf_op jit(solution)/shard_map/ppermute | solution.py:363
  108.5 1.8 %collective-permute-start.15 = (bf16[1024,128]{1,0:T(8,128)(2,1)S(1)}, bf16[1024,128]{1,0:T(8,128)(2,1)S(1)}, u32[]{:S(2)}, u32[]{:S(2)}) collective-permute-start(bf16[1024,128]{1,0:T(8,128)(2,1)S(1)} %get-tuple-element.38), channel_id=1, source_target_pairs={{0,2},{1,3},{2,0},{3,1},{4,6},{5,7},{6,4},{7,5},{8,10},{9,11},{10,... | collective-permute-start | bytes 786440 | tf_op jit(solution)/shard_map/ppermute | solution.py:363
  110.3 0.0 collective-permute-done.11.refs_2_
  110.3 0.5 collective-permute-start.17
  110.8 2.5 %collective-permute-done.12.refs_3_ = bf16[1024,128]{1,0:T(8,128)(2,1)S(1)} collective-permute-done((bf16[1024,128]{1,0:T(8,128)(2,1)}, bf16[1024,128]{1,0:T(8,128)(2,1)S(1)}, u32[]{:S(2)}, u32[]{:S(2)}) %collective-permute-start.12) | collective-permute-done | bytes 262176 | tf_op jit(solution)/shard_map/ppermute | solution.py:363
  113.3 0.9 collective-permute-start.18
  114.1 1.4 %collective-permute-start.19 = (bf16[128,128]{1,0:T(8,128)(2,1)S(1)}, bf16[128,128]{1,0:T(8,128)(2,1)S(1)}, u32[]{:S(2)}, u32[]{:S(2)}) collective-permute-start(bf16[128,128]{1,0:T(8,128)(2,1)S(1)} %get-tuple-element.60), channel_id=1, source_target_pairs={{0,48},{16,64},{32,80},{48,96},{64,112},{80,0},{96,16},{112,32},{1... | collective-permute-start | bytes 98312 | tf_op jit(solution)/shard_map/ppermute | solution.py:368
  115.5 2.8 %collective-permute-start.20 = (bf16[128,128]{1,0:T(8,128)(2,1)S(1)}, bf16[128,128]{1,0:T(8,128)(2,1)S(1)}, u32[]{:S(2)}, u32[]{:S(2)}) collective-permute-start(bf16[128,128]{1,0:T(8,128)(2,1)S(1)} %get-tuple-element.59), channel_id=1, source_target_pairs={{0,64},{16,80},{32,96},{48,112},{64,0},{80,16},{96,32},{112,48},{1... | collective-permute-start | bytes 98312 | tf_op jit(solution)/shard_map/ppermute | solution.py:368
  118.4 0.0 collective-permute-done.15.refs_6_
  118.4 2.9 %collective-permute-start.21 = (bf16[128,128]{1,0:T(8,128)(2,1)S(1)}, bf16[128,128]{1,0:T(8,128)(2,1)S(1)}, u32[]{:S(2)}, u32[]{:S(2)}) collective-permute-start(bf16[128,128]{1,0:T(8,128)(2,1)S(1)} %get-tuple-element.58), channel_id=1, source_target_pairs={{0,80},{16,96},{32,112},{48,0},{64,16},{80,32},{96,48},{112,64},{1... | collective-permute-start | bytes 98312 | tf_op jit(solution)/shard_map/ppermute | solution.py:368
  121.2 0.0 collective-permute-done.17.refs_0_
  121.2 1.2 collective-permute-start.22
  122.5 1.0 weights.1
  123.5 1.6 %collective-permute-done.22.refs_5_ = bf16[128,128]{1,0:T(8,128)(2,1)S(1)} collective-permute-done((bf16[128,128]{1,0:T(8,128)(2,1)S(1)}, bf16[128,128]{1,0:T(8,128)(2,1)S(1)}, u32[]{:S(2)}, u32[]{:S(2)}) %collective-permute-start.22) | collective-permute-done | bytes 32800 | tf_op jit(solution)/shard_map/ppermute | solution.py:368
  125.1 1.2 collective-permute-done.23.refs_6_
  126.4 0.0 all-to-all-done
  126.4 0.8 final.1
  127.1 0.7 copy.18
  127.8 0.7 copy.19
  (33 shorter events, 0.2 us)
Async XLA Ops:
  2.3 1.0 copy-start.1
  3.4 1.0 copy-start.2
  4.4 0.9 copy-start.3
  5.3 0.9 copy-start.4
  6.3 0.9 copy-start.5
  7.2 0.7 copy-start.6
  8.8 36.0 %copy-start = (bf16[10,128,384]{2,1,0:T(8,128)(2,1)}, bf16[10,128,384]{2,1,0:T(8,128)(2,1)S(1)}, u32[]{:S(2)}) copy-start(bf16[10,128,384]{2,1,0:T(8,128)(2,1)S(1)} %get-tuple-element.29.refs_2_.refs_4_.refs_5_.refs_6_.refs_7_) | copy-start | bytes 2949124
  8.8 10.6 %collective-permute-start = (bf16[64,640]{1,0:T(8,128)(2,1)S(1)}, bf16[64,640]{1,0:T(8,128)(2,1)S(1)}, u32[]{:S(2)}, u32[]{:S(2)}) collective-permute-start(bf16[64,640]{1,0:T(8,128)(2,1)S(1)} %get-tuple-element.28), channel_id=1, source_target_pairs={{0,16},{16,32},{32,48},{48,64},{64,80},{80,96},{96,112},{112,0},{1... | collective-permute-start | bytes 245768 | tf_op jit(solution)/shard_map/ppermute | solution.py:341
  10.5 10.4 %collective-permute-start.1 = (bf16[64,640]{1,0:T(8,128)(2,1)S(1)}, bf16[64,640]{1,0:T(8,128)(2,1)S(1)}, u32[]{:S(2)}, u32[]{:S(2)}) collective-permute-start(bf16[64,640]{1,0:T(8,128)(2,1)S(1)} %get-tuple-element.28), channel_id=1, source_target_pairs={{0,32},{16,48},{32,64},{48,80},{64,96},{80,112},{96,0},{112,16},{1... | collective-permute-start | bytes 245768 | tf_op jit(solution)/shard_map/ppermute | solution.py:341
  12.1 8.9 %collective-permute-start.2 = (bf16[64,640]{1,0:T(8,128)(2,1)S(1)}, bf16[64,640]{1,0:T(8,128)(2,1)S(1)}, u32[]{:S(2)}, u32[]{:S(2)}) collective-permute-start(bf16[64,640]{1,0:T(8,128)(2,1)S(1)} %get-tuple-element.28), channel_id=1, source_target_pairs={{0,48},{16,64},{32,80},{48,96},{64,112},{80,0},{96,16},{112,32},{1... | collective-permute-start | bytes 245768 | tf_op jit(solution)/shard_map/ppermute | solution.py:341
  14.3 7.5 %collective-permute-start.3 = (bf16[64,640]{1,0:T(8,128)(2,1)S(1)}, bf16[64,640]{1,0:T(8,128)(2,1)S(1)}, u32[]{:S(2)}, u32[]{:S(2)}) collective-permute-start(bf16[64,640]{1,0:T(8,128)(2,1)S(1)} %get-tuple-element.28), channel_id=1, source_target_pairs={{0,64},{16,80},{32,96},{48,112},{64,0},{80,16},{96,32},{112,48},{1... | collective-permute-start | bytes 245768 | tf_op jit(solution)/shard_map/ppermute | solution.py:341
  16.2 5.6 %collective-permute-start.4 = (bf16[64,640]{1,0:T(8,128)(2,1)S(1)}, bf16[64,640]{1,0:T(8,128)(2,1)S(1)}, u32[]{:S(2)}, u32[]{:S(2)}) collective-permute-start(bf16[64,640]{1,0:T(8,128)(2,1)S(1)} %get-tuple-element.28), channel_id=1, source_target_pairs={{0,80},{16,96},{32,112},{48,0},{64,16},{80,32},{96,48},{112,64},{1... | collective-permute-start | bytes 245768 | tf_op jit(solution)/shard_map/ppermute | solution.py:341
  19.4 4.5 %collective-permute-start.5 = (bf16[64,640]{1,0:T(8,128)(2,1)S(1)}, bf16[64,640]{1,0:T(8,128)(2,1)S(1)}, u32[]{:S(2)}, u32[]{:S(2)}) collective-permute-start(bf16[64,640]{1,0:T(8,128)(2,1)S(1)} %get-tuple-element.28), channel_id=1, source_target_pairs={{0,96},{16,112},{32,0},{48,16},{64,32},{80,48},{96,64},{112,80},{1... | collective-permute-start | bytes 245768 | tf_op jit(solution)/shard_map/ppermute | solution.py:341
  20.9 4.5 %collective-permute-start.6 = (bf16[64,640]{1,0:T(8,128)(2,1)S(1)}, bf16[64,640]{1,0:T(8,128)(2,1)S(1)}, u32[]{:S(2)}, u32[]{:S(2)}) collective-permute-start(bf16[64,640]{1,0:T(8,128)(2,1)S(1)} %get-tuple-element.28), channel_id=1, source_target_pairs={{0,112},{16,0},{32,16},{48,32},{64,48},{80,64},{96,80},{112,96},{1... | collective-permute-start | bytes 245768 | tf_op jit(solution)/shard_map/ppermute | solution.py:341
  21.0 6.8 %collective-permute-start.8 = (bf16[10,128,384]{2,1,0:T(8,128)(2,1)S(1)}, bf16[10,128,384]{2,1,0:T(8,128)(2,1)}, u32[]{:S(2)}, u32[]{:S(2)}) collective-permute-start(bf16[10,128,384]{2,1,0:T(8,128)(2,1)S(1)} %get-tuple-element.30), channel_id=1, source_target_pairs={{0,1},{1,0},{2,3},{3,2},{4,5},{5,4},{6,7},{7,6},{8,9},{9,8},{10,11... | collective-permute-start | bytes 2949128 | tf_op jit(solution)/shard_map/ppermute | solution.py:343
  25.4 2.4 %collective-permute-start.7 = (bf16[512,640]{1,0:T(8,128)(2,1)S(1)}, bf16[512,640]{1,0:T(8,128)(2,1)S(1)}, u32[]{:S(2)}, u32[]{:S(2)}) collective-permute-start(bf16[512,640]{1,0:T(8,128)(2,1)S(1)} %constant_dynamic-update-slice_fusion.refs_0_), channel_id=1, source_target_pairs={{0,1},{1,0},{2,3},{3,2},{4,5},{5,4},{6,7},{7,6},{8,9},{9,8},{10,11... | collective-permute-start | bytes 1966088 | tf_op jit(solution)/shard_map/ppermute | solution.py:345
  44.9 0.7 copy-start.7
  45.6 0.7 copy-start.9
  46.3 0.7 copy-start.11
  64.6 13.8 %copy-start.12 = (bf16[1024,128]{1,0:T(8,128)(2,1)S(1)}, bf16[1024,128]{1,0:T(8,128)(2,1)}, u32[]{:S(2)}) copy-start(bf16[1024,128]{1,0:T(8,128)(2,1)} %copy-done.11) | copy-start | bytes 786436
  64.6 19.4 %copy-start.10 = (bf16[1024,128]{1,0:T(8,128)(2,1)S(1)}, bf16[1024,128]{1,0:T(8,128)(2,1)}, u32[]{:S(2)}) copy-start(bf16[1024,128]{1,0:T(8,128)(2,1)} %copy-done.9) | copy-start | bytes 786436
  64.6 20.0 %copy-start.8 = (bf16[1024,128]{1,0:T(8,128)(2,1)S(1)}, bf16[1024,128]{1,0:T(8,128)(2,1)}, u32[]{:S(2)}) copy-start(bf16[1024,128]{1,0:T(8,128)(2,1)} %copy-done.7) | copy-start | bytes 786436
  64.6 2.9 %collective-permute-start.16 = (bf16[640,640]{1,0:T(8,128)(2,1)}, bf16[640,640]{1,0:T(8,128)(2,1)S(1)}, u32[]{:S(2)}, u32[]{:S(2)}) collective-permute-start(bf16[640,640]{1,0:T(8,128)(2,1)} %get-tuple-element.43), channel_id=1, source_target_pairs={{0,1},{1,0},{2,3},{3,2},{4,5},{5,4},{6,7},{7,6},{8,9},{9,8},{10,11... | collective-permute-start | bytes 2457608 | tf_op jit(solution)/shard_map/ppermute | solution.py:365
  68.7 57.7 %all-to-all-start = ((bf16[64,8,640]{2,1,0:T(8,128)(2,1)}), bf16[64,8,640]{2,1,0:T(8,128)(2,1)S(1)}, u32[]{:S(2)}, u32[]{:S(2)}) async-start(bf16[64,8,640]{2,1,0:T(8,128)(2,1)} %bitcast.21), calls=%async_computation | async-start | bytes 1310720 | tf_op jit(solution)/shard_map/all_to_all | solution.py:376
  78.4 21.3 %collective-permute-start.9 = (bf16[1024,128]{1,0:T(8,128)(2,1)S(1)}, bf16[1024,128]{1,0:T(8,128)(2,1)S(1)}, u32[]{:S(2)}, u32[]{:S(2)}) collective-permute-start(bf16[1024,128]{1,0:T(8,128)(2,1)S(1)} %copy-done.12), channel_id=1, source_target_pairs={{0,10},{1,11},{2,8},{3,9},{4,14},{5,15},{6,12},{7,13},{8,2},{9,3},... | collective-permute-start | bytes 786440 | tf_op jit(solution)/shard_map/ppermute | solution.py:363
  84.0 24.5 %collective-permute-start.10 = (bf16[1024,128]{1,0:T(8,128)(2,1)S(1)}, bf16[1024,128]{1,0:T(8,128)(2,1)S(1)}, u32[]{:S(2)}, u32[]{:S(2)}) collective-permute-start(bf16[1024,128]{1,0:T(8,128)(2,1)S(1)} %copy-done.10), channel_id=1, source_target_pairs={{0,8},{1,9},{2,10},{3,11},{4,12},{5,13},{6,14},{7,15},{8,0},{9,1},... | collective-permute-start | bytes 786440 | tf_op jit(solution)/shard_map/ppermute | solution.py:363
  84.6 25.7 %collective-permute-start.11 = (bf16[1024,128]{1,0:T(8,128)(2,1)S(1)}, bf16[1024,128]{1,0:T(8,128)(2,1)S(1)}, u32[]{:S(2)}, u32[]{:S(2)}) collective-permute-start(bf16[1024,128]{1,0:T(8,128)(2,1)S(1)} %copy-done.8), channel_id=1, source_target_pairs={{0,6},{1,7},{2,4},{3,5},{4,10},{5,11},{6,8},{7,9},{8,14},{9,15},{1... | collective-permute-start | bytes 786440 | tf_op jit(solution)/shard_map/ppermute | solution.py:363
  86.0 27.2 %collective-permute-start.12 = (bf16[1024,128]{1,0:T(8,128)(2,1)}, bf16[1024,128]{1,0:T(8,128)(2,1)S(1)}, u32[]{:S(2)}, u32[]{:S(2)}) collective-permute-start(bf16[1024,128]{1,0:T(8,128)(2,1)} %get-tuple-element.34), channel_id=1, source_target_pairs={{0,4},{1,5},{2,6},{3,7},{4,8},{5,9},{6,10},{7,11},{8,12},{9,13},{1... | collective-permute-start | bytes 786440 | tf_op jit(solution)/shard_map/ppermute | solution.py:363
  87.5 26.7 %collective-permute-start.13 = (bf16[1024,128]{1,0:T(8,128)(2,1)}, bf16[1024,128]{1,0:T(8,128)(2,1)S(1)}, u32[]{:S(2)}, u32[]{:S(2)}) collective-permute-start(bf16[1024,128]{1,0:T(8,128)(2,1)} %get-tuple-element.36), channel_id=1, source_target_pairs={{0,14},{1,15},{2,12},{3,13},{4,2},{5,3},{6,0},{7,1},{8,6},{9,7},{1... | collective-permute-start | bytes 786440 | tf_op jit(solution)/shard_map/ppermute | solution.py:363
  99.7 15.8 %collective-permute-start.14 = (bf16[1024,128]{1,0:T(8,128)(2,1)}, bf16[1024,128]{1,0:T(8,128)(2,1)S(1)}, u32[]{:S(2)}, u32[]{:S(2)}) collective-permute-start(bf16[1024,128]{1,0:T(8,128)(2,1)} %get-tuple-element.37), channel_id=1, source_target_pairs={{0,12},{1,13},{2,14},{3,15},{4,0},{5,1},{6,2},{7,3},{8,4},{9,5},{1... | collective-permute-start | bytes 786440 | tf_op jit(solution)/shard_map/ppermute | solution.py:363
  108.5 9.9 %collective-permute-start.15 = (bf16[1024,128]{1,0:T(8,128)(2,1)S(1)}, bf16[1024,128]{1,0:T(8,128)(2,1)S(1)}, u32[]{:S(2)}, u32[]{:S(2)}) collective-permute-start(bf16[1024,128]{1,0:T(8,128)(2,1)S(1)} %get-tuple-element.38), channel_id=1, source_target_pairs={{0,2},{1,3},{2,0},{3,1},{4,6},{5,7},{6,4},{7,5},{8,10},{9,11},{10,... | collective-permute-start | bytes 786440 | tf_op jit(solution)/shard_map/ppermute | solution.py:363
  110.3 10.9 %collective-permute-start.17 = (bf16[128,128]{1,0:T(8,128)(2,1)S(1)}, bf16[128,128]{1,0:T(8,128)(2,1)S(1)}, u32[]{:S(2)}, u32[]{:S(2)}) collective-permute-start(bf16[128,128]{1,0:T(8,128)(2,1)S(1)} %get-tuple-element.62), channel_id=1, source_target_pairs={{0,16},{16,32},{32,48},{48,64},{64,80},{80,96},{96,112},{112,0},{1... | collective-permute-start | bytes 98312 | tf_op jit(solution)/shard_map/ppermute | solution.py:368
  113.3 9.2 %collective-permute-start.18 = (bf16[128,128]{1,0:T(8,128)(2,1)S(1)}, bf16[128,128]{1,0:T(8,128)(2,1)S(1)}, u32[]{:S(2)}, u32[]{:S(2)}) collective-permute-start(bf16[128,128]{1,0:T(8,128)(2,1)S(1)} %get-tuple-element.61), channel_id=1, source_target_pairs={{0,32},{16,48},{32,64},{48,80},{64,96},{80,112},{96,0},{112,16},{1... | collective-permute-start | bytes 98312 | tf_op jit(solution)/shard_map/ppermute | solution.py:368
  114.1 9.3 %collective-permute-start.19 = (bf16[128,128]{1,0:T(8,128)(2,1)S(1)}, bf16[128,128]{1,0:T(8,128)(2,1)S(1)}, u32[]{:S(2)}, u32[]{:S(2)}) collective-permute-start(bf16[128,128]{1,0:T(8,128)(2,1)S(1)} %get-tuple-element.60), channel_id=1, source_target_pairs={{0,48},{16,64},{32,80},{48,96},{64,112},{80,0},{96,16},{112,32},{1... | collective-permute-start | bytes 98312 | tf_op jit(solution)/shard_map/ppermute | solution.py:368
  115.5 8.0 %collective-permute-start.20 = (bf16[128,128]{1,0:T(8,128)(2,1)S(1)}, bf16[128,128]{1,0:T(8,128)(2,1)S(1)}, u32[]{:S(2)}, u32[]{:S(2)}) collective-permute-start(bf16[128,128]{1,0:T(8,128)(2,1)S(1)} %get-tuple-element.59), channel_id=1, source_target_pairs={{0,64},{16,80},{32,96},{48,112},{64,0},{80,16},{96,32},{112,48},{1... | collective-permute-start | bytes 98312 | tf_op jit(solution)/shard_map/ppermute | solution.py:368
  118.4 5.1 %collective-permute-start.21 = (bf16[128,128]{1,0:T(8,128)(2,1)S(1)}, bf16[128,128]{1,0:T(8,128)(2,1)S(1)}, u32[]{:S(2)}, u32[]{:S(2)}) collective-permute-start(bf16[128,128]{1,0:T(8,128)(2,1)S(1)} %get-tuple-element.58), channel_id=1, source_target_pairs={{0,80},{16,96},{32,112},{48,0},{64,16},{80,32},{96,48},{112,64},{1... | collective-permute-start | bytes 98312 | tf_op jit(solution)/shard_map/ppermute | solution.py:368
  121.2 3.9 %collective-permute-start.22 = (bf16[128,128]{1,0:T(8,128)(2,1)S(1)}, bf16[128,128]{1,0:T(8,128)(2,1)S(1)}, u32[]{:S(2)}, u32[]{:S(2)}) collective-permute-start(bf16[128,128]{1,0:T(8,128)(2,1)S(1)} %get-tuple-element.57), channel_id=1, source_target_pairs={{0,96},{16,112},{32,0},{48,16},{64,32},{80,48},{96,64},{112,80},{1... | collective-permute-start | bytes 98312 | tf_op jit(solution)/shard_map/ppermute | solution.py:368
  122.5 3.9 %collective-permute-start.23 = (bf16[128,128]{1,0:T(8,128)(2,1)S(1)}, bf16[128,128]{1,0:T(8,128)(2,1)S(1)}, u32[]{:S(2)}, u32[]{:S(2)}) collective-permute-start(bf16[128,128]{1,0:T(8,128)(2,1)S(1)} %get-tuple-element.56), channel_id=1, source_target_pairs={{0,112},{16,0},{32,16},{48,32},{64,48},{80,64},{96,80},{112,96},{1... | collective-permute-start | bytes 98312 | tf_op jit(solution)/shard_map/ppermute | solution.py:368

commit v2 on v0

v2 whole, which is shorter than its diff:
```python
import functools

import jax
import jax.numpy as jnp
from jax import lax
from jax.experimental import pallas as pl
from jax.experimental.pallas import tpu as pltpu
from jax.sharding import PartitionSpec as P

f32 = jnp.float32
bf16 = jnp.bfloat16
LOG2E = 1.4426950408889634

ROWS = 128
SLEN = 64
LAT = 512
ROPE = 64
NOPE = 128
KW = 640
HW = 384
W = 2 * ROWS
PK = 1024
AK = PK + 2 * ROWS
SCALE = 1.0 / (NOPE + ROPE) ** 0.5


def nt(a, b):
    return lax.dot_general(a, b, (((1,), (1,)), ((), ())), preferred_element_type=f32)


def nn(a, b):
    return lax.dot_general(a, b, (((1,), (0,)), ((), ())), preferred_element_type=f32)


def params(mib=60):
    return pltpu.CompilerParams(vmem_limit_bytes=mib * 2**20)


def cost(flops, nbytes):
    return pl.CostEstimate(flops=flops, bytes_accessed=nbytes, transcendentals=0)


VM = pl.BlockSpec(memory_space=pltpu.VMEM)
SM = pl.BlockSpec(memory_space=pltpu.SMEM)


def keys_kernel(lat, rope_t, kv):
    core = lax.axis_index("comp") % 2
    x = jnp.concatenate(
        [lat[...].astype(f32), rope_t[...].astype(f32).T, jnp.zeros((ROWS, KW - LAT - ROPE), f32)],
        axis=1,
    ).reshape(8, 2, 8, KW)
    x = jnp.where(core == 0, x[:, 0], x[:, 1]).reshape(64, KW).astype(bf16)
    for k in range(8):
        kv[k] = x


def keys(lat, rope_t):
    return pl.pallas_call(
        keys_kernel,
        out_shape=jax.ShapeDtypeStruct((8, 64, KW), bf16),
        in_specs=[VM, VM],
        out_specs=VM,
        compiler_params=params(),
        name="keys",
    )(lat, rope_t)


def prep_kernel(info, lens, *refs):
    core = info[0]
    row = lax.broadcasted_iota(jnp.int32, (ROWS, 1), 0)
    limit = jnp.where(row < SLEN, lens[0], lens[1])
    valid = (row % SLEN) < limit
    lane = lax.broadcasted_iota(jnp.int32, (ROWS, 2 * ROPE), 1)
    keep, send, ww = refs[-3:]
    for h in range(2):
        qn_k, qn_s, do_k, do_s, qr, wk, wv = refs[7 * h : 7 * h + 7]
        tile = qr[...].astype(f32)
        flipped = pltpu.roll(tile, ROPE, 1)
        for out, qn, do, par in ((keep, qn_k, do_k, core), (send, qn_s, do_s, 1 - core)):
            out[h, :, 0:NOPE] = qn[...]
            x = jnp.where(lane < ROPE, jnp.where(par == 0, tile, flipped), 0.0)
            out[h, :, NOPE : 2 * NOPE] = x.astype(bf16)
            g = do[...]
            out[h, :, 2 * NOPE : HW] = jnp.where(valid, g, jnp.zeros_like(g))
        ww[h, 0:NOPE] = wk[0]
        ww[h, NOPE : 2 * NOPE] = wv[0].T


def own_kernel(clat, crop_t, after, out):
    out[:, 0:LAT] = clat[...]
    pad = jnp.zeros((ROWS, KW - LAT - ROPE), bf16)
    crop = crop_t[...].astype(f32).T.astype(bf16)
    out[:, LAT:KW] = jnp.concatenate([crop, pad], axis=1)


def own_keys(clat, crop_t, after):
    return pl.pallas_call(
        own_kernel,
        out_shape=jax.ShapeDtypeStruct((ROWS, KW), bf16),
        in_specs=[VM, VM, pl.BlockSpec(memory_space=pl.ANY)],
        out_specs=VM,
        compiler_params=params(4),
        cost_estimate=cost(3 * 10**9, 4 * 2**20),
        name="own_keys",
    )(clat, crop_t, after)


def prep(info, lens, qn, qr, do, w_uk, w_uv):
    def head(i, info, flip):
        core = info[0]
        return 2 * info[5 + i] + (1 - core if flip else core)

    in_specs, ops = [], []
    for h in range(2):

        def cols(flip, h=h):
            return pl.BlockSpec((ROWS, NOPE), lambda i, info, lens: (0, head(2 * i + h, info, flip)))

        def weight(a, b, h=h):
            return pl.BlockSpec(
                (1, a, b), lambda i, info, lens: (head(2 * i + h, info, False), 0, 0)
            )

        def pair(h=h):
            return pl.BlockSpec((ROWS, 2 * ROPE), lambda i, info, lens: (0, info[5 + 2 * i + h]))

        in_specs += [cols(False), cols(True), cols(False), cols(True), pair()]
        in_specs += [weight(NOPE, LAT), weight(LAT, NOPE)]
        ops += [qn, qn, do, do, qr, w_uk, w_uv]
    out = pl.BlockSpec((2, ROWS, HW), lambda i, info, lens: (i, 0, 0))
    return pl.pallas_call(
        prep_kernel,
        out_shape=(
            jax.ShapeDtypeStruct((8, ROWS, HW), bf16),
            jax.ShapeDtypeStruct((8, ROWS, HW), bf16),
            jax.ShapeDtypeStruct((8, 2 * NOPE, LAT), bf16),
        ),
        grid_spec=pltpu.PrefetchScalarGridSpec(
            num_scalar_prefetch=2,
            grid=(4,),
            in_specs=in_specs,
            out_specs=(
                out,
                out,
                pl.BlockSpec((2, 2 * NOPE, LAT), lambda i, info, lens: (i, 0, 0)),
            ),
        ),
        compiler_params=params(),
        cost_estimate=cost(10**9, 4 * 2**20),
        name="prep",
    )(info, lens, *ops)


HPS = 2
STEPS = 2


def attend_kernel(last, *refs):
    refs = list(refs)

    def take(n):
        return [refs.pop(0) for _ in range(n)]

    kva, kvb, ckeep, crecv, keep, recv, ww = take(7)
    if last:
        (acc,) = take(1)
        rest, stay, give_a, give_b, give_c = take(5)
    else:
        plus, minus, acc = take(3)
    kall, kt, kx, s_ref, dp_ref, pb, ds, xy, rop = take(9)
    step = pl.program_id(0)
    CH = 128
    NC = (PK + ROWS) // CH

    @pl.when(step == 0)
    def _():
        for at, ref in ((0, kva), (512, kvb)):
            kall[at : at + 512] = ref[:, 0:LAT]
            for h in range(HPS):
                kx[h, at : at + 512, 128:256] = ref[:, LAT:KW]
        for at, ref in ((PK, ckeep), (PK + ROWS, crecv)):
            kall[at : at + ROWS] = ref[:, 0:LAT]
            for h in range(HPS):
                kx[h, at : at + ROWS, 128:256] = ref[:, LAT:KW]
        for b in range(AK // 256):
            kt[:, b * 256 : b * 256 + 256] = kall[b * 256 : b * 256 + 256, :].T
        zero = jnp.zeros((ROWS, ROWS), bf16)
        for ref in (pb, ds):
            for h in range(HPS):
                ref[h, PK : PK + ROWS, ROWS:W] = zero
                ref[h, PK + ROWS : AK, 0:ROWS] = zero
        rop[...] = acc[:, LAT:KW] if last else jnp.zeros_like(rop)

    iu = lax.broadcasted_iota(jnp.int32, (ROWS, W), 0)
    it = lax.broadcasted_iota(jnp.int32, (ROWS, W), 1) % ROWS
    seen = ((iu // SLEN) == (it // SLEN)) & (iu <= it)
    queries = []
    for h in range(HPS):
        at = pl.multiple_of((step * HPS + h) * W, W)
        r = nt(kall[...], ww[pl.ds(at, W), :])
        kx[h, :, 0:128] = r[:, 0:128].astype(bf16)
        kx[h, :, 256:384] = r[:, 128:256].astype(bf16)
    for h in range(HPS):
        qx = jnp.concatenate([keep[h, :, 0:256], recv[h, :, 0:256]], axis=0)
        g = jnp.concatenate([keep[h, :, 256:HW], recv[h, :, 256:HW]], axis=0)
        queries.append((qx, g))
        s_ref[h, 0:PK] = nt(kx[h, 0:PK, 0:256], qx)
        own = nt(kx[h, PK:AK, 0:256], qx)
        own = jnp.concatenate([own[0:ROWS, 0:ROWS], own[ROWS:W, ROWS:W]], axis=1)
        s_ref[h, PK : PK + ROWS] = jnp.where(seen, own, -jnp.inf)
        dp_ref[h, 0:PK] = nt(kx[h, 0:PK, 256:384], g)
        own = nt(kx[h, PK:AK, 256:384], g)
        dp_ref[h, PK : PK + ROWS] = jnp.concatenate(
            [own[0:ROWS, 0:ROWS], own[ROWS:W, ROWS:W]], axis=1
        )
    both = []
    for h in range(HPS):
        qx, g = queries[h]
        top = jnp.full((8, W), -jnp.inf, f32)
        for c in range(NC):
            x = s_ref[h, c * CH : c * CH + CH].reshape(CH // 8, 8, W)
            top = jnp.maximum(top, jnp.max(x, axis=0))
        top = jnp.max(top, axis=0, keepdims=True)
        total = jnp.zeros((8, W), f32)
        delta = jnp.zeros((8, W), f32)
        for c in range(NC):
            cs = slice(c * CH, c * CH + CH)
            e = jnp.exp2((s_ref[h, cs] - top) * (SCALE * LOG2E))
            s_ref[h, cs] = e
            total = total + jnp.sum(e.reshape(CH // 8, 8, W), axis=0)
            delta = delta + jnp.sum((e * dp_ref[h, cs]).reshape(CH // 8, 8, W), axis=0)
        inv = 1.0 / jnp.sum(total, axis=0, keepdims=True)
        delta = jnp.sum(delta, axis=0, keepdims=True) * inv
        cinv = inv * SCALE
        for c in range(NC):
            cs = slice(c * CH, c * CH + CH)
            e = s_ref[h, cs]
            p = (e * inv).astype(bf16)
            d = (e * cinv * (dp_ref[h, cs] - delta)).astype(bf16)
            if c < NC - 1:
                pb[h, cs] = p
                ds[h, cs] = d
            else:
                for ref, x in ((pb, p), (ds, d)):
                    ref[h, PK : PK + ROWS, 0:ROWS] = x[:, 0:ROWS]
                    ref[h, PK + ROWS : AK, ROWS:W] = x[:, ROWS:W]
        x = nn(ds[h], qx)
        rop[...] += x[:, 128:256]
        y = nn(pb[h], g)
        xx = jnp.concatenate([x[:, 0:128].astype(bf16), y.astype(bf16)], axis=1)
        at = pl.multiple_of((step * HPS + h) * W, W)
        xy[:, pl.ds(at, W)] = xx
        both.append(xx)
    for h in range(HPS):
        out = nn(kt[...], both[h]).astype(bf16)
        if last:
            rest[h] = out
        elif h == 0:
            plus[0] = out
        else:
            minus[0] = out

    @pl.when(step == STEPS - 1)
    def _():
        r = nn(xy[...], ww[...])
        if last:
            r = jnp.concatenate([r + acc[:, 0:LAT], rop[...]], axis=1).astype(bf16)
            stay[0:512] = r[0:512]
            stay[512:640] = r[PK : PK + ROWS]
            give_a[...] = r[512:768]
            give_b[...] = r[768:1024]
            give_c[...] = r[PK + ROWS : AK]
        else:
            acc[:, 0:LAT] = r
            acc[:, LAT:KW] = rop[...]


def attend(last, kva, kvb, ckeep, crecv, keep, recv, ww, acc=None):
    base = 2 if last else 0

    def full(a, b):
        return pl.BlockSpec((a, b), lambda s: (0, 0))

    def block(n):
        return pl.BlockSpec((n, LAT, 2 * NOPE), lambda s: (s, 0, 0))

    def shape(n):
        return jax.ShapeDtypeStruct((n, LAT, 2 * NOPE), bf16)

    heads = pl.BlockSpec((HPS, ROWS, HW), lambda s: (base + s, 0, 0))
    ckeys = full(ROWS, KW)
    weights = pl.BlockSpec((STEPS * HPS * W, LAT), lambda s: (base // 2, 0))
    in_specs = [full(512, KW), full(512, KW), ckeys, ckeys, heads, heads, weights]
    ops = [kva, kvb, ckeep, crecv, keep, recv, ww]
    scratch = [
        pltpu.VMEM((AK, LAT), bf16),
        pltpu.VMEM((LAT, AK), bf16),
        pltpu.VMEM((HPS, AK, 384), bf16),
        pltpu.VMEM((HPS, PK + ROWS, W), f32),
        pltpu.VMEM((HPS, PK + ROWS, W), f32),
        pltpu.VMEM((HPS, AK, W), bf16),
        pltpu.VMEM((HPS, AK, W), bf16),
        pltpu.VMEM((AK, STEPS * HPS * W), bf16),
        pltpu.VMEM((AK, 128), f32),
    ]
    if last:
        in_specs.append(full(AK, KW))
        ops.append(acc)
        out_shape = [shape(4)]
        out_specs = [block(2)]
        for n in (640, 256, 256, ROWS):
            out_shape.append(jax.ShapeDtypeStruct((n, KW), bf16))
            out_specs.append(full(n, KW))
    else:
        out_shape = (shape(2), shape(2), jax.ShapeDtypeStruct((AK, KW), f32))
        out_specs = (block(1), block(1), full(AK, KW))
    return pl.pallas_call(
        functools.partial(attend_kernel, last),
        out_shape=out_shape,
        grid=(STEPS,),
        in_specs=in_specs,
        out_specs=out_specs,
        scratch_shapes=scratch,
        compiler_params=params(36),
        cost_estimate=cost(10**10, 10 * 2**20),
        name="attend",
    )(*ops)


YW = 768


def join_kernel(info, stay, got_a, got_b, got_c, o0, o1, o2, o3):
    y = info[1]
    crope = stay[512:640, LAT:KW].astype(f32) + got_c[:, LAT:KW].astype(f32)
    for k, out in enumerate((o0, o1, o2, o3)):
        to = lax.rem(y + k, 4)
        at = pl.multiple_of(to * 128, 128)
        row = pl.ds(at, 128)
        half = pl.ds(pl.multiple_of(lax.rem(to, 2) * 128, 128), 128)
        got = jnp.where(to < 2, got_a[half, :].astype(f32), got_b[half, :].astype(f32))
        x = stay[row, :].astype(f32) + got
        c = stay[512:640, row].astype(f32) + got_c[:, row].astype(f32)
        r = pltpu.roll(crope, lax.rem(KW - LAT + ROPE - 16 * to, KW - LAT), 1)
        lane = lax.broadcasted_iota(jnp.int32, (ROWS, KW - LAT), 1)
        tail = jnp.where(lane < ROPE, x[:, LAT:KW], r)
        out[:, 0:LAT] = x[:, 0:LAT].astype(bf16)
        out[:, LAT:KW] = tail.astype(bf16)
        out[:, KW:YW] = c.astype(bf16)


def join(info, stay, *got):
    return pl.pallas_call(
        join_kernel,
        out_shape=(jax.ShapeDtypeStruct((128, YW), bf16),) * 4,
        in_specs=[SM] + [VM] * 4,
        out_specs=(VM,) * 4,
        compiler_params=params(24),
        name="join",
    )(info, stay, *got)


def sum_y_kernel(info, a0, a1, a2, a3, out, mine, send):
    xl = info[2]
    x = a0[...].astype(f32) + a1[...].astype(f32) + a2[...].astype(f32) + a3[...].astype(f32)
    out[...] = x[:, 0:KW].astype(bf16)
    lane = lax.broadcasted_iota(jnp.int32, (ROWS, 128), 1)
    lat, rope = x[:, KW:YW], x[:, LAT:KW]
    for ref, flip in ((mine, 0), (send, 1)):
        to = xl ^ flip
        c = pltpu.roll(lat, lax.rem(128 - 64 * to, 128), 1)
        r = pltpu.roll(rope, lax.rem(128 - 8 * to, 128), 1)
        ref[...] = jnp.where(lane < 64, c, r).astype(bf16)


def sum_y(info, *parts):
    return pl.pallas_call(
        sum_y_kernel,
        out_shape=(
            jax.ShapeDtypeStruct((128, KW), bf16),
            jax.ShapeDtypeStruct((ROWS, 128), bf16),
            jax.ShapeDtypeStruct((ROWS, 128), bf16),
        ),
        in_specs=[SM] + [VM] * 4,
        out_specs=(VM,) * 3,
        compiler_params=params(24),
        name="sum_y",
    )(info, *parts)


def final_kernel(mine, got, dlat, after, ol, orp, ocl, ocr):
    c = (mine[...].astype(f32) + got[...].astype(f32)).T
    ocl[...] = c[0:64]
    ocr[...] = c[64:72]
    x = jnp.sum(dlat[...].astype(f32).reshape(16, 8, KW), axis=0)
    ol[...] = x[:, 0:LAT]
    orp[...] = x[:, LAT : LAT + ROPE]


def final(mine, got, dlat, after):
    return pl.pallas_call(
        final_kernel,
        out_shape=(
            jax.ShapeDtypeStruct((8, LAT), f32),
            jax.ShapeDtypeStruct((8, ROPE), f32),
            jax.ShapeDtypeStruct((64, ROWS), f32),
            jax.ShapeDtypeStruct((8, ROWS), f32),
        ),
        in_specs=[VM] * 4,
        out_specs=(VM,) * 4,
        compiler_params=params(24),
        name="final",
    )(mine, got, dlat, after)


def ring_kernel(rest, p, m, after, a, b):
    a[...] = (rest[0].astype(f32) + p[0].astype(f32)).astype(bf16)
    b[...] = (rest[1].astype(f32) + m[0].astype(f32)).astype(bf16)


def ring(rest, p, m, after):
    block = jax.ShapeDtypeStruct((LAT, 2 * NOPE), bf16)
    return pl.pallas_call(
        ring_kernel,
        out_shape=(block, block),
        in_specs=[VM] * 3 + [pl.BlockSpec(memory_space=pl.ANY)],
        out_specs=(VM, VM),
        compiler_params=params(24),
        name="ring",
    )(rest, p, m, after)


def pair_kernel(info, rest, p, m, a, b, mine, send):
    first = rest[2].astype(f32) + m[1].astype(f32) + a[...].astype(f32)
    second = rest[3].astype(f32) + p[1].astype(f32) + b[...].astype(f32)
    own = info[3] == 0
    mine[...] = jnp.where(own, first, second).astype(bf16)
    send[...] = jnp.where(own, second, first).astype(bf16)


def pair(info, rest, p, m, a, b):
    block = jax.ShapeDtypeStruct((LAT, 2 * NOPE), bf16)
    return pl.pallas_call(
        pair_kernel,
        out_shape=(block, block),
        in_specs=[SM] + [VM] * 5,
        out_specs=(VM, VM),
        compiler_params=params(24),
        name="pair",
    )(info, rest, p, m, a, b)


def weights_kernel(mine, got, dwk, dwv, done):
    done[...] = jnp.zeros_like(done)
    x = mine[...].astype(f32) + got[...].astype(f32)
    dwk[...] = x[:, 0:NOPE].T
    dwv[...] = x[:, NOPE : 2 * NOPE]


def weights(mine, got):
    return pl.pallas_call(
        weights_kernel,
        out_shape=(
            jax.ShapeDtypeStruct((NOPE, LAT), f32),
            jax.ShapeDtypeStruct((LAT, NOPE), f32),
            jax.ShapeDtypeStruct((8, 128), f32),
        ),
        in_specs=[VM, VM],
        out_specs=(VM, VM, VM),
        compiler_params=params(24),
        name="weights",
    )(mine, got)


def local(q_nope, q_rope, d_out, w_uk, w_uv, latent, rope_key, comp_latent, comp_rope, lengths):
    comp = lax.axis_index("comp").astype(jnp.int32)
    prm = lax.axis_index("prompt").astype(jnp.int32)
    z = comp // 4
    far, after, before = (z + 2) % 4, (z + 1) % 4, (z + 3) % 4
    info = jnp.stack(
        [comp % 2, prm // 2, prm % 2, (comp // 2) % 2, z]
        + [2 * far, 2 * far + 1, 2 * after + 1, 2 * before]
        + [2 * after, 2 * before + 1, 2 * z, 2 * z + 1]
    )
    swap = [(c, c ^ 1) for c in range(16)]
    up = [(c, (c + 4) % 16) for c in range(16)]
    down = [(c, (c + 12) % 16) for c in range(16)]
    kv = keys(latent, rope_key.T)
    kva = lax.all_to_all(kv, "prompt", 0, 0, tiled=True).reshape(512, KW)
    keep, send, ww = prep(
        info, lengths, q_nope, q_rope, d_out, w_uk, w_uv
    )
    recv = lax.ppermute(send, "comp", swap)
    ckeep = own_keys(comp_latent, comp_rope.T, ww)
    crecv = lax.ppermute(ckeep, "comp", swap)
    kvb = lax.ppermute(kva, "comp", swap)
    ops = (kva, kvb, ckeep, crecv, keep, recv, ww.reshape(8 * W, LAT))
    plus, minus, acc = attend(False, *ops)
    plus = lax.ppermute(plus, "comp", up)
    minus = lax.ppermute(minus, "comp", down)
    rest, stay, *give = attend(True, *ops, acc)
    got = [lax.ppermute(x, "comp", swap) for x in give]
    o = join(info, stay, *got)
    o = [o[0]] + [
        lax.ppermute(o[k], "prompt", [(i, (i + 2 * k) % 8) for i in range(8)]) for k in (1, 2, 3)
    ]
    a, b = ring(rest, plus, minus, o[0])
    a = lax.ppermute(a, "comp", up)
    b = lax.ppermute(b, "comp", down)
    dlat, cmine, csend = sum_y(info, *o)
    planes = [
        [(2 * y + xl) * 16 + 2 * i + core for xl in range(2) for i in range(8)]
        for y in range(4)
        for core in range(2)
    ]
    cgot = lax.ppermute(csend, "prompt", [(i, i ^ 1) for i in range(8)])
    dlat = lax.all_to_all(
        dlat, ("prompt", "comp"), 0, 0, tiled=True, axis_index_groups=planes
    )
    mine, send = pair(info, rest, plus, minus, a, b)
    other = lax.ppermute(send, "comp", [(c, c ^ 2) for c in range(16)])
    dwk, dwv, done = weights(mine, other)
    ol, orp, ocl, ocr = final(cmine, cgot, dlat, done)
    return dwk[None], dwv[None], ol, orp, ocl.T, ocr.T


def solution(mesh):
    in_specs = (
        P("comp", "prompt"),
        P("comp", "prompt"),
        P("comp", "prompt"),
        P("prompt", None, None),
        P("prompt", None, None),
        P("prompt", None),
        P("prompt", None),
        P("comp", None),
        P("comp", None),
        P("comp"),
    )
    out_specs = (
        P(("prompt", "comp"), None, None),
        P(("prompt", "comp"), None, None),
        P(("prompt", "comp"), None),
        P(("prompt", "comp"), None),
        P("comp", "prompt"),
        P("comp", "prompt"),
    )
    return jax.shard_map(local, mesh=mesh, in_specs=in_specs, out_specs=out_specs, check_vma=False)
```

time: 1250 us -> 81.3 us (0.07)
  waiting for transfers between devices: 963 us -> 18.6 us
  matrix products: 106 us -> 0 us
  blocking collectives: 59.5 us -> 0 us
  local copies, waits for them, and re-layouts: 60.7 us -> 2.21 us
  other arithmetic: 43 us -> 0 us
  Pallas kernels: 0 us -> 32.3 us
  starting transfers between devices: 0.24 us -> 27 us
  between operations: 14.9 us -> 0.74 us
    reduce_scatter x4 -> x0, waiting for transfers between devices: 843 us -> none  [the longest x1 642 us: local(): lax.psum_scatter(carry[0], ('prompt', 'comp'), scatter_dimension=0, tiled...]
    unnamed x7 -> x0, waiting for transfers between devices: 108 us -> none
    dot_general x72 -> x0, matrix products: 106 us -> none  [the longest x4 15.1 us: group_step(): jnp.einsum('hrn,hrl->hnl', qn, d_qlat, preferred_element_type=f32)]
    pallas_call x0 -> x11, Pallas kernels: none -> 32.3 us  [the longest x2 19.9 us: attend(): pl.pallas_call(functools.partial(attend_kernel, last), out_shape=out_shap...]
    unnamed x1 -> x0, blocking collectives: 32.1 us -> none
    all_gather x1 -> x0, blocking collectives: 27.4 us -> none  [local(): lax.all_gather(rope_key, 'prompt', axis=0, tiled=True)]
    add x24 -> x0, other arithmetic: 19.3 us -> none  [the longest x4 5.84 us: group_step(): d_clat + (jnp.einsum('hstu,hstl->sul', dss, ql_s, preferred_element_type=...]
    ppermute x0 -> x15, starting transfers between devices: none -> 17.4 us  [the longest x3 3.49 us: local(): lax.ppermute(o[k], 'prompt', [(i, (i + 2 * k) % 8) for i in range(8)])]
  transfers between devices with their start and end apart: 6 -> 17, of which waited for: 6 -> 8; matrix products, arithmetic and copies ran while one was open for 1% -> 1% of each run, Pallas kernels for 0% -> 24%
where the time goes in v2:
time: 81.3 us; the launch traced here: 80.9 us
  Pallas kernels  32.3 us (40%)
  starting transfers between devices  27 us (33%)
  waiting for transfers between devices  18.6 us (23%)
  local copies, waits for them, and re-layouts  2.21 us (3%)
    pallas_call x2, Pallas kernels, attend(): pl.pallas_call(functools.partial(attend_kernel, last), out_shape=out_shap...  19.9 us
    pallas_call x1, Pallas kernels, prep(): pl.pallas_call(prep_kernel, out_shape=(jax.ShapeDtypeStruct((8, ROWS, HW)...  5.75 us
    all_to_all x1, starting transfers between devices, local(): kva = lax.all_to_all(kv, 'prompt', 0, 0, tiled=True).reshape(512, KW)  5.48 us
    all_to_all x1, waiting for transfers between devices, local(): kva = lax.all_to_all(kv, 'prompt', 0, 0, tiled=True).reshape(512, KW)  5.06 us
    all_to_all x1, starting transfers between devices, local(): lax.all_to_all(dlat, ('prompt', 'comp'), 0, 0, tiled=True, axis_index_gro...  4.11 us
    ppermute x3, starting transfers between devices, local(): lax.ppermute(o[k], 'prompt', [(i, (i + 2 * k) % 8) for i in range(8)])  3.49 us
    all_to_all x1, waiting for transfers between devices, local(): lax.all_to_all(dlat, ('prompt', 'comp'), 0, 0, tiled=True, axis_index_gro...  3.33 us
    ppermute x1, starting transfers between devices, local(): b = lax.ppermute(b, 'comp', down)  3.03 us
  transfers between devices with their start and end apart: 17, of which 8 were waited for; matrix products, arithmetic and copies ran while one was open for 1% of the time, Pallas kernels for 24%

profile of v2, /device:TPU:0, one launch (start us, length us, event | category | flops | bytes accessed | tf_op | source)
XLA Modules:
  0.0 80.9 jit_solution(11575580360767449355)
XLA Ops:
  0.6 1.9 %keys.1 = bf16[8,64,640]{2,1,0:T(8,128)(2,1)} custom-call(bf16[128,512]{1,0:T(8,128)(2,1)} %lat.1, bf16[64,128]{1,0:T(8,128)(2,1)} %bitcast.30), custom_call_target="tpu_custom_call" | custom-call | tf_op jit(solution)/shard_map/keys/pallas_call | solution.py:59
  2.5 5.5 %all-to-all-start = ((bf16[8,64,640]{2,1,0:T(8,128)(2,1)}), bf16[8,64,640]{2,1,0:T(8,128)(2,1)S(1)}, u32[]{:S(2)}, u32[]{:S(2)}) async-start(bf16[8,64,640]{2,1,0:T(8,128)(2,1)} %keys.1), calls=%async_computation | async-start | bytes 1310720 | tf_op jit(solution)/shard_map/all_to_all | solution.py:490
  8.0 0.6 stack.55.info
  8.6 0.0 copy-start.4
  8.6 0.0 copy-start.5
  8.6 5.7 %prep.1 = (bf16[8,128,384]{2,1,0:T(8,128)(2,1)}, bf16[8,128,384]{2,1,0:T(8,128)(2,1)}, bf16[8,256,512]{2,1,0:T(8,128)(2,1)}) custom-call(s32[13]{0:T(128)} %stack.55.info, s32[2]{0:T(128)} %lens.1, bf16[128,2048]{1,0:T(8,128)(2,1)} %refs_8_.1, bf16[128,2048]{1,0:T(8,128)(2,1)} %refs_8_.1, bf16[128,2048]{1,0:T(8,128)(2,1)} %refs_10_.1, ...), custom_call_target="tpu_custom_call" | custom-call | flops 1000000000 | bytes 4194304 | tf_op jit(solution)/shard_map/prep/pallas_call | solution.py:132
  14.3 0.1 collective-permute-start.2
  14.4 5.1 %all-to-all-done = bf16[8,64,640]{2,1,0:T(8,128)(2,1)S(1)} async-done(((bf16[8,64,640]{2,1,0:T(8,128)(2,1)}), bf16[8,64,640]{2,1,0:T(8,128)(2,1)S(1)}, u32[]{:S(2)}, u32[]{:S(2)}) %all-to-all-start) | async-done | bytes 655392 | tf_op jit(solution)/shard_map/all_to_all | solution.py:490
  19.5 0.0 collective-permute-start
  19.5 0.0 copy-done.4
  19.5 0.0 copy-done.5
  19.5 0.0 copy-start.1
  19.5 1.6 %copy-done.1 = bf16[8,256,512]{2,1,0:T(8,128)(2,1)S(1)} copy-done((bf16[8,256,512]{2,1,0:T(8,128)(2,1)S(1)}, bf16[8,256,512]{2,1,0:T(8,128)(2,1)}, u32[]{:S(2)}) %copy-start.1) | copy-done | bytes 2097176
  21.1 0.0 copy-start.2
  21.1 0.0 copy-start.3
  21.1 0.1 own_keys.1.refs_2_
  21.2 0.6 collective-permute-start.1
  21.8 1.0 %collective-permute-done.1.refs_3_ = bf16[128,640]{1,0:T(8,128)(2,1)S(1)} collective-permute-done((bf16[128,640]{1,0:T(8,128)(2,1)S(1)}, bf16[128,640]{1,0:T(8,128)(2,1)S(1)}, u32[]{:S(2)}, u32[]{:S(2)}) %collective-permute-start.1) | collective-permute-done | bytes 163872 | tf_op jit(solution)/shard_map/ppermute | solution.py:496
  22.8 0.0 collective-permute-done.2.refs_5_
  22.8 0.0 collective-permute-done.refs_1_
  22.8 0.0 copy-done.2
  22.8 0.0 copy-done.3
  22.8 9.9 %attend.2 = (bf16[2,512,256]{2,1,0:T(8,128)(2,1)S(1)}, bf16[2,512,256]{2,1,0:T(8,128)(2,1)S(1)}, f32[1280,640]{1,0:T(8,128)S(1)}) custom-call(bf16[512,640]{1,0:T(8,128)(2,1)S(1)} %bitcast.24, bf16[512,640]{1,0:T(8,128)(2,1)S(1)} %collective-permute-done.refs_1_, bf16[128,640]{1,0:T(8,128)(2,1)S(1)} %own_keys.1.refs_2_, ...), custom_call_target="tpu_custom_call" | custom-call | flops 10000000000 | bytes 10485760 | tf_op jit(solution)/shard_map/attend/pallas_call | solution.py:318
  32.8 2.0 %collective-permute-start.3 = (bf16[2,512,256]{2,1,0:T(8,128)(2,1)S(1)}, bf16[2,512,256]{2,1,0:T(8,128)(2,1)S(1)}, u32[]{:S(2)}, u32[]{:S(2)}) collective-permute-start(bf16[2,512,256]{2,1,0:T(8,128)(2,1)S(1)} %get-tuple-element.40), channel_id=1, source_target_pairs={{0,4},{1,5},{2,6},{3,7},{4,8},{5,9},{6,10},{7,11},{8,12},{9,13},{1... | collective-permute-start | bytes 1572872 | tf_op jit(solution)/shard_map/ppermute | solution.py:500
  34.7 2.4 %collective-permute-start.4 = (bf16[2,512,256]{2,1,0:T(8,128)(2,1)S(1)}, bf16[2,512,256]{2,1,0:T(8,128)(2,1)S(1)}, u32[]{:S(2)}, u32[]{:S(2)}) collective-permute-start(bf16[2,512,256]{2,1,0:T(8,128)(2,1)S(1)} %get-tuple-element.41), channel_id=1, source_target_pairs={{0,12},{1,13},{2,14},{3,15},{4,0},{5,1},{6,2},{7,3},{8,4},{9,5},{1... | collective-permute-start | bytes 1572872 | tf_op jit(solution)/shard_map/ppermute | solution.py:501
  37.1 0.0 copy-start
  37.1 10.0 %attend.3 = (bf16[4,512,256]{2,1,0:T(8,128)(2,1)S(1)}, bf16[640,640]{1,0:T(8,128)(2,1)S(1)}, bf16[256,640]{1,0:T(8,128)(2,1)S(1)}, bf16[256,640]{1,0:T(8,128)(2,1)S(1)}, bf16[128,640]{1,0:T(8,128)(2,1)S(1)}) custom-call(bf16[512,640]{1,0:T(8,128)(2,1)S(1)} %bitcast.25, bf16[512,640]{1,0:T(8,128)(2,1)S(1)} %collective-permute-done.refs_1_, ...), custom_call_target="tpu_custom_call" | custom-call | flops 10000000000 | bytes 10485760 | tf_op jit(solution)/shard_map/attend/pallas_call | solution.py:318
  47.1 0.3 collective-permute-start.5
  47.4 0.3 collective-permute-start.6
  47.7 0.2 collective-permute-start.7
  47.9 1.6 %collective-permute-done.7.got_c = bf16[128,640]{1,0:T(8,128)(2,1)S(1)} collective-permute-done((bf16[128,640]{1,0:T(8,128)(2,1)S(1)}, bf16[128,640]{1,0:T(8,128)(2,1)S(1)}, u32[]{:S(2)}, u32[]{:S(2)}) %collective-permute-start.7) | collective-permute-done | bytes 163872 | tf_op jit(solution)/shard_map/ppermute | solution.py:503
  49.5 0.0 collective-permute-done.5.got_a
  49.5 0.0 collective-permute-done.6.got_b
  49.5 0.0 copy-done
  49.5 0.9 %join.1 = (bf16[128,768]{1,0:T(8,128)(2,1)S(1)}, bf16[128,768]{1,0:T(8,128)(2,1)S(1)}, bf16[128,768]{1,0:T(8,128)(2,1)S(1)}, bf16[128,768]{1,0:T(8,128)(2,1)S(1)}) custom-call(s32[13]{0:T(128)S(1)} %copy-done, bf16[640,640]{1,0:T(8,128)(2,1)S(1)} %get-tuple-element.42.stay, bf16[256,640]{1,0:T(8,128)(2,1)S(1)} %collective-permute-done.5.got_a, ...), custom_call_target="tpu_custom_call" | custom-call | tf_op jit(solution)/shard_map/join/pallas_call | solution.py:354
  50.5 0.0 collective-permute-done.3.p
  50.5 0.0 collective-permute-done.4.m
  50.5 0.1 ring.1
  50.6 0.3 collective-permute-start.8
  50.9 3.0 %collective-permute-start.9 = (bf16[512,256]{1,0:T(8,128)(2,1)S(1)}, bf16[512,256]{1,0:T(8,128)(2,1)S(1)}, u32[]{:S(2)}, u32[]{:S(2)}) collective-permute-start(bf16[512,256]{1,0:T(8,128)(2,1)S(1)} %get-tuple-element.48), channel_id=1, source_target_pairs={{0,12},{1,13},{2,14},{3,15},{4,0},{5,1},{6,2},{7,3},{8,4},{9,5},{1... | collective-permute-start | bytes 786440 | tf_op jit(solution)/shard_map/ppermute | solution.py:510
  53.9 0.0 collective-permute-start.11
  53.9 2.3 %collective-permute-start.12 = (bf16[128,768]{1,0:T(8,128)(2,1)S(1)}, bf16[128,768]{1,0:T(8,128)(2,1)S(1)}, u32[]{:S(2)}, u32[]{:S(2)}) collective-permute-start(bf16[128,768]{1,0:T(8,128)(2,1)S(1)} %get-tuple-element.54), channel_id=1, source_target_pairs={{0,64},{16,80},{32,96},{48,112},{64,0},{80,16},{96,32},{112,48},{1... | collective-permute-start | bytes 589832 | tf_op jit(solution)/shard_map/ppermute | solution.py:506
  56.3 1.2 %collective-permute-start.13 = (bf16[128,768]{1,0:T(8,128)(2,1)S(1)}, bf16[128,768]{1,0:T(8,128)(2,1)S(1)}, u32[]{:S(2)}, u32[]{:S(2)}) collective-permute-start(bf16[128,768]{1,0:T(8,128)(2,1)S(1)} %get-tuple-element.55), channel_id=1, source_target_pairs={{0,96},{16,112},{32,0},{48,16},{64,32},{80,48},{96,64},{112,80},{1... | collective-permute-start | bytes 589832 | tf_op jit(solution)/shard_map/ppermute | solution.py:506
  57.4 2.9 %collective-permute-done.8.a = bf16[512,256]{1,0:T(8,128)(2,1)S(1)} collective-permute-done((bf16[512,256]{1,0:T(8,128)(2,1)S(1)}, bf16[512,256]{1,0:T(8,128)(2,1)S(1)}, u32[]{:S(2)}, u32[]{:S(2)}) %collective-permute-start.8) | collective-permute-done | bytes 262176 | tf_op jit(solution)/shard_map/ppermute | solution.py:509
  60.3 0.0 collective-permute-done.9.b
  60.3 0.8 pair.1
  61.1 2.8 %collective-permute-start.10 = (bf16[512,256]{1,0:T(8,128)(2,1)S(1)}, bf16[512,256]{1,0:T(8,128)(2,1)S(1)}, u32[]{:S(2)}, u32[]{:S(2)}) collective-permute-start(bf16[512,256]{1,0:T(8,128)(2,1)S(1)} %get-tuple-element.50), channel_id=1, source_target_pairs={{0,2},{1,3},{2,0},{3,1},{4,6},{5,7},{6,4},{7,5},{8,10},{9,11},{10,... | collective-permute-start | bytes 786440 | tf_op jit(solution)/shard_map/ppermute | solution.py:522
  63.9 1.9 %collective-permute-done.11.a1 = bf16[128,768]{1,0:T(8,128)(2,1)S(1)} collective-permute-done((bf16[128,768]{1,0:T(8,128)(2,1)S(1)}, bf16[128,768]{1,0:T(8,128)(2,1)S(1)}, u32[]{:S(2)}, u32[]{:S(2)}) %collective-permute-start.11) | collective-permute-done | bytes 196640 | tf_op jit(solution)/shard_map/ppermute | solution.py:506
  65.8 0.0 collective-permute-done.12.a2
  65.8 0.6 collective-permute-done.13.a3
  66.5 1.3 %sum_y.1 = (bf16[128,640]{1,0:T(8,128)(2,1)}, bf16[128,128]{1,0:T(8,128)(2,1)S(1)}, bf16[128,128]{1,0:T(8,128)(2,1)S(1)}) custom-call(s32[13]{0:T(128)S(1)} %copy-done, bf16[128,768]{1,0:T(8,128)(2,1)S(1)} %get-tuple-element.46.after.a0, bf16[128,768]{1,0:T(8,128)(2,1)S(1)} %collective-permute-done.11.a1, bf16[128,768]{1,0:T(8,128)(2,1)S(1)} %collective-permute-done.12.a2, ...), custom_call_target="tpu_custom_call" | custom-call | tf_op jit(solution)/shard_map/sum_y/pallas_call | solution.py:378
  67.8 4.1 %all-to-all-start.1 = ((bf16[16,8,640]{2,1,0:T(8,128)(2,1)}), bf16[16,8,640]{2,1,0:T(8,128)(2,1)S(1)}, u32[]{:S(2)}, u32[]{:S(2)}) async-start(bf16[16,8,640]{2,1,0:T(8,128)(2,1)} %bitcast.19), calls=%async_computation.1 | async-start | bytes 327680 | tf_op jit(solution)/shard_map/all_to_all | solution.py:518
  71.9 1.9 %collective-permute-start.14 = (bf16[128,128]{1,0:T(8,128)(2,1)S(1)}, bf16[128,128]{1,0:T(8,128)(2,1)S(1)}, u32[]{:S(2)}, u32[]{:S(2)}) collective-permute-start(bf16[128,128]{1,0:T(8,128)(2,1)S(1)} %get-tuple-element.57), channel_id=1, source_target_pairs={{0,16},{16,0},{32,48},{48,32},{64,80},{80,64},{96,112},{112,96},{1... | collective-permute-start | bytes 98312 | tf_op jit(solution)/shard_map/ppermute | solution.py:517
  73.8 0.0 collective-permute-done.10.got
  73.8 0.8 %weights.1 = (f32[128,512]{1,0:T(8,128)}, f32[512,128]{1,0:T(8,128)}, f32[8,128]{1,0:T(8,128)S(1)}) custom-call(bf16[512,256]{1,0:T(8,128)(2,1)S(1)} %get-tuple-element.49.mine, bf16[512,256]{1,0:T(8,128)(2,1)S(1)} %collective-permute-done.10.got), custom_call_target="tpu_custom_call" | custom-call | tf_op jit(solution)/shard_map/weights/pallas_call | solution.py:462
  74.7 2.1 %collective-permute-done.14.got = bf16[128,128]{1,0:T(8,128)(2,1)S(1)} collective-permute-done((bf16[128,128]{1,0:T(8,128)(2,1)S(1)}, bf16[128,128]{1,0:T(8,128)(2,1)S(1)}, u32[]{:S(2)}, u32[]{:S(2)}) %collective-permute-start.14) | collective-permute-done | bytes 32800 | tf_op jit(solution)/shard_map/ppermute | solution.py:517
  76.8 3.3 %all-to-all-done.1 = bf16[16,8,640]{2,1,0:T(8,128)(2,1)S(1)} async-done(((bf16[16,8,640]{2,1,0:T(8,128)(2,1)}), bf16[16,8,640]{2,1,0:T(8,128)(2,1)S(1)}, u32[]{:S(2)}, u32[]{:S(2)}) %all-to-all-start.1) | async-done | bytes 163872 | tf_op jit(solution)/shard_map/all_to_all | solution.py:518
  80.2 0.7 final.1
Async XLA Ops:
  2.5 17.0 %all-to-all-start = ((bf16[8,64,640]{2,1,0:T(8,128)(2,1)}), bf16[8,64,640]{2,1,0:T(8,128)(2,1)S(1)}, u32[]{:S(2)}, u32[]{:S(2)}) async-start(bf16[8,64,640]{2,1,0:T(8,128)(2,1)} %keys.1), calls=%async_computation | async-start | bytes 1310720 | tf_op jit(solution)/shard_map/all_to_all | solution.py:490
  8.6 10.9 %copy-start.4 = (bf16[128,512]{1,0:T(8,128)(2,1)S(1)}, bf16[128,512]{1,0:T(8,128)(2,1)}, u32[]{:S(2)}) copy-start(bf16[128,512]{1,0:T(8,128)(2,1)} %clat.1) | copy-start | bytes 393220
  8.6 10.9 %copy-start.5 = (bf16[128,64]{0,1:T(8,128)(2,1)S(1)}, bf16[128,64]{0,1:T(8,128)(2,1)}, u32[]{:S(2)}) copy-start(bf16[128,64]{0,1:T(8,128)(2,1)} %param.18) | copy-start | bytes 49156
  14.3 8.5 %collective-permute-start.2 = (bf16[8,128,384]{2,1,0:T(8,128)(2,1)}, bf16[8,128,384]{2,1,0:T(8,128)(2,1)S(1)}, u32[]{:S(2)}, u32[]{:S(2)}) collective-permute-start(bf16[8,128,384]{2,1,0:T(8,128)(2,1)} %get-tuple-element.37), channel_id=1, source_target_pairs={{0,1},{1,0},{2,3},{3,2},{4,5},{5,4},{6,7},{7,6},{8,9},{9,8},{10,11... | collective-permute-start | bytes 2359304 | tf_op jit(solution)/shard_map/ppermute | solution.py:494
  19.5 3.3 %collective-permute-start = (bf16[512,640]{1,0:T(8,128)(2,1)S(1)}, bf16[512,640]{1,0:T(8,128)(2,1)S(1)}, u32[]{:S(2)}, u32[]{:S(2)}) collective-permute-start(bf16[512,640]{1,0:T(8,128)(2,1)S(1)} %bitcast.23), channel_id=1, source_target_pairs={{0,1},{1,0},{2,3},{3,2},{4,5},{5,4},{6,7},{7,6},{8,9},{9,8},{10,11... | collective-permute-start | bytes 1966088 | tf_op jit(solution)/shard_map/ppermute | solution.py:497
  19.5 1.6 %copy-start.1 = (bf16[8,256,512]{2,1,0:T(8,128)(2,1)S(1)}, bf16[8,256,512]{2,1,0:T(8,128)(2,1)}, u32[]{:S(2)}) copy-start(bf16[8,256,512]{2,1,0:T(8,128)(2,1)} %get-tuple-element.35.after) | copy-start | bytes 6291460
  21.1 1.7 %copy-start.2 = (bf16[8,256,512]{2,1,0:T(8,128)(2,1)S(1)}, bf16[8,256,512]{2,1,0:T(8,128)(2,1)}, u32[]{:S(2)}) copy-start(bf16[8,256,512]{2,1,0:T(8,128)(2,1)} %get-tuple-element.35.after) | copy-start | bytes 6291460
  21.1 1.8 %copy-start.3 = (bf16[8,128,384]{2,1,0:T(8,128)(2,1)S(1)}, bf16[8,128,384]{2,1,0:T(8,128)(2,1)}, u32[]{:S(2)}) copy-start(bf16[8,128,384]{2,1,0:T(8,128)(2,1)} %get-tuple-element.36.refs_4_) | copy-start | bytes 2359300
  21.2 1.6 %collective-permute-start.1 = (bf16[128,640]{1,0:T(8,128)(2,1)S(1)}, bf16[128,640]{1,0:T(8,128)(2,1)S(1)}, u32[]{:S(2)}, u32[]{:S(2)}) collective-permute-start(bf16[128,640]{1,0:T(8,128)(2,1)S(1)} %own_keys.1.refs_2_), channel_id=1, source_target_pairs={{0,1},{1,0},{2,3},{3,2},{4,5},{5,4},{6,7},{7,6},{8,9},{9,8},{10,11... | collective-permute-start | bytes 491528 | tf_op jit(solution)/shard_map/ppermute | solution.py:496
  32.8 17.7 %collective-permute-start.3 = (bf16[2,512,256]{2,1,0:T(8,128)(2,1)S(1)}, bf16[2,512,256]{2,1,0:T(8,128)(2,1)S(1)}, u32[]{:S(2)}, u32[]{:S(2)}) collective-permute-start(bf16[2,512,256]{2,1,0:T(8,128)(2,1)S(1)} %get-tuple-element.40), channel_id=1, source_target_pairs={{0,4},{1,5},{2,6},{3,7},{4,8},{5,9},{6,10},{7,11},{8,12},{9,13},{1... | collective-permute-start | bytes 1572872 | tf_op jit(solution)/shard_map/ppermute | solution.py:500
  34.7 15.7 %collective-permute-start.4 = (bf16[2,512,256]{2,1,0:T(8,128)(2,1)S(1)}, bf16[2,512,256]{2,1,0:T(8,128)(2,1)S(1)}, u32[]{:S(2)}, u32[]{:S(2)}) collective-permute-start(bf16[2,512,256]{2,1,0:T(8,128)(2,1)S(1)} %get-tuple-element.41), channel_id=1, source_target_pairs={{0,12},{1,13},{2,14},{3,15},{4,0},{5,1},{6,2},{7,3},{8,4},{9,5},{1... | collective-permute-start | bytes 1572872 | tf_op jit(solution)/shard_map/ppermute | solution.py:501
  37.1 12.4 %copy-start = (s32[13]{0:T(128)S(1)}, s32[13]{0:T(128)}, u32[]{:S(2)}) copy-start(s32[13]{0:T(128)} %stack.55.info) | copy-start | bytes 160
  47.1 2.4 %collective-permute-start.5 = (bf16[256,640]{1,0:T(8,128)(2,1)S(1)}, bf16[256,640]{1,0:T(8,128)(2,1)S(1)}, u32[]{:S(2)}, u32[]{:S(2)}) collective-permute-start(bf16[256,640]{1,0:T(8,128)(2,1)S(1)} %get-tuple-element.43), channel_id=1, source_target_pairs={{0,1},{1,0},{2,3},{3,2},{4,5},{5,4},{6,7},{7,6},{8,9},{9,8},{10,11... | collective-permute-start | bytes 983048 | tf_op jit(solution)/shard_map/ppermute | solution.py:503
  47.4 2.1 %collective-permute-start.6 = (bf16[256,640]{1,0:T(8,128)(2,1)S(1)}, bf16[256,640]{1,0:T(8,128)(2,1)S(1)}, u32[]{:S(2)}, u32[]{:S(2)}) collective-permute-start(bf16[256,640]{1,0:T(8,128)(2,1)S(1)} %get-tuple-element.44), channel_id=1, source_target_pairs={{0,1},{1,0},{2,3},{3,2},{4,5},{5,4},{6,7},{7,6},{8,9},{9,8},{10,11... | collective-permute-start | bytes 983048 | tf_op jit(solution)/shard_map/ppermute | solution.py:503
  47.7 1.8 %collective-permute-start.7 = (bf16[128,640]{1,0:T(8,128)(2,1)S(1)}, bf16[128,640]{1,0:T(8,128)(2,1)S(1)}, u32[]{:S(2)}, u32[]{:S(2)}) collective-permute-start(bf16[128,640]{1,0:T(8,128)(2,1)S(1)} %get-tuple-element.45), channel_id=1, source_target_pairs={{0,1},{1,0},{2,3},{3,2},{4,5},{5,4},{6,7},{7,6},{8,9},{9,8},{10,11... | collective-permute-start | bytes 491528 | tf_op jit(solution)/shard_map/ppermute | solution.py:503
  50.6 9.7 %collective-permute-start.8 = (bf16[512,256]{1,0:T(8,128)(2,1)S(1)}, bf16[512,256]{1,0:T(8,128)(2,1)S(1)}, u32[]{:S(2)}, u32[]{:S(2)}) collective-permute-start(bf16[512,256]{1,0:T(8,128)(2,1)S(1)} %get-tuple-element.47), channel_id=1, source_target_pairs={{0,4},{1,5},{2,6},{3,7},{4,8},{5,9},{6,10},{7,11},{8,12},{9,13},{1... | collective-permute-start | bytes 786440 | tf_op jit(solution)/shard_map/ppermute | solution.py:509
  50.9 9.4 %collective-permute-start.9 = (bf16[512,256]{1,0:T(8,128)(2,1)S(1)}, bf16[512,256]{1,0:T(8,128)(2,1)S(1)}, u32[]{:S(2)}, u32[]{:S(2)}) collective-permute-start(bf16[512,256]{1,0:T(8,128)(2,1)S(1)} %get-tuple-element.48), channel_id=1, source_target_pairs={{0,12},{1,13},{2,14},{3,15},{4,0},{5,1},{6,2},{7,3},{8,4},{9,5},{1... | collective-permute-start | bytes 786440 | tf_op jit(solution)/shard_map/ppermute | solution.py:510
  53.9 11.9 %collective-permute-start.11 = (bf16[128,768]{1,0:T(8,128)(2,1)S(1)}, bf16[128,768]{1,0:T(8,128)(2,1)S(1)}, u32[]{:S(2)}, u32[]{:S(2)}) collective-permute-start(bf16[128,768]{1,0:T(8,128)(2,1)S(1)} %get-tuple-element.53), channel_id=1, source_target_pairs={{0,32},{16,48},{32,64},{48,80},{64,96},{80,112},{96,0},{112,16},{1... | collective-permute-start | bytes 589832 | tf_op jit(solution)/shard_map/ppermute | solution.py:506
  53.9 11.9 %collective-permute-start.12 = (bf16[128,768]{1,0:T(8,128)(2,1)S(1)}, bf16[128,768]{1,0:T(8,128)(2,1)S(1)}, u32[]{:S(2)}, u32[]{:S(2)}) collective-permute-start(bf16[128,768]{1,0:T(8,128)(2,1)S(1)} %get-tuple-element.54), channel_id=1, source_target_pairs={{0,64},{16,80},{32,96},{48,112},{64,0},{80,16},{96,32},{112,48},{1... | collective-permute-start | bytes 589832 | tf_op jit(solution)/shard_map/ppermute | solution.py:506
  56.3 10.2 %collective-permute-start.13 = (bf16[128,768]{1,0:T(8,128)(2,1)S(1)}, bf16[128,768]{1,0:T(8,128)(2,1)S(1)}, u32[]{:S(2)}, u32[]{:S(2)}) collective-permute-start(bf16[128,768]{1,0:T(8,128)(2,1)S(1)} %get-tuple-element.55), channel_id=1, source_target_pairs={{0,96},{16,112},{32,0},{48,16},{64,32},{80,48},{96,64},{112,80},{1... | collective-permute-start | bytes 589832 | tf_op jit(solution)/shard_map/ppermute | solution.py:506
  61.1 12.7 %collective-permute-start.10 = (bf16[512,256]{1,0:T(8,128)(2,1)S(1)}, bf16[512,256]{1,0:T(8,128)(2,1)S(1)}, u32[]{:S(2)}, u32[]{:S(2)}) collective-permute-start(bf16[512,256]{1,0:T(8,128)(2,1)S(1)} %get-tuple-element.50), channel_id=1, source_target_pairs={{0,2},{1,3},{2,0},{3,1},{4,6},{5,7},{6,4},{7,5},{8,10},{9,11},{10,... | collective-permute-start | bytes 786440 | tf_op jit(solution)/shard_map/ppermute | solution.py:522
  67.8 12.4 %all-to-all-start.1 = ((bf16[16,8,640]{2,1,0:T(8,128)(2,1)}), bf16[16,8,640]{2,1,0:T(8,128)(2,1)S(1)}, u32[]{:S(2)}, u32[]{:S(2)}) async-start(bf16[16,8,640]{2,1,0:T(8,128)(2,1)} %bitcast.19), calls=%async_computation.1 | async-start | bytes 327680 | tf_op jit(solution)/shard_map/all_to_all | solution.py:518
  71.9 4.9 %collective-permute-start.14 = (bf16[128,128]{1,0:T(8,128)(2,1)S(1)}, bf16[128,128]{1,0:T(8,128)(2,1)S(1)}, u32[]{:S(2)}, u32[]{:S(2)}) collective-permute-start(bf16[128,128]{1,0:T(8,128)(2,1)S(1)} %get-tuple-element.57), channel_id=1, source_target_pairs={{0,16},{16,0},{32,48},{48,32},{64,80},{80,64},{96,112},{112,96},{1... | collective-permute-start | bytes 98312 | tf_op jit(solution)/shard_map/ppermute | solution.py:517

commit v3 on v2

--- a/solution.py
+++ b/solution.py
@@ -72,7 +72,8 @@
     limit = jnp.where(row < SLEN, lens[0], lens[1])
     valid = (row % SLEN) < limit
     lane = lax.broadcasted_iota(jnp.int32, (ROWS, 2 * ROPE), 1)
-    keep, send, ww = refs[-3:]
+    keep, send, ww, done = refs[-4:]
+    done[...] = jnp.zeros_like(done)
     for h in range(2):
         qn_k, qn_s, do_k, do_s, qr, wk, wv = refs[7 * h : 7 * h + 7]
         tile = qr[...].astype(f32)
@@ -135,6 +136,7 @@
             jax.ShapeDtypeStruct((8, ROWS, HW), bf16),
             jax.ShapeDtypeStruct((8, ROWS, HW), bf16),
             jax.ShapeDtypeStruct((8, 2 * NOPE, LAT), bf16),
+            jax.ShapeDtypeStruct((8, 128), f32),
         ),
         grid_spec=pltpu.PrefetchScalarGridSpec(
             num_scalar_prefetch=2,
@@ -144,6 +146,7 @@
                 out,
                 out,
                 pl.BlockSpec((2, 2 * NOPE, LAT), lambda i, info, lens: (i, 0, 0)),
+                pl.BlockSpec((8, 128), lambda i, info, lens: (0, 0)),
             ),
         ),
         compiler_params=params(),
@@ -331,8 +334,8 @@
 YW = 768
 
 
-def join_kernel(info, stay, got_a, got_b, got_c, o0, o1, o2, o3):
-    y = info[1]
+def join_kernel(stay, got_a, got_b, got_c, o0, o1, o2, o3):
+    y = lax.axis_index("prompt") // 2
     crope = stay[512:640, LAT:KW].astype(f32) + got_c[:, LAT:KW].astype(f32)
     for k, out in enumerate((o0, o1, o2, o3)):
         to = lax.rem(y + k, 4)
@@ -350,19 +353,19 @@
         out[:, KW:YW] = c.astype(bf16)
 
 
-def join(info, stay, *got):
+def join(stay, *got):
     return pl.pallas_call(
         join_kernel,
         out_shape=(jax.ShapeDtypeStruct((128, YW), bf16),) * 4,
-        in_specs=[SM] + [VM] * 4,
+        in_specs=[VM] * 4,
         out_specs=(VM,) * 4,
         compiler_params=params(24),
         name="join",
-    )(info, stay, *got)
-
-
-def sum_y_kernel(info, a0, a1, a2, a3, out, mine, send):
-    xl = info[2]
+    )(stay, *got)
+
+
+def sum_y_kernel(a0, a1, a2, a3, out, mine, send):
+    xl = lax.axis_index("prompt") % 2
     x = a0[...].astype(f32) + a1[...].astype(f32) + a2[...].astype(f32) + a3[...].astype(f32)
     out[...] = x[:, 0:KW].astype(bf16)
     lane = lax.broadcasted_iota(jnp.int32, (ROWS, 128), 1)
@@ -374,7 +377,7 @@
         ref[...] = jnp.where(lane < 64, c, r).astype(bf16)
 
 
-def sum_y(info, *parts):
+def sum_y(*parts):
     return pl.pallas_call(
         sum_y_kernel,
         out_shape=(
@@ -382,11 +385,11 @@
             jax.ShapeDtypeStruct((ROWS, 128), bf16),
             jax.ShapeDtypeStruct((ROWS, 128), bf16),
         ),
-        in_specs=[SM] + [VM] * 4,
+        in_specs=[VM] * 4,
         out_specs=(VM,) * 3,
         compiler_params=params(24),
         name="sum_y",
-    )(info, *parts)
+    )(*parts)
 
 
 def final_kernel(mine, got, dlat, after, ol, orp, ocl, ocr):
@@ -431,24 +434,24 @@
     )(rest, p, m, after)
 
 
-def pair_kernel(info, rest, p, m, a, b, mine, send):
+def pair_kernel(rest, p, m, a, b, mine, send):
     first = rest[2].astype(f32) + m[1].astype(f32) + a[...].astype(f32)
     second = rest[3].astype(f32) + p[1].astype(f32) + b[...].astype(f32)
-    own = info[3] == 0
+    own = (lax.axis_index("comp") // 2) % 2 == 0
     mine[...] = jnp.where(own, first, second).astype(bf16)
     send[...] = jnp.where(own, second, first).astype(bf16)
 
 
-def pair(info, rest, p, m, a, b):
+def pair(rest, p, m, a, b):
     block = jax.ShapeDtypeStruct((LAT, 2 * NOPE), bf16)
     return pl.pallas_call(
         pair_kernel,
         out_shape=(block, block),
-        in_specs=[SM] + [VM] * 5,
+        in_specs=[VM] * 5,
         out_specs=(VM, VM),
         compiler_params=params(24),
         name="pair",
-    )(info, rest, p, m, a, b)
+    )(rest, p, m, a, b)
 
 
 def weights_kernel(mine, got, dwk, dwv, done):
@@ -488,11 +491,11 @@
     down = [(c, (c + 12) % 16) for c in range(16)]
     kv = keys(latent, rope_key.T)
     kva = lax.all_to_all(kv, "prompt", 0, 0, tiled=True).reshape(512, KW)
-    keep, send, ww = prep(
+    keep, send, ww, done = prep(
         info, lengths, q_nope, q_rope, d_out, w_uk, w_uv
     )
     recv = lax.ppermute(send, "comp", swap)
-    ckeep = own_keys(comp_latent, comp_rope.T, ww)
+    ckeep = own_keys(comp_latent, comp_rope.T, done)
     crecv = lax.ppermute(ckeep, "comp", swap)
     kvb = lax.ppermute(kva, "comp", swap)
     ops = (kva, kvb, ckeep, crecv, keep, recv, ww.reshape(8 * W, LAT))
@@ -501,14 +504,14 @@
     minus = lax.ppermute(minus, "comp", down)
     rest, stay, *give = attend(True, *ops, acc)
     got = [lax.ppermute(x, "comp", swap) for x in give]
-    o = join(info, stay, *got)
+    o = join(stay, *got)
     o = [o[0]] + [
         lax.ppermute(o[k], "prompt", [(i, (i + 2 * k) % 8) for i in range(8)]) for k in (1, 2, 3)
     ]
     a, b = ring(rest, plus, minus, o[0])
     a = lax.ppermute(a, "comp", up)
     b = lax.ppermute(b, "comp", down)
-    dlat, cmine, csend = sum_y(info, *o)
+    dlat, cmine, csend = sum_y(*o)
     planes = [
         [(2 * y + xl) * 16 + 2 * i + core for xl in range(2) for i in range(8)]
         for y in range(4)
@@ -518,7 +521,7 @@
     dlat = lax.all_to_all(
         dlat, ("prompt", "comp"), 0, 0, tiled=True, axis_index_groups=planes
     )
-    mine, send = pair(info, rest, plus, minus, a, b)
+    mine, send = pair(rest, plus, minus, a, b)
     other = lax.ppermute(send, "comp", [(c, c ^ 2) for c in range(16)])
     dwk, dwv, done = weights(mine, other)
     ol, orp, ocl, ocr = final(cmine, cgot, dlat, done)

time: 81.3 us -> 79.7 us (0.980)
  Pallas kernels: 32.3 us -> 30.6 us
    unnamed x12 -> x10, local copies, waits for them, and re-layouts: 1.63 us -> 0.73 us
  transfers between devices with their start and end apart: 17 -> 17, of which waited for: 8 -> 8; matrix products, arithmetic and copies ran while one was open for 1% -> 1% of each run, Pallas kernels for 24% -> 23%
where the time goes in v3:
time: 79.7 us; the launch traced here: 79.3 us
  Pallas kernels  30.6 us (38%)
  starting transfers between devices  27.5 us (35%)
  waiting for transfers between devices  19 us (24%)
  local copies, waits for them, and re-layouts  1.41 us (2%)
    pallas_call x2, Pallas kernels, attend(): pl.pallas_call(functools.partial(attend_kernel, last), out_shape=out_shap...  19.8 us
    pallas_call x1, Pallas kernels, prep(): pl.pallas_call(prep_kernel, out_shape=(jax.ShapeDtypeStruct((8, ROWS, HW)...  5.75 us
    all_to_all x1, starting transfers between devices, local(): kva = lax.all_to_all(kv, 'prompt', 0, 0, tiled=True).reshape(512, KW)  5.48 us
    all_to_all x1, waiting for transfers between devices, local(): kva = lax.all_to_all(kv, 'prompt', 0, 0, tiled=True).reshape(512, KW)  4.95 us
    all_to_all x1, starting transfers between devices, local(): lax.all_to_all(dlat, ('prompt', 'comp'), 0, 0, tiled=True, axis_index_gro...  4.6 us
    ppermute x3, starting transfers between devices, local(): lax.ppermute(o[k], 'prompt', [(i, (i + 2 * k) % 8) for i in range(8)])  3.49 us
    all_to_all x1, waiting for transfers between devices, local(): lax.all_to_all(dlat, ('prompt', 'comp'), 0, 0, tiled=True, axis_index_gro...  3.33 us
    ppermute x3, waiting for transfers between devices, local(): lax.ppermute(o[k], 'prompt', [(i, (i + 2 * k) % 8) for i in range(8)])  3.06 us
  transfers between devices with their start and end apart: 17, of which 8 were waited for; matrix products, arithmetic and copies ran while one was open for 1% of the time, Pallas kernels for 23%

profile of v3, /device:TPU:0, one launch (start us, length us, event | category | flops | bytes accessed | tf_op | source)
XLA Modules:
  0.0 79.3 jit_solution(7181372626273564013)
XLA Ops:
  0.6 1.9 %keys.1 = bf16[8,64,640]{2,1,0:T(8,128)(2,1)} custom-call(bf16[128,512]{1,0:T(8,128)(2,1)} %lat.1, bf16[64,128]{1,0:T(8,128)(2,1)} %bitcast.30), custom_call_target="tpu_custom_call" | custom-call | tf_op jit(solution)/shard_map/keys/pallas_call | solution.py:59
  2.5 5.5 %all-to-all-start = ((bf16[8,64,640]{2,1,0:T(8,128)(2,1)}), bf16[8,64,640]{2,1,0:T(8,128)(2,1)S(1)}, u32[]{:S(2)}, u32[]{:S(2)}) async-start(bf16[8,64,640]{2,1,0:T(8,128)(2,1)} %keys.1), calls=%async_computation | async-start | bytes 1310720 | tf_op jit(solution)/shard_map/all_to_all | solution.py:493
  8.0 0.7 stack.55.info
  8.7 0.0 copy-start.2
  8.7 0.0 copy-start.3
  8.7 5.8 %prep.1 = (bf16[8,128,384]{2,1,0:T(8,128)(2,1)}, bf16[8,128,384]{2,1,0:T(8,128)(2,1)}, bf16[8,256,512]{2,1,0:T(8,128)(2,1)}, f32[8,128]{1,0:T(8,128)}) custom-call(s32[13]{0:T(128)} %stack.55.info, s32[2]{0:T(128)} %lens.1, bf16[128,2048]{1,0:T(8,128)(2,1)} %refs_8_.1, bf16[128,2048]{1,0:T(8,128)(2,1)} %refs_8_.1, bf16[128,2048]{1,0:T(8,128)(2,1)} %refs_10_.1, ...), custom_call_target="tpu_custom_call" | custom-call | flops 1000000000 | bytes 4194304 | tf_op jit(solution)/shard_map/prep/pallas_call | solution.py:133
  14.4 0.1 collective-permute-start.2
  14.5 4.9 %all-to-all-done = bf16[8,64,640]{2,1,0:T(8,128)(2,1)S(1)} async-done(((bf16[8,64,640]{2,1,0:T(8,128)(2,1)}), bf16[8,64,640]{2,1,0:T(8,128)(2,1)S(1)}, u32[]{:S(2)}, u32[]{:S(2)}) %all-to-all-start) | async-done | bytes 655392 | tf_op jit(solution)/shard_map/all_to_all | solution.py:493
  19.5 0.0 collective-permute-start
  19.5 0.0 copy-done.2
  19.5 0.0 copy-done.3
  19.5 0.0 copy-start.4
  19.5 0.7 copy-done.4
  20.2 0.0 copy-start
  20.2 0.0 copy-start.1
  20.2 0.1 own_keys.1.refs_2_
  20.3 0.6 collective-permute-start.1
  20.9 1.0 %collective-permute-done.1.refs_3_ = bf16[128,640]{1,0:T(8,128)(2,1)S(1)} collective-permute-done((bf16[128,640]{1,0:T(8,128)(2,1)S(1)}, bf16[128,640]{1,0:T(8,128)(2,1)S(1)}, u32[]{:S(2)}, u32[]{:S(2)}) %collective-permute-start.1) | collective-permute-done | bytes 163872 | tf_op jit(solution)/shard_map/ppermute | solution.py:499
  21.9 0.0 collective-permute-done.2.refs_5_
  21.9 0.0 collective-permute-done.refs_1_
  21.9 0.0 copy-done
  21.9 0.0 copy-done.1
  21.9 9.9 %attend.2 = (bf16[2,512,256]{2,1,0:T(8,128)(2,1)S(1)}, bf16[2,512,256]{2,1,0:T(8,128)(2,1)S(1)}, f32[1280,640]{1,0:T(8,128)S(1)}) custom-call(bf16[512,640]{1,0:T(8,128)(2,1)S(1)} %bitcast.24, bf16[512,640]{1,0:T(8,128)(2,1)S(1)} %collective-permute-done.refs_1_, bf16[128,640]{1,0:T(8,128)(2,1)S(1)} %own_keys.1.refs_2_, ...), custom_call_target="tpu_custom_call" | custom-call | flops 10000000000 | bytes 10485760 | tf_op jit(solution)/shard_map/attend/pallas_call | solution.py:321
  31.8 2.0 %collective-permute-start.3 = (bf16[2,512,256]{2,1,0:T(8,128)(2,1)S(1)}, bf16[2,512,256]{2,1,0:T(8,128)(2,1)S(1)}, u32[]{:S(2)}, u32[]{:S(2)}) collective-permute-start(bf16[2,512,256]{2,1,0:T(8,128)(2,1)S(1)} %get-tuple-element.42), channel_id=1, source_target_pairs={{0,4},{1,5},{2,6},{3,7},{4,8},{5,9},{6,10},{7,11},{8,12},{9,13},{1... | collective-permute-start | bytes 1572872 | tf_op jit(solution)/shard_map/ppermute | solution.py:503
  33.8 2.4 %collective-permute-start.4 = (bf16[2,512,256]{2,1,0:T(8,128)(2,1)S(1)}, bf16[2,512,256]{2,1,0:T(8,128)(2,1)S(1)}, u32[]{:S(2)}, u32[]{:S(2)}) collective-permute-start(bf16[2,512,256]{2,1,0:T(8,128)(2,1)S(1)} %get-tuple-element.43), channel_id=1, source_target_pairs={{0,12},{1,13},{2,14},{3,15},{4,0},{5,1},{6,2},{7,3},{8,4},{9,5},{1... | collective-permute-start | bytes 1572872 | tf_op jit(solution)/shard_map/ppermute | solution.py:504
  36.2 9.9 %attend.3 = (bf16[4,512,256]{2,1,0:T(8,128)(2,1)S(1)}, bf16[640,640]{1,0:T(8,128)(2,1)S(1)}, bf16[256,640]{1,0:T(8,128)(2,1)S(1)}, bf16[256,640]{1,0:T(8,128)(2,1)S(1)}, bf16[128,640]{1,0:T(8,128)(2,1)S(1)}) custom-call(bf16[512,640]{1,0:T(8,128)(2,1)S(1)} %bitcast.25, bf16[512,640]{1,0:T(8,128)(2,1)S(1)} %collective-permute-done.refs_1_, ...), custom_call_target="tpu_custom_call" | custom-call | flops 10000000000 | bytes 10485760 | tf_op jit(solution)/shard_map/attend/pallas_call | solution.py:321
  46.1 0.3 collective-permute-start.5
  46.4 0.3 collective-permute-start.6
  46.7 0.2 collective-permute-start.7
  46.9 1.6 %collective-permute-done.7.got_c = bf16[128,640]{1,0:T(8,128)(2,1)S(1)} collective-permute-done((bf16[128,640]{1,0:T(8,128)(2,1)S(1)}, bf16[128,640]{1,0:T(8,128)(2,1)S(1)}, u32[]{:S(2)}, u32[]{:S(2)}) %collective-permute-start.7) | collective-permute-done | bytes 163872 | tf_op jit(solution)/shard_map/ppermute | solution.py:506
  48.5 0.0 collective-permute-done.5.got_a
  48.5 0.0 collective-permute-done.6.got_b
  48.5 0.4 join.1
  48.9 0.0 collective-permute-done.3.p
  48.9 0.0 collective-permute-done.4.m
  49.0 0.1 ring.1
  49.1 0.9 %collective-permute-start.8 = (bf16[512,256]{1,0:T(8,128)(2,1)S(1)}, bf16[512,256]{1,0:T(8,128)(2,1)S(1)}, u32[]{:S(2)}, u32[]{:S(2)}) collective-permute-start(bf16[512,256]{1,0:T(8,128)(2,1)S(1)} %get-tuple-element.49), channel_id=1, source_target_pairs={{0,4},{1,5},{2,6},{3,7},{4,8},{5,9},{6,10},{7,11},{8,12},{9,13},{1... | collective-permute-start | bytes 786440 | tf_op jit(solution)/shard_map/ppermute | solution.py:512
  50.0 2.4 %collective-permute-start.9 = (bf16[512,256]{1,0:T(8,128)(2,1)S(1)}, bf16[512,256]{1,0:T(8,128)(2,1)S(1)}, u32[]{:S(2)}, u32[]{:S(2)}) collective-permute-start(bf16[512,256]{1,0:T(8,128)(2,1)S(1)} %get-tuple-element.50), channel_id=1, source_target_pairs={{0,12},{1,13},{2,14},{3,15},{4,0},{5,1},{6,2},{7,3},{8,4},{9,5},{1... | collective-permute-start | bytes 786440 | tf_op jit(solution)/shard_map/ppermute | solution.py:513
  52.4 0.0 collective-permute-start.11
  52.4 2.3 %collective-permute-start.12 = (bf16[128,768]{1,0:T(8,128)(2,1)S(1)}, bf16[128,768]{1,0:T(8,128)(2,1)S(1)}, u32[]{:S(2)}, u32[]{:S(2)}) collective-permute-start(bf16[128,768]{1,0:T(8,128)(2,1)S(1)} %get-tuple-element.56), channel_id=1, source_target_pairs={{0,64},{16,80},{32,96},{48,112},{64,0},{80,16},{96,32},{112,48},{1... | collective-permute-start | bytes 589832 | tf_op jit(solution)/shard_map/ppermute | solution.py:509
  54.7 1.2 %collective-permute-start.13 = (bf16[128,768]{1,0:T(8,128)(2,1)S(1)}, bf16[128,768]{1,0:T(8,128)(2,1)S(1)}, u32[]{:S(2)}, u32[]{:S(2)}) collective-permute-start(bf16[128,768]{1,0:T(8,128)(2,1)S(1)} %get-tuple-element.57), channel_id=1, source_target_pairs={{0,96},{16,112},{32,0},{48,16},{64,32},{80,48},{96,64},{112,80},{1... | collective-permute-start | bytes 589832 | tf_op jit(solution)/shard_map/ppermute | solution.py:509
  55.9 2.9 %collective-permute-done.8.a = bf16[512,256]{1,0:T(8,128)(2,1)S(1)} collective-permute-done((bf16[512,256]{1,0:T(8,128)(2,1)S(1)}, bf16[512,256]{1,0:T(8,128)(2,1)S(1)}, u32[]{:S(2)}, u32[]{:S(2)}) %collective-permute-start.8) | collective-permute-done | bytes 262176 | tf_op jit(solution)/shard_map/ppermute | solution.py:512
  58.8 0.0 collective-permute-done.9.b
  58.8 0.2 pair.1
  59.1 2.8 %collective-permute-start.10 = (bf16[512,256]{1,0:T(8,128)(2,1)S(1)}, bf16[512,256]{1,0:T(8,128)(2,1)S(1)}, u32[]{:S(2)}, u32[]{:S(2)}) collective-permute-start(bf16[512,256]{1,0:T(8,128)(2,1)S(1)} %get-tuple-element.52), channel_id=1, source_target_pairs={{0,2},{1,3},{2,0},{3,1},{4,6},{5,7},{6,4},{7,5},{8,10},{9,11},{10,... | collective-permute-start | bytes 786440 | tf_op jit(solution)/shard_map/ppermute | solution.py:525
  61.9 2.4 %collective-permute-done.11.a1 = bf16[128,768]{1,0:T(8,128)(2,1)S(1)} collective-permute-done((bf16[128,768]{1,0:T(8,128)(2,1)S(1)}, bf16[128,768]{1,0:T(8,128)(2,1)S(1)}, u32[]{:S(2)}, u32[]{:S(2)}) %collective-permute-start.11) | collective-permute-done | bytes 196640 | tf_op jit(solution)/shard_map/ppermute | solution.py:509
  64.3 0.0 collective-permute-done.12.a2
  64.3 0.6 collective-permute-done.13.a3
  64.9 0.8 %sum_y.1 = (bf16[128,640]{1,0:T(8,128)(2,1)}, bf16[128,128]{1,0:T(8,128)(2,1)S(1)}, bf16[128,128]{1,0:T(8,128)(2,1)S(1)}) custom-call(bf16[128,768]{1,0:T(8,128)(2,1)S(1)} %get-tuple-element.48.after.a0, bf16[128,768]{1,0:T(8,128)(2,1)S(1)} %collective-permute-done.11.a1, bf16[128,768]{1,0:T(8,128)(2,1)S(1)} %collective-permute-done.12.a2, ...), custom_call_target="tpu_custom_call" | custom-call | tf_op jit(solution)/shard_map/sum_y/pallas_call | solution.py:381
  65.7 4.6 %all-to-all-start.1 = ((bf16[16,8,640]{2,1,0:T(8,128)(2,1)}), bf16[16,8,640]{2,1,0:T(8,128)(2,1)S(1)}, u32[]{:S(2)}, u32[]{:S(2)}) async-start(bf16[16,8,640]{2,1,0:T(8,128)(2,1)} %bitcast.19), calls=%async_computation.1 | async-start | bytes 327680 | tf_op jit(solution)/shard_map/all_to_all | solution.py:521
  70.3 1.9 %collective-permute-start.14 = (bf16[128,128]{1,0:T(8,128)(2,1)S(1)}, bf16[128,128]{1,0:T(8,128)(2,1)S(1)}, u32[]{:S(2)}, u32[]{:S(2)}) collective-permute-start(bf16[128,128]{1,0:T(8,128)(2,1)S(1)} %get-tuple-element.59), channel_id=1, source_target_pairs={{0,16},{16,0},{32,48},{48,32},{64,80},{80,64},{96,112},{112,96},{1... | collective-permute-start | bytes 98312 | tf_op jit(solution)/shard_map/ppermute | solution.py:520
  72.3 0.0 collective-permute-done.10.got
  72.3 0.8 %weights.1 = (f32[128,512]{1,0:T(8,128)}, f32[512,128]{1,0:T(8,128)}, f32[8,128]{1,0:T(8,128)S(1)}) custom-call(bf16[512,256]{1,0:T(8,128)(2,1)S(1)} %get-tuple-element.51.mine, bf16[512,256]{1,0:T(8,128)(2,1)S(1)} %collective-permute-done.10.got), custom_call_target="tpu_custom_call" | custom-call | tf_op jit(solution)/shard_map/weights/pallas_call | solution.py:465
  73.1 2.1 %collective-permute-done.14.got = bf16[128,128]{1,0:T(8,128)(2,1)S(1)} collective-permute-done((bf16[128,128]{1,0:T(8,128)(2,1)S(1)}, bf16[128,128]{1,0:T(8,128)(2,1)S(1)}, u32[]{:S(2)}, u32[]{:S(2)}) %collective-permute-start.14) | collective-permute-done | bytes 32800 | tf_op jit(solution)/shard_map/ppermute | solution.py:520
  75.2 3.3 %all-to-all-done.1 = bf16[16,8,640]{2,1,0:T(8,128)(2,1)S(1)} async-done(((bf16[16,8,640]{2,1,0:T(8,128)(2,1)}), bf16[16,8,640]{2,1,0:T(8,128)(2,1)S(1)}, u32[]{:S(2)}, u32[]{:S(2)}) %all-to-all-start.1) | async-done | bytes 163872 | tf_op jit(solution)/shard_map/all_to_all | solution.py:521
  78.6 0.7 final.1
Async XLA Ops:
  2.5 17.0 %all-to-all-start = ((bf16[8,64,640]{2,1,0:T(8,128)(2,1)}), bf16[8,64,640]{2,1,0:T(8,128)(2,1)S(1)}, u32[]{:S(2)}, u32[]{:S(2)}) async-start(bf16[8,64,640]{2,1,0:T(8,128)(2,1)} %keys.1), calls=%async_computation | async-start | bytes 1310720 | tf_op jit(solution)/shard_map/all_to_all | solution.py:493
  8.7 10.8 %copy-start.2 = (bf16[128,512]{1,0:T(8,128)(2,1)S(1)}, bf16[128,512]{1,0:T(8,128)(2,1)}, u32[]{:S(2)}) copy-start(bf16[128,512]{1,0:T(8,128)(2,1)} %clat.1) | copy-start | bytes 393220
  8.7 10.8 %copy-start.3 = (bf16[128,64]{0,1:T(8,128)(2,1)S(1)}, bf16[128,64]{0,1:T(8,128)(2,1)}, u32[]{:S(2)}) copy-start(bf16[128,64]{0,1:T(8,128)(2,1)} %param.18) | copy-start | bytes 49156
  14.4 7.5 %collective-permute-start.2 = (bf16[8,128,384]{2,1,0:T(8,128)(2,1)}, bf16[8,128,384]{2,1,0:T(8,128)(2,1)S(1)}, u32[]{:S(2)}, u32[]{:S(2)}) collective-permute-start(bf16[8,128,384]{2,1,0:T(8,128)(2,1)} %get-tuple-element.38), channel_id=1, source_target_pairs={{0,1},{1,0},{2,3},{3,2},{4,5},{5,4},{6,7},{7,6},{8,9},{9,8},{10,11... | collective-permute-start | bytes 2359304 | tf_op jit(solution)/shard_map/ppermute | solution.py:497
  19.5 2.4 %collective-permute-start = (bf16[512,640]{1,0:T(8,128)(2,1)S(1)}, bf16[512,640]{1,0:T(8,128)(2,1)S(1)}, u32[]{:S(2)}, u32[]{:S(2)}) collective-permute-start(bf16[512,640]{1,0:T(8,128)(2,1)S(1)} %bitcast.23), channel_id=1, source_target_pairs={{0,1},{1,0},{2,3},{3,2},{4,5},{5,4},{6,7},{7,6},{8,9},{9,8},{10,11... | collective-permute-start | bytes 1966088 | tf_op jit(solution)/shard_map/ppermute | solution.py:500
  19.5 0.7 copy-start.4
  20.2 1.7 %copy-start = (bf16[8,256,512]{2,1,0:T(8,128)(2,1)S(1)}, bf16[8,256,512]{2,1,0:T(8,128)(2,1)}, u32[]{:S(2)}) copy-start(bf16[8,256,512]{2,1,0:T(8,128)(2,1)} %get-tuple-element.39) | copy-start | bytes 6291460
  20.2 1.8 %copy-start.1 = (bf16[8,128,384]{2,1,0:T(8,128)(2,1)S(1)}, bf16[8,128,384]{2,1,0:T(8,128)(2,1)}, u32[]{:S(2)}) copy-start(bf16[8,128,384]{2,1,0:T(8,128)(2,1)} %get-tuple-element.37.refs_4_) | copy-start | bytes 2359300
  20.3 1.6 %collective-permute-start.1 = (bf16[128,640]{1,0:T(8,128)(2,1)S(1)}, bf16[128,640]{1,0:T(8,128)(2,1)S(1)}, u32[]{:S(2)}, u32[]{:S(2)}) collective-permute-start(bf16[128,640]{1,0:T(8,128)(2,1)S(1)} %own_keys.1.refs_2_), channel_id=1, source_target_pairs={{0,1},{1,0},{2,3},{3,2},{4,5},{5,4},{6,7},{7,6},{8,9},{9,8},{10,11... | collective-permute-start | bytes 491528 | tf_op jit(solution)/shard_map/ppermute | solution.py:499
  31.8 17.1 %collective-permute-start.3 = (bf16[2,512,256]{2,1,0:T(8,128)(2,1)S(1)}, bf16[2,512,256]{2,1,0:T(8,128)(2,1)S(1)}, u32[]{:S(2)}, u32[]{:S(2)}) collective-permute-start(bf16[2,512,256]{2,1,0:T(8,128)(2,1)S(1)} %get-tuple-element.42), channel_id=1, source_target_pairs={{0,4},{1,5},{2,6},{3,7},{4,8},{5,9},{6,10},{7,11},{8,12},{9,13},{1... | collective-permute-start | bytes 1572872 | tf_op jit(solution)/shard_map/ppermute | solution.py:503
  33.8 15.1 %collective-permute-start.4 = (bf16[2,512,256]{2,1,0:T(8,128)(2,1)S(1)}, bf16[2,512,256]{2,1,0:T(8,128)(2,1)S(1)}, u32[]{:S(2)}, u32[]{:S(2)}) collective-permute-start(bf16[2,512,256]{2,1,0:T(8,128)(2,1)S(1)} %get-tuple-element.43), channel_id=1, source_target_pairs={{0,12},{1,13},{2,14},{3,15},{4,0},{5,1},{6,2},{7,3},{8,4},{9,5},{1... | collective-permute-start | bytes 1572872 | tf_op jit(solution)/shard_map/ppermute | solution.py:504
  46.1 2.4 %collective-permute-start.5 = (bf16[256,640]{1,0:T(8,128)(2,1)S(1)}, bf16[256,640]{1,0:T(8,128)(2,1)S(1)}, u32[]{:S(2)}, u32[]{:S(2)}) collective-permute-start(bf16[256,640]{1,0:T(8,128)(2,1)S(1)} %get-tuple-element.45), channel_id=1, source_target_pairs={{0,1},{1,0},{2,3},{3,2},{4,5},{5,4},{6,7},{7,6},{8,9},{9,8},{10,11... | collective-permute-start | bytes 983048 | tf_op jit(solution)/shard_map/ppermute | solution.py:506
  46.4 2.1 %collective-permute-start.6 = (bf16[256,640]{1,0:T(8,128)(2,1)S(1)}, bf16[256,640]{1,0:T(8,128)(2,1)S(1)}, u32[]{:S(2)}, u32[]{:S(2)}) collective-permute-start(bf16[256,640]{1,0:T(8,128)(2,1)S(1)} %get-tuple-element.46), channel_id=1, source_target_pairs={{0,1},{1,0},{2,3},{3,2},{4,5},{5,4},{6,7},{7,6},{8,9},{9,8},{10,11... | collective-permute-start | bytes 983048 | tf_op jit(solution)/shard_map/ppermute | solution.py:506
  46.7 1.8 %collective-permute-start.7 = (bf16[128,640]{1,0:T(8,128)(2,1)S(1)}, bf16[128,640]{1,0:T(8,128)(2,1)S(1)}, u32[]{:S(2)}, u32[]{:S(2)}) collective-permute-start(bf16[128,640]{1,0:T(8,128)(2,1)S(1)} %get-tuple-element.47), channel_id=1, source_target_pairs={{0,1},{1,0},{2,3},{3,2},{4,5},{5,4},{6,7},{7,6},{8,9},{9,8},{10,11... | collective-permute-start | bytes 491528 | tf_op jit(solution)/shard_map/ppermute | solution.py:506
  49.1 9.7 %collective-permute-start.8 = (bf16[512,256]{1,0:T(8,128)(2,1)S(1)}, bf16[512,256]{1,0:T(8,128)(2,1)S(1)}, u32[]{:S(2)}, u32[]{:S(2)}) collective-permute-start(bf16[512,256]{1,0:T(8,128)(2,1)S(1)} %get-tuple-element.49), channel_id=1, source_target_pairs={{0,4},{1,5},{2,6},{3,7},{4,8},{5,9},{6,10},{7,11},{8,12},{9,13},{1... | collective-permute-start | bytes 786440 | tf_op jit(solution)/shard_map/ppermute | solution.py:512
  50.0 8.8 %collective-permute-start.9 = (bf16[512,256]{1,0:T(8,128)(2,1)S(1)}, bf16[512,256]{1,0:T(8,128)(2,1)S(1)}, u32[]{:S(2)}, u32[]{:S(2)}) collective-permute-start(bf16[512,256]{1,0:T(8,128)(2,1)S(1)} %get-tuple-element.50), channel_id=1, source_target_pairs={{0,12},{1,13},{2,14},{3,15},{4,0},{5,1},{6,2},{7,3},{8,4},{9,5},{1... | collective-permute-start | bytes 786440 | tf_op jit(solution)/shard_map/ppermute | solution.py:513
  52.4 11.9 %collective-permute-start.11 = (bf16[128,768]{1,0:T(8,128)(2,1)S(1)}, bf16[128,768]{1,0:T(8,128)(2,1)S(1)}, u32[]{:S(2)}, u32[]{:S(2)}) collective-permute-start(bf16[128,768]{1,0:T(8,128)(2,1)S(1)} %get-tuple-element.55), channel_id=1, source_target_pairs={{0,32},{16,48},{32,64},{48,80},{64,96},{80,112},{96,0},{112,16},{1... | collective-permute-start | bytes 589832 | tf_op jit(solution)/shard_map/ppermute | solution.py:509
  52.4 11.9 %collective-permute-start.12 = (bf16[128,768]{1,0:T(8,128)(2,1)S(1)}, bf16[128,768]{1,0:T(8,128)(2,1)S(1)}, u32[]{:S(2)}, u32[]{:S(2)}) collective-permute-start(bf16[128,768]{1,0:T(8,128)(2,1)S(1)} %get-tuple-element.56), channel_id=1, source_target_pairs={{0,64},{16,80},{32,96},{48,112},{64,0},{80,16},{96,32},{112,48},{1... | collective-permute-start | bytes 589832 | tf_op jit(solution)/shard_map/ppermute | solution.py:509
  54.7 10.2 %collective-permute-start.13 = (bf16[128,768]{1,0:T(8,128)(2,1)S(1)}, bf16[128,768]{1,0:T(8,128)(2,1)S(1)}, u32[]{:S(2)}, u32[]{:S(2)}) collective-permute-start(bf16[128,768]{1,0:T(8,128)(2,1)S(1)} %get-tuple-element.57), channel_id=1, source_target_pairs={{0,96},{16,112},{32,0},{48,16},{64,32},{80,48},{96,64},{112,80},{1... | collective-permute-start | bytes 589832 | tf_op jit(solution)/shard_map/ppermute | solution.py:509
  59.1 13.2 %collective-permute-start.10 = (bf16[512,256]{1,0:T(8,128)(2,1)S(1)}, bf16[512,256]{1,0:T(8,128)(2,1)S(1)}, u32[]{:S(2)}, u32[]{:S(2)}) collective-permute-start(bf16[512,256]{1,0:T(8,128)(2,1)S(1)} %get-tuple-element.52), channel_id=1, source_target_pairs={{0,2},{1,3},{2,0},{3,1},{4,6},{5,7},{6,4},{7,5},{8,10},{9,11},{10,... | collective-permute-start | bytes 786440 | tf_op jit(solution)/shard_map/ppermute | solution.py:525
  65.7 12.8 %all-to-all-start.1 = ((bf16[16,8,640]{2,1,0:T(8,128)(2,1)}), bf16[16,8,640]{2,1,0:T(8,128)(2,1)S(1)}, u32[]{:S(2)}, u32[]{:S(2)}) async-start(bf16[16,8,640]{2,1,0:T(8,128)(2,1)} %bitcast.19), calls=%async_computation.1 | async-start | bytes 327680 | tf_op jit(solution)/shard_map/all_to_all | solution.py:521
  70.3 4.9 %collective-permute-start.14 = (bf16[128,128]{1,0:T(8,128)(2,1)S(1)}, bf16[128,128]{1,0:T(8,128)(2,1)S(1)}, u32[]{:S(2)}, u32[]{:S(2)}) collective-permute-start(bf16[128,128]{1,0:T(8,128)(2,1)S(1)} %get-tuple-element.59), channel_id=1, source_target_pairs={{0,16},{16,0},{32,48},{48,32},{64,80},{80,64},{96,112},{112,96},{1... | collective-permute-start | bytes 98312 | tf_op jit(solution)/shard_map/ppermute | solution.py:520

commit v4 on v3

--- a/solution.py
+++ b/solution.py
@@ -172,129 +172,114 @@
     else:
         plus, minus, acc = take(3)
     kall, kt, kx, s_ref, dp_ref, pb, ds, xy, rop = take(9)
-    step = pl.program_id(0)
+    base = 4 if last else 0
     CH = 128
     NC = (PK + ROWS) // CH
 
-    @pl.when(step == 0)
-    def _():
-        for at, ref in ((0, kva), (512, kvb)):
-            kall[at : at + 512] = ref[:, 0:LAT]
-            for h in range(HPS):
-                kx[h, at : at + 512, 128:256] = ref[:, LAT:KW]
-        for at, ref in ((PK, ckeep), (PK + ROWS, crecv)):
-            kall[at : at + ROWS] = ref[:, 0:LAT]
-            for h in range(HPS):
-                kx[h, at : at + ROWS, 128:256] = ref[:, LAT:KW]
-        for b in range(AK // 256):
-            kt[:, b * 256 : b * 256 + 256] = kall[b * 256 : b * 256 + 256, :].T
-        zero = jnp.zeros((ROWS, ROWS), bf16)
-        for ref in (pb, ds):
-            for h in range(HPS):
-                ref[h, PK : PK + ROWS, ROWS:W] = zero
-                ref[h, PK + ROWS : AK, 0:ROWS] = zero
-        rop[...] = acc[:, LAT:KW] if last else jnp.zeros_like(rop)
+    for at, ref in ((0, kva), (512, kvb)):
+        kall[at : at + 512] = ref[:, 0:LAT]
+        for h in range(HPS):
+            kx[h, at : at + 512, 128:256] = ref[:, LAT:KW]
+    for at, ref in ((PK, ckeep), (PK + ROWS, crecv)):
+        kall[at : at + ROWS] = ref[:, 0:LAT]
+        for h in range(HPS):
+            kx[h, at : at + ROWS, 128:256] = ref[:, LAT:KW]
+    for b in range(AK // 256):
+        kt[:, b * 256 : b * 256 + 256] = kall[b * 256 : b * 256 + 256, :].T
+    zero = jnp.zeros((ROWS, ROWS), bf16)
+    for ref in (pb, ds):
+        for h in range(HPS):
+            ref[h, PK : PK + ROWS, ROWS:W] = zero
+            ref[h, PK + ROWS : AK, 0:ROWS] = zero
+    rop[...] = acc[:, LAT:KW] if last else jnp.zeros_like(rop)
 
     iu = lax.broadcasted_iota(jnp.int32, (ROWS, W), 0)
     it = lax.broadcasted_iota(jnp.int32, (ROWS, W), 1) % ROWS
     seen = ((iu // SLEN) == (it // SLEN)) & (iu <= it)
-    queries = []
-    for h in range(HPS):
-        at = pl.multiple_of((step * HPS + h) * W, W)
-        r = nt(kall[...], ww[pl.ds(at, W), :])
-        kx[h, :, 0:128] = r[:, 0:128].astype(bf16)
-        kx[h, :, 256:384] = r[:, 128:256].astype(bf16)
-    for h in range(HPS):
-        qx = jnp.concatenate([keep[h, :, 0:256], recv[h, :, 0:256]], axis=0)
-        g = jnp.concatenate([keep[h, :, 256:HW], recv[h, :, 256:HW]], axis=0)
-        queries.append((qx, g))
-        s_ref[h, 0:PK] = nt(kx[h, 0:PK, 0:256], qx)
-        own = nt(kx[h, PK:AK, 0:256], qx)
-        own = jnp.concatenate([own[0:ROWS, 0:ROWS], own[ROWS:W, ROWS:W]], axis=1)
-        s_ref[h, PK : PK + ROWS] = jnp.where(seen, own, -jnp.inf)
-        dp_ref[h, 0:PK] = nt(kx[h, 0:PK, 256:384], g)
-        own = nt(kx[h, PK:AK, 256:384], g)
-        dp_ref[h, PK : PK + ROWS] = jnp.concatenate(
-            [own[0:ROWS, 0:ROWS], own[ROWS:W, ROWS:W]], axis=1
-        )
-    both = []
-    for h in range(HPS):
-        qx, g = queries[h]
-        top = jnp.full((8, W), -jnp.inf, f32)
-        for c in range(NC):
-            x = s_ref[h, c * CH : c * CH + CH].reshape(CH // 8, 8, W)
-            top = jnp.maximum(top, jnp.max(x, axis=0))
-        top = jnp.max(top, axis=0, keepdims=True)
-        total = jnp.zeros((8, W), f32)
-        delta = jnp.zeros((8, W), f32)
-        for c in range(NC):
-            cs = slice(c * CH, c * CH + CH)
-            e = jnp.exp2((s_ref[h, cs] - top) * (SCALE * LOG2E))
-            s_ref[h, cs] = e
-            total = total + jnp.sum(e.reshape(CH // 8, 8, W), axis=0)
-            delta = delta + jnp.sum((e * dp_ref[h, cs]).reshape(CH // 8, 8, W), axis=0)
-        inv = 1.0 / jnp.sum(total, axis=0, keepdims=True)
-        delta = jnp.sum(delta, axis=0, keepdims=True) * inv
-        cinv = inv * SCALE
-        for c in range(NC):
-            cs = slice(c * CH, c * CH + CH)
-            e = s_ref[h, cs]
-            p = (e * inv).astype(bf16)
-            d = (e * cinv * (dp_ref[h, cs] - delta)).astype(bf16)
-            if c < NC - 1:
-                pb[h, cs] = p
-                ds[h, cs] = d
+    for step in range(STEPS):
+        queries = []
+        for h in range(HPS):
+            at = (step * HPS + h) * W
+            r = nt(kall[...], ww[base * W + at : base * W + at + W, :])
+            kx[h, :, 0:128] = r[:, 0:128].astype(bf16)
+            kx[h, :, 256:384] = r[:, 128:256].astype(bf16)
+        for h in range(HPS):
+            qx = jnp.concatenate([keep[base + step * HPS + h, :, 0:256], recv[base + step * HPS + h, :, 0:256]], axis=0)
+            g = jnp.concatenate([keep[base + step * HPS + h, :, 256:HW], recv[base + step * HPS + h, :, 256:HW]], axis=0)
+            queries.append((qx, g))
+            s_ref[h, 0:PK] = nt(kx[h, 0:PK, 0:256], qx)
+            own = nt(kx[h, PK:AK, 0:256], qx)
+            own = jnp.concatenate([own[0:ROWS, 0:ROWS], own[ROWS:W, ROWS:W]], axis=1)
+            s_ref[h, PK : PK + ROWS] = jnp.where(seen, own, -jnp.inf)
+            dp_ref[h, 0:PK] = nt(kx[h, 0:PK, 256:384], g)
+            own = nt(kx[h, PK:AK, 256:384], g)
+            dp_ref[h, PK : PK + ROWS] = jnp.concatenate(
+                [own[0:ROWS, 0:ROWS], own[ROWS:W, ROWS:W]], axis=1
+            )
+        both = []
+        for h in range(HPS):
+            qx, g = queries[h]
+            top = jnp.full((8, W), -jnp.inf, f32)
+            for c in range(NC):
+                x = s_ref[h, c * CH : c * CH + CH].reshape(CH // 8, 8, W)
+                top = jnp.maximum(top, jnp.max(x, axis=0))
+            top = jnp.max(top, axis=0, keepdims=True)
+            total = jnp.zeros((8, W), f32)
+            delta = jnp.zeros((8, W), f32)
+            for c in range(NC):
+                cs = slice(c * CH, c * CH + CH)
+                e = jnp.exp2((s_ref[h, cs] - top) * (SCALE * LOG2E))
+                s_ref[h, cs] = e
+                total = total + jnp.sum(e.reshape(CH // 8, 8, W), axis=0)
+                delta = delta + jnp.sum((e * dp_ref[h, cs]).reshape(CH // 8, 8, W), axis=0)
+            inv = 1.0 / jnp.sum(total, axis=0, keepdims=True)
+            delta = jnp.sum(delta, axis=0, keepdims=True) * inv
+            cinv = inv * SCALE
+            for c in range(NC):
+                cs = slice(c * CH, c * CH + CH)
+                e = s_ref[h, cs]
+                p = (e * inv).astype(bf16)
+                d = (e * cinv * (dp_ref[h, cs] - delta)).astype(bf16)
+                if c < NC - 1:
+                    pb[h, cs] = p
+                    ds[h, cs] = d
+                else:
+                    for ref, x in ((pb, p), (ds, d)):
+                        ref[h, PK : PK + ROWS, 0:ROWS] = x[:, 0:ROWS]
+                        ref[h, PK + ROWS : AK, ROWS:W] = x[:, ROWS:W]
+            x = nn(ds[h], qx)
+            rop[...] += x[:, 128:256]
+            y = nn(pb[h], g)
+            xx = jnp.concatenate([x[:, 0:128].astype(bf16), y.astype(bf16)], axis=1)
+            at = (step * HPS + h) * W
+            xy[:, at : at + W] = xx
+            both.append(xx)
+        for h in range(HPS):
+            out = nn(kt[...], both[h]).astype(bf16)
+            if last:
+                rest[step * HPS + h] = out
+            elif h == 0:
+                plus[step] = out
             else:
-                for ref, x in ((pb, p), (ds, d)):
-                    ref[h, PK : PK + ROWS, 0:ROWS] = x[:, 0:ROWS]
-                    ref[h, PK + ROWS : AK, ROWS:W] = x[:, ROWS:W]
-        x = nn(ds[h], qx)
-        rop[...] += x[:, 128:256]
-        y = nn(pb[h], g)
-        xx = jnp.concatenate([x[:, 0:128].astype(bf16), y.astype(bf16)], axis=1)
-        at = pl.multiple_of((step * HPS + h) * W, W)
-        xy[:, pl.ds(at, W)] = xx
-        both.append(xx)
-    for h in range(HPS):
-        out = nn(kt[...], both[h]).astype(bf16)
-        if last:
-            rest[h] = out
-        elif h == 0:
-            plus[0] = out
-        else:
-            minus[0] = out
-
-    @pl.when(step == STEPS - 1)
-    def _():
-        r = nn(xy[...], ww[...])
-        if last:
-            r = jnp.concatenate([r + acc[:, 0:LAT], rop[...]], axis=1).astype(bf16)
-            stay[0:512] = r[0:512]
-            stay[512:640] = r[PK : PK + ROWS]
-            give_a[...] = r[512:768]
-            give_b[...] = r[768:1024]
-            give_c[...] = r[PK + ROWS : AK]
-        else:
-            acc[:, 0:LAT] = r
-            acc[:, LAT:KW] = rop[...]
+                minus[step] = out
+
+    r = nn(xy[...], ww[base * W : (base + 4) * W, :])
+    if last:
+        r = jnp.concatenate([r + acc[:, 0:LAT], rop[...]], axis=1).astype(bf16)
+        stay[0:512] = r[0:512]
+        stay[512:640] = r[PK : PK + ROWS]
+        give_a[...] = r[512:768]
+        give_b[...] = r[768:1024]
+        give_c[...] = r[PK + ROWS : AK]
+    else:
+        acc[:, 0:LAT] = r
+        acc[:, LAT:KW] = rop[...]
 
 
 def attend(last, kva, kvb, ckeep, crecv, keep, recv, ww, acc=None):
-    base = 2 if last else 0
-
-    def full(a, b):
-        return pl.BlockSpec((a, b), lambda s: (0, 0))
-
-    def block(n):
-        return pl.BlockSpec((n, LAT, 2 * NOPE), lambda s: (s, 0, 0))
-
     def shape(n):
         return jax.ShapeDtypeStruct((n, LAT, 2 * NOPE), bf16)
 
-    heads = pl.BlockSpec((HPS, ROWS, HW), lambda s: (base + s, 0, 0))
-    ckeys = full(ROWS, KW)
-    weights = pl.BlockSpec((STEPS * HPS * W, LAT), lambda s: (base // 2, 0))
-    in_specs = [full(512, KW), full(512, KW), ckeys, ckeys, heads, heads, weights]
     ops = [kva, kvb, ckeep, crecv, keep, recv, ww]
     scratch = [
         pltpu.VMEM((AK, LAT), bf16),
@@ -308,24 +293,19 @@
         pltpu.VMEM((AK, 128), f32),
     ]
     if last:
-        in_specs.append(full(AK, KW))
         ops.append(acc)
         out_shape = [shape(4)]
-        out_specs = [block(2)]
         for n in (640, 256, 256, ROWS):
             out_shape.append(jax.ShapeDtypeStruct((n, KW), bf16))
-            out_specs.append(full(n, KW))
     else:
-        out_shape = (shape(2), shape(2), jax.ShapeDtypeStruct((AK, KW), f32))
-        out_specs = (block(1), block(1), full(AK, KW))
+        out_shape = [shape(2), shape(2), jax.ShapeDtypeStruct((AK, KW), f32)]
     return pl.pallas_call(
         functools.partial(attend_kernel, last),
         out_shape=out_shape,
-        grid=(STEPS,),
-        in_specs=in_specs,
-        out_specs=out_specs,
+        in_specs=[VM] * len(ops),
+        out_specs=[VM] * len(out_shape),
         scratch_shapes=scratch,
-        compiler_params=params(36),
+        compiler_params=params(30),
         cost_estimate=cost(10**10, 10 * 2**20),
         name="attend",
     )(*ops)
@@ -392,7 +372,7 @@
     )(*parts)
 
 
-def final_kernel(mine, got, dlat, after, ol, orp, ocl, ocr):
+def final_kernel(mine, got, dlat, ol, orp, ocl, ocr):
     c = (mine[...].astype(f32) + got[...].astype(f32)).T
     ocl[...] = c[0:64]
     ocr[...] = c[64:72]
@@ -401,7 +381,7 @@
     orp[...] = x[:, LAT : LAT + ROPE]
 
 
-def final(mine, got, dlat, after):
+def final(mine, got, dlat):
     return pl.pallas_call(
         final_kernel,
         out_shape=(
@@ -410,11 +390,11 @@
             jax.ShapeDtypeStruct((64, ROWS), f32),
             jax.ShapeDtypeStruct((8, ROWS), f32),
         ),
-        in_specs=[VM] * 4,
+        in_specs=[VM] * 3,
         out_specs=(VM,) * 4,
         compiler_params=params(24),
         name="final",
-    )(mine, got, dlat, after)
+    )(mine, got, dlat)
 
 
 def ring_kernel(rest, p, m, after, a, b):
@@ -454,8 +434,7 @@
     )(rest, p, m, a, b)
 
 
-def weights_kernel(mine, got, dwk, dwv, done):
-    done[...] = jnp.zeros_like(done)
+def weights_kernel(mine, got, dwk, dwv):
     x = mine[...].astype(f32) + got[...].astype(f32)
     dwk[...] = x[:, 0:NOPE].T
     dwv[...] = x[:, NOPE : 2 * NOPE]
@@ -467,10 +446,9 @@
         out_shape=(
             jax.ShapeDtypeStruct((NOPE, LAT), f32),
             jax.ShapeDtypeStruct((LAT, NOPE), f32),
-            jax.ShapeDtypeStruct((8, 128), f32),
         ),
         in_specs=[VM, VM],
-        out_specs=(VM, VM, VM),
+        out_specs=(VM, VM),
         compiler_params=params(24),
         name="weights",
     )(mine, got)
@@ -523,8 +501,8 @@
     )
     mine, send = pair(rest, plus, minus, a, b)
     other = lax.ppermute(send, "comp", [(c, c ^ 2) for c in range(16)])
-    dwk, dwv, done = weights(mine, other)
-    ol, orp, ocl, ocr = final(cmine, cgot, dlat, done)
+    dwk, dwv = weights(mine, other)
+    ol, orp, ocl, ocr = final(cmine, cgot, dlat)
     return dwk[None], dwv[None], ol, orp, ocl.T, ocr.T
 
 

time: 79.7 us -> 79.5 us (level)
  Pallas kernels: 30.6 us -> 28.6 us
  waiting for transfers between devices: 19 us -> 20.3 us
    pallas_call x2, Pallas kernels: 19.8 us -> 17.7 us  [attend(): pl.pallas_call(functools.partial(attend_kernel, last), out_shape=out_shap...]
    ppermute x1, waiting for transfers between devices: 2.12 us -> 2.97 us  [local(): cgot = lax.ppermute(csend, 'prompt', [(i, i ^ 1) for i in range(8)])]
  transfers between devices with their start and end apart: 17 -> 17, of which waited for: 8 -> 9; matrix products, arithmetic and copies ran while one was open for 1% -> 1% of each run, Pallas kernels for 23% -> 21%
where the time goes in v4:
time: 79.5 us; the launch traced here: 79.1 us
  Pallas kernels  28.6 us (36%)
  starting transfers between devices  28.1 us (35%)
  waiting for transfers between devices  20.3 us (26%)
  local copies, waits for them, and re-layouts  1.41 us (2%)
    pallas_call x2, Pallas kernels, attend(): pl.pallas_call(functools.partial(attend_kernel, last), out_shape=out_shap...  17.7 us
    pallas_call x1, Pallas kernels, prep(): pl.pallas_call(prep_kernel, out_shape=(jax.ShapeDtypeStruct((8, ROWS, HW)...  5.75 us
    all_to_all x1, starting transfers between devices, local(): kva = lax.all_to_all(kv, 'prompt', 0, 0, tiled=True).reshape(512, KW)  5.48 us
    all_to_all x1, starting transfers between devices, local(): lax.all_to_all(dlat, ('prompt', 'comp'), 0, 0, tiled=True, axis_index_gro...  5.21 us
    all_to_all x1, waiting for transfers between devices, local(): kva = lax.all_to_all(kv, 'prompt', 0, 0, tiled=True).reshape(512, KW)  4.95 us
    ppermute x3, starting transfers between devices, local(): lax.ppermute(o[k], 'prompt', [(i, (i + 2 * k) % 8) for i in range(8)])  3.48 us
    all_to_all x1, waiting for transfers between devices, local(): lax.all_to_all(dlat, ('prompt', 'comp'), 0, 0, tiled=True, axis_index_gro...  3.33 us
    ppermute x3, waiting for transfers between devices, local(): lax.ppermute(o[k], 'prompt', [(i, (i + 2 * k) % 8) for i in range(8)])  3.13 us
  transfers between devices with their start and end apart: 17, of which 9 were waited for; matrix products, arithmetic and copies ran while one was open for 1% of the time, Pallas kernels for 21%

profile of v4, /device:TPU:0, one launch (start us, length us, event | category | flops | bytes accessed | tf_op | source)
XLA Modules:
  0.0 79.1 jit_solution(1280440546306133172)
XLA Ops:
  0.6 1.9 %keys.1 = bf16[8,64,640]{2,1,0:T(8,128)(2,1)} custom-call(bf16[128,512]{1,0:T(8,128)(2,1)} %lat.1, bf16[64,128]{1,0:T(8,128)(2,1)} %bitcast.30), custom_call_target="tpu_custom_call" | custom-call | tf_op jit(solution)/shard_map/keys/pallas_call | solution.py:59
  2.5 5.5 %all-to-all-start = ((bf16[8,64,640]{2,1,0:T(8,128)(2,1)}), bf16[8,64,640]{2,1,0:T(8,128)(2,1)S(1)}, u32[]{:S(2)}, u32[]{:S(2)}) async-start(bf16[8,64,640]{2,1,0:T(8,128)(2,1)} %keys.1), calls=%async_computation | async-start | bytes 1310720 | tf_op jit(solution)/shard_map/all_to_all | solution.py:471
  8.0 0.7 stack.55.info
  8.7 0.0 copy-start.2
  8.7 0.0 copy-start.3
  8.7 5.8 %prep.1 = (bf16[8,128,384]{2,1,0:T(8,128)(2,1)}, bf16[8,128,384]{2,1,0:T(8,128)(2,1)}, bf16[8,256,512]{2,1,0:T(8,128)(2,1)}, f32[8,128]{1,0:T(8,128)}) custom-call(s32[13]{0:T(128)} %stack.55.info, s32[2]{0:T(128)} %lens.1, bf16[128,2048]{1,0:T(8,128)(2,1)} %refs_8_.1, bf16[128,2048]{1,0:T(8,128)(2,1)} %refs_8_.1, bf16[128,2048]{1,0:T(8,128)(2,1)} %refs_10_.1, ...), custom_call_target="tpu_custom_call" | custom-call | flops 1000000000 | bytes 4194304 | tf_op jit(solution)/shard_map/prep/pallas_call | solution.py:133
  14.4 0.1 collective-permute-start.2
  14.5 4.9 %all-to-all-done = bf16[8,64,640]{2,1,0:T(8,128)(2,1)S(1)} async-done(((bf16[8,64,640]{2,1,0:T(8,128)(2,1)}), bf16[8,64,640]{2,1,0:T(8,128)(2,1)S(1)}, u32[]{:S(2)}, u32[]{:S(2)}) %all-to-all-start) | async-done | bytes 655392 | tf_op jit(solution)/shard_map/all_to_all | solution.py:471
  19.5 0.0 collective-permute-start
  19.5 0.0 copy-done.2
  19.5 0.0 copy-done.3
  19.5 0.0 copy-start.4
  19.5 0.7 copy-done.4
  20.2 0.0 copy-start
  20.2 0.0 copy-start.1
  20.2 0.1 own_keys.1.refs_2_
  20.3 0.6 collective-permute-start.1
  20.9 1.0 %collective-permute-done.1.refs_3_ = bf16[128,640]{1,0:T(8,128)(2,1)S(1)} collective-permute-done((bf16[128,640]{1,0:T(8,128)(2,1)S(1)}, bf16[128,640]{1,0:T(8,128)(2,1)S(1)}, u32[]{:S(2)}, u32[]{:S(2)}) %collective-permute-start.1) | collective-permute-done | bytes 163872 | tf_op jit(solution)/shard_map/ppermute | solution.py:477
  21.9 0.0 collective-permute-done.2.refs_5_
  21.9 0.0 collective-permute-done.refs_1_
  21.9 0.0 copy-done
  21.9 0.0 copy-done.1
  21.9 8.9 %attend.2 = (bf16[2,512,256]{2,1,0:T(8,128)(2,1)S(1)}, bf16[2,512,256]{2,1,0:T(8,128)(2,1)S(1)}, f32[1280,640]{1,0:T(8,128)S(1)}) custom-call(bf16[512,640]{1,0:T(8,128)(2,1)S(1)} %bitcast.24, bf16[512,640]{1,0:T(8,128)(2,1)S(1)} %collective-permute-done.refs_1_, bf16[128,640]{1,0:T(8,128)(2,1)S(1)} %own_keys.1.refs_2_, ...), custom_call_target="tpu_custom_call" | custom-call | flops 10000000000 | bytes 10485760 | tf_op jit(solution)/shard_map/attend/pallas_call | solution.py:302
  30.8 2.0 %collective-permute-start.3 = (bf16[2,512,256]{2,1,0:T(8,128)(2,1)S(1)}, bf16[2,512,256]{2,1,0:T(8,128)(2,1)S(1)}, u32[]{:S(2)}, u32[]{:S(2)}) collective-permute-start(bf16[2,512,256]{2,1,0:T(8,128)(2,1)S(1)} %get-tuple-element.41), channel_id=1, source_target_pairs={{0,4},{1,5},{2,6},{3,7},{4,8},{5,9},{6,10},{7,11},{8,12},{9,13},{1... | collective-permute-start | bytes 1572872 | tf_op jit(solution)/shard_map/ppermute | solution.py:481
  32.8 2.4 %collective-permute-start.4 = (bf16[2,512,256]{2,1,0:T(8,128)(2,1)S(1)}, bf16[2,512,256]{2,1,0:T(8,128)(2,1)S(1)}, u32[]{:S(2)}, u32[]{:S(2)}) collective-permute-start(bf16[2,512,256]{2,1,0:T(8,128)(2,1)S(1)} %get-tuple-element.42), channel_id=1, source_target_pairs={{0,12},{1,13},{2,14},{3,15},{4,0},{5,1},{6,2},{7,3},{8,4},{9,5},{1... | collective-permute-start | bytes 1572872 | tf_op jit(solution)/shard_map/ppermute | solution.py:482
  35.2 8.9 %attend.3 = (bf16[4,512,256]{2,1,0:T(8,128)(2,1)S(1)}, bf16[640,640]{1,0:T(8,128)(2,1)S(1)}, bf16[256,640]{1,0:T(8,128)(2,1)S(1)}, bf16[256,640]{1,0:T(8,128)(2,1)S(1)}, bf16[128,640]{1,0:T(8,128)(2,1)S(1)}) custom-call(bf16[512,640]{1,0:T(8,128)(2,1)S(1)} %bitcast.25, bf16[512,640]{1,0:T(8,128)(2,1)S(1)} %collective-permute-done.refs_1_, ...), custom_call_target="tpu_custom_call" | custom-call | flops 10000000000 | bytes 10485760 | tf_op jit(solution)/shard_map/attend/pallas_call | solution.py:302
  44.0 0.3 collective-permute-start.5
  44.3 0.3 collective-permute-start.6
  44.6 0.2 collective-permute-start.7
  44.9 1.6 %collective-permute-done.7.got_c = bf16[128,640]{1,0:T(8,128)(2,1)S(1)} collective-permute-done((bf16[128,640]{1,0:T(8,128)(2,1)S(1)}, bf16[128,640]{1,0:T(8,128)(2,1)S(1)}, u32[]{:S(2)}, u32[]{:S(2)}) %collective-permute-start.7) | collective-permute-done | bytes 163872 | tf_op jit(solution)/shard_map/ppermute | solution.py:484
  46.5 0.0 collective-permute-done.5.got_a
  46.5 0.0 collective-permute-done.6.got_b
  46.5 0.4 join.1
  46.9 0.6 collective-permute-done.3.p
  47.5 0.0 collective-permute-done.4.m
  47.5 0.1 ring.1
  47.6 1.3 %collective-permute-start.8 = (bf16[512,256]{1,0:T(8,128)(2,1)S(1)}, bf16[512,256]{1,0:T(8,128)(2,1)S(1)}, u32[]{:S(2)}, u32[]{:S(2)}) collective-permute-start(bf16[512,256]{1,0:T(8,128)(2,1)S(1)} %get-tuple-element.48), channel_id=1, source_target_pairs={{0,4},{1,5},{2,6},{3,7},{4,8},{5,9},{6,10},{7,11},{8,12},{9,13},{1... | collective-permute-start | bytes 786440 | tf_op jit(solution)/shard_map/ppermute | solution.py:490
  49.0 2.0 %collective-permute-start.9 = (bf16[512,256]{1,0:T(8,128)(2,1)S(1)}, bf16[512,256]{1,0:T(8,128)(2,1)S(1)}, u32[]{:S(2)}, u32[]{:S(2)}) collective-permute-start(bf16[512,256]{1,0:T(8,128)(2,1)S(1)} %get-tuple-element.49), channel_id=1, source_target_pairs={{0,12},{1,13},{2,14},{3,15},{4,0},{5,1},{6,2},{7,3},{8,4},{9,5},{1... | collective-permute-start | bytes 786440 | tf_op jit(solution)/shard_map/ppermute | solution.py:491
  51.0 0.0 collective-permute-start.11
  51.0 2.3 %collective-permute-start.12 = (bf16[128,768]{1,0:T(8,128)(2,1)S(1)}, bf16[128,768]{1,0:T(8,128)(2,1)S(1)}, u32[]{:S(2)}, u32[]{:S(2)}) collective-permute-start(bf16[128,768]{1,0:T(8,128)(2,1)S(1)} %get-tuple-element.55), channel_id=1, source_target_pairs={{0,64},{16,80},{32,96},{48,112},{64,0},{80,16},{96,32},{112,48},{1... | collective-permute-start | bytes 589832 | tf_op jit(solution)/shard_map/ppermute | solution.py:487
  53.3 1.2 %collective-permute-start.13 = (bf16[128,768]{1,0:T(8,128)(2,1)S(1)}, bf16[128,768]{1,0:T(8,128)(2,1)S(1)}, u32[]{:S(2)}, u32[]{:S(2)}) collective-permute-start(bf16[128,768]{1,0:T(8,128)(2,1)S(1)} %get-tuple-element.56), channel_id=1, source_target_pairs={{0,96},{16,112},{32,0},{48,16},{64,32},{80,48},{96,64},{112,80},{1... | collective-permute-start | bytes 589832 | tf_op jit(solution)/shard_map/ppermute | solution.py:487
  54.5 2.6 %collective-permute-done.8.a = bf16[512,256]{1,0:T(8,128)(2,1)S(1)} collective-permute-done((bf16[512,256]{1,0:T(8,128)(2,1)S(1)}, bf16[512,256]{1,0:T(8,128)(2,1)S(1)}, u32[]{:S(2)}, u32[]{:S(2)}) %collective-permute-start.8) | collective-permute-done | bytes 262176 | tf_op jit(solution)/shard_map/ppermute | solution.py:490
  57.1 0.0 collective-permute-done.9.b
  57.1 0.2 pair.1
  57.4 2.8 %collective-permute-start.10 = (bf16[512,256]{1,0:T(8,128)(2,1)S(1)}, bf16[512,256]{1,0:T(8,128)(2,1)S(1)}, u32[]{:S(2)}, u32[]{:S(2)}) collective-permute-start(bf16[512,256]{1,0:T(8,128)(2,1)S(1)} %get-tuple-element.51), channel_id=1, source_target_pairs={{0,2},{1,3},{2,0},{3,1},{4,6},{5,7},{6,4},{7,5},{8,10},{9,11},{10,... | collective-permute-start | bytes 786440 | tf_op jit(solution)/shard_map/ppermute | solution.py:503
  60.2 2.5 %collective-permute-done.11.a1 = bf16[128,768]{1,0:T(8,128)(2,1)S(1)} collective-permute-done((bf16[128,768]{1,0:T(8,128)(2,1)S(1)}, bf16[128,768]{1,0:T(8,128)(2,1)S(1)}, u32[]{:S(2)}, u32[]{:S(2)}) %collective-permute-start.11) | collective-permute-done | bytes 196640 | tf_op jit(solution)/shard_map/ppermute | solution.py:487
  62.7 0.0 collective-permute-done.12.a2
  62.7 0.6 collective-permute-done.13.a3
  63.3 0.8 %sum_y.1 = (bf16[128,640]{1,0:T(8,128)(2,1)}, bf16[128,128]{1,0:T(8,128)(2,1)S(1)}, bf16[128,128]{1,0:T(8,128)(2,1)S(1)}) custom-call(bf16[128,768]{1,0:T(8,128)(2,1)S(1)} %get-tuple-element.47.after.a0, bf16[128,768]{1,0:T(8,128)(2,1)S(1)} %collective-permute-done.11.a1, bf16[128,768]{1,0:T(8,128)(2,1)S(1)} %collective-permute-done.12.a2, ...), custom_call_target="tpu_custom_call" | custom-call | tf_op jit(solution)/shard_map/sum_y/pallas_call | solution.py:361
  64.1 5.2 %all-to-all-start.1 = ((bf16[16,8,640]{2,1,0:T(8,128)(2,1)}), bf16[16,8,640]{2,1,0:T(8,128)(2,1)S(1)}, u32[]{:S(2)}, u32[]{:S(2)}) async-start(bf16[16,8,640]{2,1,0:T(8,128)(2,1)} %bitcast.19), calls=%async_computation.1 | async-start | bytes 327680 | tf_op jit(solution)/shard_map/all_to_all | solution.py:499
  69.3 1.9 %collective-permute-start.14 = (bf16[128,128]{1,0:T(8,128)(2,1)S(1)}, bf16[128,128]{1,0:T(8,128)(2,1)S(1)}, u32[]{:S(2)}, u32[]{:S(2)}) collective-permute-start(bf16[128,128]{1,0:T(8,128)(2,1)S(1)} %get-tuple-element.58), channel_id=1, source_target_pairs={{0,16},{16,0},{32,48},{48,32},{64,80},{80,64},{96,112},{112,96},{1... | collective-permute-start | bytes 98312 | tf_op jit(solution)/shard_map/ppermute | solution.py:498
  71.3 3.0 %collective-permute-done.14.got = bf16[128,128]{1,0:T(8,128)(2,1)S(1)} collective-permute-done((bf16[128,128]{1,0:T(8,128)(2,1)S(1)}, bf16[128,128]{1,0:T(8,128)(2,1)S(1)}, u32[]{:S(2)}, u32[]{:S(2)}) %collective-permute-start.14) | collective-permute-done | bytes 32800 | tf_op jit(solution)/shard_map/ppermute | solution.py:498
  74.2 3.3 %all-to-all-done.1 = bf16[16,8,640]{2,1,0:T(8,128)(2,1)S(1)} async-done(((bf16[16,8,640]{2,1,0:T(8,128)(2,1)}), bf16[16,8,640]{2,1,0:T(8,128)(2,1)S(1)}, u32[]{:S(2)}, u32[]{:S(2)}) %all-to-all-start.1) | async-done | bytes 163872 | tf_op jit(solution)/shard_map/all_to_all | solution.py:499
  77.6 0.7 final.1
  78.3 0.0 collective-permute-done.10.got
  78.3 0.8 %weights.1 = (f32[128,512]{1,0:T(8,128)}, f32[512,128]{1,0:T(8,128)}) custom-call(bf16[512,256]{1,0:T(8,128)(2,1)S(1)} %get-tuple-element.50.mine, bf16[512,256]{1,0:T(8,128)(2,1)S(1)} %collective-permute-done.10.got), custom_call_target="tpu_custom_call" | custom-call | tf_op jit(solution)/shard_map/weights/pallas_call | solution.py:444
Async XLA Ops:
  2.5 17.0 %all-to-all-start = ((bf16[8,64,640]{2,1,0:T(8,128)(2,1)}), bf16[8,64,640]{2,1,0:T(8,128)(2,1)S(1)}, u32[]{:S(2)}, u32[]{:S(2)}) async-start(bf16[8,64,640]{2,1,0:T(8,128)(2,1)} %keys.1), calls=%async_computation | async-start | bytes 1310720 | tf_op jit(solution)/shard_map/all_to_all | solution.py:471
  8.7 10.8 %copy-start.2 = (bf16[128,512]{1,0:T(8,128)(2,1)S(1)}, bf16[128,512]{1,0:T(8,128)(2,1)}, u32[]{:S(2)}) copy-start(bf16[128,512]{1,0:T(8,128)(2,1)} %clat.1) | copy-start | bytes 393220
  8.7 10.8 %copy-start.3 = (bf16[128,64]{0,1:T(8,128)(2,1)S(1)}, bf16[128,64]{0,1:T(8,128)(2,1)}, u32[]{:S(2)}) copy-start(bf16[128,64]{0,1:T(8,128)(2,1)} %param.18) | copy-start | bytes 49156
  14.4 7.5 %collective-permute-start.2 = (bf16[8,128,384]{2,1,0:T(8,128)(2,1)}, bf16[8,128,384]{2,1,0:T(8,128)(2,1)S(1)}, u32[]{:S(2)}, u32[]{:S(2)}) collective-permute-start(bf16[8,128,384]{2,1,0:T(8,128)(2,1)} %get-tuple-element.37), channel_id=1, source_target_pairs={{0,1},{1,0},{2,3},{3,2},{4,5},{5,4},{6,7},{7,6},{8,9},{9,8},{10,11... | collective-permute-start | bytes 2359304 | tf_op jit(solution)/shard_map/ppermute | solution.py:475
  19.5 2.4 %collective-permute-start = (bf16[512,640]{1,0:T(8,128)(2,1)S(1)}, bf16[512,640]{1,0:T(8,128)(2,1)S(1)}, u32[]{:S(2)}, u32[]{:S(2)}) collective-permute-start(bf16[512,640]{1,0:T(8,128)(2,1)S(1)} %bitcast.23), channel_id=1, source_target_pairs={{0,1},{1,0},{2,3},{3,2},{4,5},{5,4},{6,7},{7,6},{8,9},{9,8},{10,11... | collective-permute-start | bytes 1966088 | tf_op jit(solution)/shard_map/ppermute | solution.py:478
  19.5 0.7 copy-start.4
  20.2 1.7 %copy-start = (bf16[8,256,512]{2,1,0:T(8,128)(2,1)S(1)}, bf16[8,256,512]{2,1,0:T(8,128)(2,1)}, u32[]{:S(2)}) copy-start(bf16[8,256,512]{2,1,0:T(8,128)(2,1)} %get-tuple-element.38) | copy-start | bytes 6291460
  20.2 1.8 %copy-start.1 = (bf16[8,128,384]{2,1,0:T(8,128)(2,1)S(1)}, bf16[8,128,384]{2,1,0:T(8,128)(2,1)}, u32[]{:S(2)}) copy-start(bf16[8,128,384]{2,1,0:T(8,128)(2,1)} %get-tuple-element.36.refs_4_) | copy-start | bytes 2359300
  20.3 1.6 %collective-permute-start.1 = (bf16[128,640]{1,0:T(8,128)(2,1)S(1)}, bf16[128,640]{1,0:T(8,128)(2,1)S(1)}, u32[]{:S(2)}, u32[]{:S(2)}) collective-permute-start(bf16[128,640]{1,0:T(8,128)(2,1)S(1)} %own_keys.1.refs_2_), channel_id=1, source_target_pairs={{0,1},{1,0},{2,3},{3,2},{4,5},{5,4},{6,7},{7,6},{8,9},{9,8},{10,11... | collective-permute-start | bytes 491528 | tf_op jit(solution)/shard_map/ppermute | solution.py:477
  30.8 16.7 %collective-permute-start.3 = (bf16[2,512,256]{2,1,0:T(8,128)(2,1)S(1)}, bf16[2,512,256]{2,1,0:T(8,128)(2,1)S(1)}, u32[]{:S(2)}, u32[]{:S(2)}) collective-permute-start(bf16[2,512,256]{2,1,0:T(8,128)(2,1)S(1)} %get-tuple-element.41), channel_id=1, source_target_pairs={{0,4},{1,5},{2,6},{3,7},{4,8},{5,9},{6,10},{7,11},{8,12},{9,13},{1... | collective-permute-start | bytes 1572872 | tf_op jit(solution)/shard_map/ppermute | solution.py:481
  32.8 14.7 %collective-permute-start.4 = (bf16[2,512,256]{2,1,0:T(8,128)(2,1)S(1)}, bf16[2,512,256]{2,1,0:T(8,128)(2,1)S(1)}, u32[]{:S(2)}, u32[]{:S(2)}) collective-permute-start(bf16[2,512,256]{2,1,0:T(8,128)(2,1)S(1)} %get-tuple-element.42), channel_id=1, source_target_pairs={{0,12},{1,13},{2,14},{3,15},{4,0},{5,1},{6,2},{7,3},{8,4},{9,5},{1... | collective-permute-start | bytes 1572872 | tf_op jit(solution)/shard_map/ppermute | solution.py:482
  44.0 2.4 %collective-permute-start.5 = (bf16[256,640]{1,0:T(8,128)(2,1)S(1)}, bf16[256,640]{1,0:T(8,128)(2,1)S(1)}, u32[]{:S(2)}, u32[]{:S(2)}) collective-permute-start(bf16[256,640]{1,0:T(8,128)(2,1)S(1)} %get-tuple-element.44), channel_id=1, source_target_pairs={{0,1},{1,0},{2,3},{3,2},{4,5},{5,4},{6,7},{7,6},{8,9},{9,8},{10,11... | collective-permute-start | bytes 983048 | tf_op jit(solution)/shard_map/ppermute | solution.py:484
  44.3 2.1 %collective-permute-start.6 = (bf16[256,640]{1,0:T(8,128)(2,1)S(1)}, bf16[256,640]{1,0:T(8,128)(2,1)S(1)}, u32[]{:S(2)}, u32[]{:S(2)}) collective-permute-start(bf16[256,640]{1,0:T(8,128)(2,1)S(1)} %get-tuple-element.45), channel_id=1, source_target_pairs={{0,1},{1,0},{2,3},{3,2},{4,5},{5,4},{6,7},{7,6},{8,9},{9,8},{10,11... | collective-permute-start | bytes 983048 | tf_op jit(solution)/shard_map/ppermute | solution.py:484
  44.6 1.8 %collective-permute-start.7 = (bf16[128,640]{1,0:T(8,128)(2,1)S(1)}, bf16[128,640]{1,0:T(8,128)(2,1)S(1)}, u32[]{:S(2)}, u32[]{:S(2)}) collective-permute-start(bf16[128,640]{1,0:T(8,128)(2,1)S(1)} %get-tuple-element.46), channel_id=1, source_target_pairs={{0,1},{1,0},{2,3},{3,2},{4,5},{5,4},{6,7},{7,6},{8,9},{9,8},{10,11... | collective-permute-start | bytes 491528 | tf_op jit(solution)/shard_map/ppermute | solution.py:484
  47.6 9.5 %collective-permute-start.8 = (bf16[512,256]{1,0:T(8,128)(2,1)S(1)}, bf16[512,256]{1,0:T(8,128)(2,1)S(1)}, u32[]{:S(2)}, u32[]{:S(2)}) collective-permute-start(bf16[512,256]{1,0:T(8,128)(2,1)S(1)} %get-tuple-element.48), channel_id=1, source_target_pairs={{0,4},{1,5},{2,6},{3,7},{4,8},{5,9},{6,10},{7,11},{8,12},{9,13},{1... | collective-permute-start | bytes 786440 | tf_op jit(solution)/shard_map/ppermute | solution.py:490
  49.0 8.2 %collective-permute-start.9 = (bf16[512,256]{1,0:T(8,128)(2,1)S(1)}, bf16[512,256]{1,0:T(8,128)(2,1)S(1)}, u32[]{:S(2)}, u32[]{:S(2)}) collective-permute-start(bf16[512,256]{1,0:T(8,128)(2,1)S(1)} %get-tuple-element.49), channel_id=1, source_target_pairs={{0,12},{1,13},{2,14},{3,15},{4,0},{5,1},{6,2},{7,3},{8,4},{9,5},{1... | collective-permute-start | bytes 786440 | tf_op jit(solution)/shard_map/ppermute | solution.py:491
  51.0 11.7 %collective-permute-start.11 = (bf16[128,768]{1,0:T(8,128)(2,1)S(1)}, bf16[128,768]{1,0:T(8,128)(2,1)S(1)}, u32[]{:S(2)}, u32[]{:S(2)}) collective-permute-start(bf16[128,768]{1,0:T(8,128)(2,1)S(1)} %get-tuple-element.54), channel_id=1, source_target_pairs={{0,32},{16,48},{32,64},{48,80},{64,96},{80,112},{96,0},{112,16},{1... | collective-permute-start | bytes 589832 | tf_op jit(solution)/shard_map/ppermute | solution.py:487
  51.0 11.7 %collective-permute-start.12 = (bf16[128,768]{1,0:T(8,128)(2,1)S(1)}, bf16[128,768]{1,0:T(8,128)(2,1)S(1)}, u32[]{:S(2)}, u32[]{:S(2)}) collective-permute-start(bf16[128,768]{1,0:T(8,128)(2,1)S(1)} %get-tuple-element.55), channel_id=1, source_target_pairs={{0,64},{16,80},{32,96},{48,112},{64,0},{80,16},{96,32},{112,48},{1... | collective-permute-start | bytes 589832 | tf_op jit(solution)/shard_map/ppermute | solution.py:487
  53.3 10.0 %collective-permute-start.13 = (bf16[128,768]{1,0:T(8,128)(2,1)S(1)}, bf16[128,768]{1,0:T(8,128)(2,1)S(1)}, u32[]{:S(2)}, u32[]{:S(2)}) collective-permute-start(bf16[128,768]{1,0:T(8,128)(2,1)S(1)} %get-tuple-element.56), channel_id=1, source_target_pairs={{0,96},{16,112},{32,0},{48,16},{64,32},{80,48},{96,64},{112,80},{1... | collective-permute-start | bytes 589832 | tf_op jit(solution)/shard_map/ppermute | solution.py:487
  57.4 20.9 %collective-permute-start.10 = (bf16[512,256]{1,0:T(8,128)(2,1)S(1)}, bf16[512,256]{1,0:T(8,128)(2,1)S(1)}, u32[]{:S(2)}, u32[]{:S(2)}) collective-permute-start(bf16[512,256]{1,0:T(8,128)(2,1)S(1)} %get-tuple-element.51), channel_id=1, source_target_pairs={{0,2},{1,3},{2,0},{3,1},{4,6},{5,7},{6,4},{7,5},{8,10},{9,11},{10,... | collective-permute-start | bytes 786440 | tf_op jit(solution)/shard_map/ppermute | solution.py:503
  64.1 13.4 %all-to-all-start.1 = ((bf16[16,8,640]{2,1,0:T(8,128)(2,1)}), bf16[16,8,640]{2,1,0:T(8,128)(2,1)S(1)}, u32[]{:S(2)}, u32[]{:S(2)}) async-start(bf16[16,8,640]{2,1,0:T(8,128)(2,1)} %bitcast.19), calls=%async_computation.1 | async-start | bytes 327680 | tf_op jit(solution)/shard_map/all_to_all | solution.py:499
  69.3 4.9 %collective-permute-start.14 = (bf16[128,128]{1,0:T(8,128)(2,1)S(1)}, bf16[128,128]{1,0:T(8,128)(2,1)S(1)}, u32[]{:S(2)}, u32[]{:S(2)}) collective-permute-start(bf16[128,128]{1,0:T(8,128)(2,1)S(1)} %get-tuple-element.58), channel_id=1, source_target_pairs={{0,16},{16,0},{32,48},{48,32},{64,80},{80,64},{96,112},{112,96},{1... | collective-permute-start | bytes 98312 | tf_op jit(solution)/shard_map/ppermute | solution.py:498
